TPU v7x, 32 devices: a whole 2x2x4 slice. The times are simulated.
32 devices in a mesh: dp: 8 (over y, x, core), expert: 4 (over z).
Axes of the slice: x: 2, y: 2, z: 4, core: 2. Of those that a mesh axis runs over, the one named last changes fastest.
Arguments:
- tokens: bfloat16 [5120, 1536], P(('dp', 'expert')), may hold values from -6 to 6
- cotangent: bfloat16 [5120, 1536], P(('dp', 'expert')), may hold values from -6 to 6
- gain_attn: bfloat16 [1536], P('dp'), may hold values from 0.5 to 1.5
- gain_ffn: bfloat16 [1536], P('dp'), may hold values from 0.5 to 1.5
- w_query: bfloat16 [1536, 1536], P('dp'), may hold values from -0.4375 to 0.4375
- key_weight: bfloat16 [1536, 512], P('dp'), may hold values from -0.4375 to 0.4375
- value_weight: bfloat16 [1536, 512], P('dp'), may hold values from -0.15625 to 0.15625
- w_out: bfloat16 [1536, 1536], P('dp'), may hold values from -6 to 6
- expert_gate: bfloat16 [1536, 20, 512], P('dp', 'expert'), may hold values from -0.15625 to 0.15625
- expert_up: bfloat16 [1536, 20, 512], P('dp', 'expert'), may hold values from -0.15625 to 0.15625
- expert_down: bfloat16 [1536, 20, 512], P('dp', 'expert'), may hold values from -4 to 4
- expert_ids: int32 [5120, 8], P(('dp', 'expert')), may hold values from 0 to 19, all different within a row; in each aligned block of 80 rows (0 to 79, 80 to 159, ...) at most 64 rows name the same one
- gates: float32 [5120, 8], P(('dp', 'expert')), as said below
- lengths: int32 [8, 3], P('dp'), may hold values from 1 to 638, as said below
- order: int32 [8, 3], P('dp'), may hold values from 0 to 2, each once within a row
Outputs:
- output: bfloat16 [5120, 1536], P(('dp', 'expert'))
- grad_tokens: float32 [5120, 1536], P(('dp', 'expert'))
- grad_gain_attn: float32 [1536], P('dp')
- grad_gain_ffn: float32 [1536], P('dp')
- grad_w_query: float32 [1536, 1536], P('dp')
- grad_w_key: float32 [1536, 512], P('dp')
- grad_w_value: float32 [1536, 512], P('dp')
- grad_w_out: float32 [1536, 1536], P('dp')
- grad_expert_gate: float32 [1536, 20, 512], P('dp', 'expert')
- grad_expert_up: float32 [1536, 20, 512], P('dp', 'expert')
- grad_expert_down: float32 [1536, 20, 512], P('dp', 'expert')
Inputs may be any that keep to these rules, and one draw needn't show every extreme that they name: lengths[g, :] are the lengths of the 3 sequences of index g of dp; a row sums to at most 640. Each row of order is a permutation. `expert_ids`: each row names 8 different experts; in each aligned block of 80 rows no expert is named by more than 64 rows. Each row of gates is positive and sums to one.
All inputs are finite; a program needn't handle non-finite values.
Results may differ from a plain program's by a relative error of at most 0.02.
Values may be sent and summed in bfloat16 or wider, within the bound.
A program may use at most 256 MiB of HBM per device.

v0:
```python
import jax
import jax.numpy as jnp
from jax import lax
from jax.sharding import PartitionSpec as P

QUERY_HEADS = 24
KEY_VALUE_HEADS = 8
HEAD_SIZE = 64
TOP = 8
EXP_DEV = 5


epsilon = 1e-06
rope_base = 10000.0
score_scale = 0.015625
branch_scale = 0.22


def layout(lengths_row, order_row, sequence_span_rows):
    slot_ids = jnp.arange(lengths_row.shape[0], dtype=jnp.int32)
    picked = jnp.sum(
        jnp.where(order_row[:, None] == slot_ids[None, :], lengths_row[None, :], 0), axis=1
    )
    seq_ends = jnp.cumsum(picked)
    key_place = jnp.arange(sequence_span_rows, dtype=jnp.int32)
    passed = key_place[:, None] >= seq_ends[None, :]
    segment = jnp.sum(passed.astype(jnp.int32), axis=1)
    seq_start = jnp.sum(jnp.where(passed, picked[None, :], 0), axis=1)
    return (segment, (key_place - seq_start).astype(jnp.float32))


def rotation(position, head_dim):
    half_dim = head_dim // 2
    frequency = rope_base ** (-(jnp.arange(half_dim, dtype=jnp.float32) * (2.0 / head_dim)))
    angles = position[:, None] * frequency[None, :]
    return (jnp.cos(angles), jnp.sin(angles))


def apply_rotary(vector, cosine_table, sine_table):
    half_dim = vector.shape[-1] // 2
    leading = vector[..., :half_dim]
    trailing = vector[..., half_dim:]
    cos_part = cosine_table[:, None, :]
    sin_part = sine_table[:, None, :]
    return jnp.concatenate(
        [leading * cos_part - trailing * sin_part, trailing * cos_part + leading * sin_part],
        axis=-1,
    )


def invert_rotary(vector, cosine_table, sine_table):
    half_dim = vector.shape[-1] // 2
    leading = vector[..., :half_dim]
    trailing = vector[..., half_dim:]
    cos_part = cosine_table[:, None, :]
    sin_part = sine_table[:, None, :]
    return jnp.concatenate(
        [leading * cos_part + trailing * sin_part, trailing * cos_part - leading * sin_part],
        axis=-1,
    )


def normalize_parts(field_in, gain_in):
    factor = lax.rsqrt(jnp.mean(field_in * field_in, axis=-1, keepdims=True) + epsilon)
    return (field_in * factor * gain_in, factor)


def norm_back(field_in, factor, gain_in, grad_in):
    scaled = gain_in * grad_in
    grad_gain = jnp.sum(grad_in * field_in * factor, axis=0)
    cubed = factor * factor * factor
    grad_field = factor * scaled - field_in * cubed * jnp.mean(
        scaled * field_in, axis=-1, keepdims=True
    )
    return (grad_field, grad_gain)


def local_rank(onehot):
    pair_count = onehot.shape[0]
    block_width = 128
    blocks = onehot.reshape(pair_count // block_width, block_width, onehot.shape[1]).astype(
        jnp.bfloat16
    )
    indices = jnp.arange(block_width, dtype=jnp.int32)
    lower_tri = (indices[:, None] >= indices[None, :]).astype(jnp.bfloat16)
    within_block = jnp.einsum("ab,nbe->nae", lower_tri, blocks, preferred_element_type=jnp.float32)
    block_sums = within_block[:, -1, :]
    block_base = jnp.cumsum(block_sums, axis=0) - block_sums
    running = (within_block + block_base[:, None, :]).reshape(pair_count, onehot.shape[1])
    return (jnp.sum(jnp.where(onehot, running, 0.0), axis=1) - 1.0).astype(jnp.int32)


def attend_forward(query_rows, keys_here, values_here, allowed):
    scores = (
        jnp.einsum("irh,jh->rij", query_rows, keys_here, preferred_element_type=jnp.float32)
        * score_scale
    )
    scores = jnp.where(allowed[None], scores, -1e30)
    peak = jnp.max(scores, axis=-1, keepdims=True)
    exponent = jnp.exp(scores - peak)
    normalizer = jnp.sum(exponent, axis=-1, keepdims=True)
    probs = (exponent / normalizer).astype(jnp.bfloat16)
    result = jnp.einsum("rij,jh->irh", probs, values_here, preferred_element_type=jnp.float32)
    return (result, (peak + jnp.log(normalizer))[..., 0])


def attend_backward(query_rows, keys_here, values_here, logsum, grad_out, allowed):
    scores = (
        jnp.einsum("irh,jh->rij", query_rows, keys_here, preferred_element_type=jnp.float32)
        * score_scale
    )
    scores = jnp.where(allowed[None], scores, -1e30)
    probs = jnp.exp(scores - logsum[..., None])
    probs_low = probs.astype(jnp.bfloat16)
    grad_probs = jnp.einsum(
        "irh,jh->rij", grad_out, values_here, preferred_element_type=jnp.float32
    )
    grad_scores = (
        probs * (grad_probs - jnp.sum(probs * grad_probs, axis=-1, keepdims=True))
    ).astype(jnp.bfloat16)
    grad_query = (
        jnp.einsum("rij,jh->irh", grad_scores, keys_here, preferred_element_type=jnp.float32)
        * score_scale
    )
    grad_key = (
        jnp.einsum("rij,irh->jh", grad_scores, query_rows, preferred_element_type=jnp.float32)
        * score_scale
    )
    grad_value = jnp.einsum("rij,irh->jh", probs_low, grad_out, preferred_element_type=jnp.float32)
    return (grad_query, grad_key, grad_value)


def shards(
    tokens,
    cotangent,
    gain_attn,
    gain_ffn,
    w_query,
    key_weight,
    value_weight,
    w_out,
    expert_gate,
    expert_up,
    expert_down,
    expert_ids,
    gates,
    lengths,
    order,
):
    token_rows = tokens.shape[0]
    width = tokens.shape[1]
    members = lax.axis_size("expert")
    member = lax.axis_index("expert")
    sequence_span_rows = token_rows * members
    half_rows = token_rows // 2
    repeat_heads = QUERY_HEADS // KEY_VALUE_HEADS
    experts_all = EXP_DEV * members
    most_rows = 2 * token_rows * TOP // experts_all
    capacity = token_rows * TOP // EXP_DEV
    pair_count = token_rows * TOP
    half_pairs = half_rows * TOP
    slot_total = experts_all * most_rows
    device_list = jnp.arange(members, dtype=jnp.int32)
    first_block = 2 * member
    second_block = 2 * member + 1
    first_of = 2 * device_list
    second_of = 2 * device_list + 1
    key_rows = jnp.arange(sequence_span_rows, dtype=jnp.int32)
    key_device = key_rows // token_rows
    key_within = key_rows % token_rows
    key_slots = jnp.where(
        key_within < half_rows,
        first_of[key_device] * half_rows + key_within,
        second_of[key_device] * half_rows + key_within - half_rows,
    )
    own_rows = jnp.arange(token_rows, dtype=jnp.int32)
    my_slots = jnp.where(
        own_rows < half_rows,
        first_block * half_rows + own_rows,
        second_block * half_rows + own_rows - half_rows,
    )
    count_blocks = jnp.stack([first_of, second_of], axis=1).reshape(2 * members)
    inputs = tokens.astype(jnp.float32)
    grad_in = cotangent.astype(jnp.float32)
    segment, position = layout(lengths[0], order[0], sequence_span_rows)
    seg_mine = segment[my_slots]
    pos_mine = position[my_slots]
    seg_keys = segment[key_slots]
    cosine_table, sine_table = rotation(pos_mine, HEAD_SIZE)
    allowed = (seg_mine[:, None] == seg_keys[None, :]) & (key_slots[None, :] <= my_slots[:, None])
    gathered = (
        lax.all_gather(gain_attn, "dp", axis=0, tiled=True),
        lax.all_gather(gain_ffn, "dp", axis=0, tiled=True),
        lax.all_gather(w_query, "dp", axis=0, tiled=True),
        lax.all_gather(key_weight, "dp", axis=0, tiled=True),
        lax.all_gather(value_weight, "dp", axis=0, tiled=True),
        lax.all_gather(w_out, "dp", axis=0, tiled=True),
    )
    experts_full = (
        lax.all_gather(expert_gate, "dp", axis=0, tiled=True),
        lax.all_gather(expert_up, "dp", axis=0, tiled=True),
        lax.all_gather(expert_down, "dp", axis=0, tiled=True),
    )
    gain_one = gathered[0].astype(jnp.float32)
    gain_two = gathered[1].astype(jnp.float32)
    wq_full, full_key_weight, full_value_weight, wo_full = (
        gathered[2],
        gathered[3],
        gathered[4],
        gathered[5],
    )
    gate_full, up_full, down_full = (experts_full[0], experts_full[1], experts_full[2])
    chosen = expert_ids.reshape(pair_count)
    onehot = chosen[:, None] == jnp.arange(experts_all, dtype=jnp.int32)[None, :]
    onehot_int = onehot.astype(jnp.int32)
    counts_first = jnp.sum(onehot_int[:half_pairs], axis=0)
    counts_second = jnp.sum(onehot_int[half_pairs:], axis=0)
    block_counts = jnp.stack([counts_first, counts_second]).astype(jnp.bfloat16)
    normed_pre, factor_one = normalize_parts(inputs, gain_one)
    normalized_input = normed_pre.astype(jnp.bfloat16)
    query_rows = apply_rotary(
        jnp.dot(normalized_input, wq_full, preferred_element_type=jnp.float32).reshape(
            token_rows, QUERY_HEADS, HEAD_SIZE
        ),
        cosine_table,
        sine_table,
    ).astype(jnp.bfloat16)
    keys_mine = (
        apply_rotary(
            jnp.dot(normalized_input, full_key_weight, preferred_element_type=jnp.float32).reshape(
                token_rows, KEY_VALUE_HEADS, HEAD_SIZE
            ),
            cosine_table,
            sine_table,
        )
        .astype(jnp.bfloat16)
        .reshape(token_rows, KEY_VALUE_HEADS * HEAD_SIZE)
    )
    values_mine = jnp.dot(
        normalized_input, full_value_weight, preferred_element_type=jnp.float32
    ).astype(jnp.bfloat16)
    every_key, every_value, counts_all = (
        lax.all_gather(keys_mine, "expert", axis=0, tiled=True),
        lax.all_gather(values_mine, "expert", axis=0, tiled=True),
        lax.all_gather(block_counts, "expert", axis=0, tiled=True),
    )
    query_head_rows = jnp.moveaxis(
        query_rows.reshape(token_rows, KEY_VALUE_HEADS, repeat_heads, HEAD_SIZE), 1, 0
    )
    key_head_rows = jnp.moveaxis(
        every_key.reshape(sequence_span_rows, KEY_VALUE_HEADS, HEAD_SIZE), 1, 0
    )
    value_head_rows = jnp.moveaxis(
        every_value.reshape(sequence_span_rows, KEY_VALUE_HEADS, HEAD_SIZE), 1, 0
    )
    attended, logsum = lax.map(
        lambda packed: attend_forward(packed[0], packed[1], packed[2], allowed),
        (query_head_rows, key_head_rows, value_head_rows),
    )
    attended = (
        jnp.moveaxis(attended, 0, 1)
        .reshape(token_rows, QUERY_HEADS * HEAD_SIZE)
        .astype(jnp.bfloat16)
    )
    attn_out = jnp.einsum("tc,dc->td", attended, wo_full, preferred_element_type=jnp.float32)
    residual = inputs + branch_scale * attn_out
    normed_pre_two, factor_two = normalize_parts(residual, gain_two)
    normed_ffn = normed_pre_two.astype(jnp.bfloat16)
    counts_float = counts_all.astype(jnp.float32)
    before_first = jnp.sum(
        jnp.where((count_blocks < first_block)[:, None], counts_float, 0.0), axis=0
    ).astype(jnp.int32)
    before_second = jnp.sum(
        jnp.where((count_blocks < second_block)[:, None], counts_float, 0.0), axis=0
    ).astype(jnp.int32)
    in_first = (jnp.arange(pair_count, dtype=jnp.int32) < half_pairs)[:, None]
    base_row = jnp.where(in_first, before_first[None, :], (before_second - counts_first)[None, :])
    local_slot = local_rank(onehot)
    slot_base = jnp.sum(jnp.where(onehot, base_row, 0), axis=1)
    within = slot_base + local_slot < capacity
    slot_target = jnp.where(within, chosen * most_rows + local_slot, slot_total)
    pair_table = (
        jnp.full((slot_total + 1,), pair_count, jnp.int32)
        .at[slot_target]
        .set(jnp.arange(pair_count, dtype=jnp.int32))[:slot_total]
    )
    token_table = jnp.where(pair_table < pair_count, pair_table // TOP, token_rows)
    zero_row = jnp.zeros((1, width), jnp.bfloat16)
    outgoing = jnp.concatenate([normed_ffn, zero_row], axis=0)[token_table].reshape(
        members, EXP_DEV, most_rows, width
    )
    run_received = lax.all_to_all(outgoing, "expert", split_axis=0, concat_axis=0, tiled=True)
    pre_gate = jnp.einsum(
        "semd,def->semf", run_received, gate_full, preferred_element_type=jnp.float32
    )
    pre_up = jnp.einsum("semd,def->semf", run_received, up_full, preferred_element_type=jnp.float32)
    run_activ = (jax.nn.silu(pre_gate) * pre_up).astype(jnp.bfloat16)
    produced = jnp.einsum(
        "semf,def->semd", run_activ, down_full, preferred_element_type=jnp.float32
    ).astype(jnp.bfloat16)
    returned = lax.all_to_all(produced, "expert", split_axis=0, concat_axis=0, tiled=True)
    returned, received, activ, pre_gate, pre_up = (
        returned,
        run_received,
        run_activ,
        pre_gate,
        pre_up,
    )
    per_pair = jnp.concatenate([returned.reshape(slot_total, width), zero_row], axis=0)[
        slot_target
    ].reshape(token_rows, TOP, width)
    mixture = jnp.einsum("tkd,tk->td", per_pair, gates)
    output_rows = (residual + branch_scale * mixture).astype(jnp.bfloat16)
    regathered = (
        lax.all_gather(gain_attn, "dp", axis=0, tiled=True),
        lax.all_gather(gain_ffn, "dp", axis=0, tiled=True),
        lax.all_gather(w_query, "dp", axis=0, tiled=True),
        lax.all_gather(key_weight, "dp", axis=0, tiled=True),
        lax.all_gather(value_weight, "dp", axis=0, tiled=True),
        lax.all_gather(w_out, "dp", axis=0, tiled=True),
        lax.all_gather(expert_gate, "dp", axis=0, tiled=True),
        lax.all_gather(expert_up, "dp", axis=0, tiled=True),
        lax.all_gather(expert_down, "dp", axis=0, tiled=True),
    )
    gain_back_one = regathered[0].astype(jnp.float32)
    gain_back_two = regathered[1].astype(jnp.float32)
    wq_back, wk_back, wv_back, wo_back = (
        regathered[2],
        regathered[3],
        regathered[4],
        regathered[5],
    )
    gate_back, up_back, down_back = (regathered[6], regathered[7], regathered[8])
    grad_pairs = (
        (gates[:, :, None] * (branch_scale * grad_in)[:, None, :])
        .astype(jnp.bfloat16)
        .reshape(pair_count, width)
    )
    grad_outgoing = jnp.concatenate([grad_pairs, zero_row], axis=0)[pair_table].reshape(
        members, EXP_DEV, most_rows, width
    )
    grad_received = lax.all_to_all(grad_outgoing, "expert", split_axis=0, concat_axis=0, tiled=True)
    grad_activ = jnp.einsum(
        "semd,def->semf", grad_received, down_back, preferred_element_type=jnp.float32
    )
    sigmoid_h = jax.nn.sigmoid(pre_gate)
    grad_pre_gate = (grad_activ * pre_up * sigmoid_h * (1.0 + pre_gate * (1.0 - sigmoid_h))).astype(
        jnp.bfloat16
    )
    grad_pre_up = (grad_activ * jax.nn.silu(pre_gate)).astype(jnp.bfloat16)
    grad_rows = jnp.einsum(
        "semf,def->semd", grad_pre_gate, gate_back, preferred_element_type=jnp.float32
    )
    grad_rows = (
        grad_rows
        + jnp.einsum("semf,def->semd", grad_pre_up, up_back, preferred_element_type=jnp.float32)
    ).astype(jnp.bfloat16)
    grad_returned = lax.all_to_all(grad_rows, "expert", split_axis=0, concat_axis=0, tiled=True)
    part_gate = jnp.einsum(
        "semd,semf->def", received, grad_pre_gate, preferred_element_type=jnp.float32
    )
    part_up = jnp.einsum(
        "semd,semf->def", received, grad_pre_up, preferred_element_type=jnp.float32
    )
    part_down = jnp.einsum(
        "semd,semf->def", grad_received, activ, preferred_element_type=jnp.float32
    )
    expert_grads = lax.psum_scatter(
        jnp.concatenate([part_gate, part_up, part_down], axis=1).astype(jnp.bfloat16),
        "dp",
        scatter_dimension=0,
        tiled=True,
    ).astype(jnp.float32)
    grad_expert_gate = expert_grads[:, :EXP_DEV]
    grad_expert_up = expert_grads[:, EXP_DEV : 2 * EXP_DEV]
    grad_expert_down = expert_grads[:, 2 * EXP_DEV :]
    pair_grads = jnp.concatenate([grad_returned.reshape(slot_total, width), zero_row], axis=0)[
        slot_target
    ].reshape(token_rows, TOP, width)
    grad_normed_ffn = jnp.sum(pair_grads, axis=1, dtype=jnp.float32)
    grad_res_norm, grad_gain_ffn = norm_back(residual, factor_two, gain_back_two, grad_normed_ffn)
    grad_residual = grad_in + grad_res_norm
    grad_attn_out = (branch_scale * grad_residual).astype(jnp.bfloat16)
    term_out = jnp.einsum("td,tc->dc", grad_attn_out, attended, preferred_element_type=jnp.float32)
    attended_gradient = jnp.dot(grad_attn_out, wo_back, preferred_element_type=jnp.float32).astype(
        jnp.bfloat16
    )
    head_gradients = jnp.moveaxis(
        attended_gradient.reshape(token_rows, KEY_VALUE_HEADS, repeat_heads, HEAD_SIZE), 1, 0
    )
    grad_q, key_gradient, value_gradient = lax.map(
        lambda packed: attend_backward(
            packed[0], packed[1], packed[2], packed[3], packed[4], allowed
        ),
        (query_head_rows, key_head_rows, value_head_rows, logsum, head_gradients),
    )
    shifted_keys = jnp.moveaxis(key_gradient, 0, 1).reshape(
        sequence_span_rows, KEY_VALUE_HEADS * HEAD_SIZE
    )
    shifted_values = jnp.moveaxis(value_gradient, 0, 1).reshape(
        sequence_span_rows, KEY_VALUE_HEADS * HEAD_SIZE
    )
    key_gradient_rows, value_grads = (
        lax.psum_scatter(
            shifted_keys.astype(jnp.bfloat16), "expert", scatter_dimension=0, tiled=True
        ).astype(jnp.float32),
        lax.psum_scatter(
            shifted_values.astype(jnp.bfloat16), "expert", scatter_dimension=0, tiled=True
        ).astype(jnp.float32),
    )
    grad_query = (
        invert_rotary(
            jnp.moveaxis(grad_q, 0, 1).reshape(token_rows, QUERY_HEADS, HEAD_SIZE),
            cosine_table,
            sine_table,
        )
        .reshape(token_rows, QUERY_HEADS * HEAD_SIZE)
        .astype(jnp.bfloat16)
    )
    grad_key = (
        invert_rotary(
            key_gradient_rows.reshape(token_rows, KEY_VALUE_HEADS, HEAD_SIZE),
            cosine_table,
            sine_table,
        )
        .reshape(token_rows, KEY_VALUE_HEADS * HEAD_SIZE)
        .astype(jnp.bfloat16)
    )
    grad_value = value_grads.astype(jnp.bfloat16)
    grad_normed = jnp.einsum("tc,dc->td", grad_query, wq_back, preferred_element_type=jnp.float32)
    grad_normed = grad_normed + jnp.einsum(
        "tc,dc->td", grad_key, wk_back, preferred_element_type=jnp.float32
    )
    grad_normed = grad_normed + jnp.einsum(
        "tc,dc->td", grad_value, wv_back, preferred_element_type=jnp.float32
    )
    grad_input_norm, grad_gain_attn = norm_back(inputs, factor_one, gain_back_one, grad_normed)
    grad_rows_in = grad_residual + grad_input_norm
    term_query = jnp.einsum(
        "td,tc->dc", normalized_input, grad_query, preferred_element_type=jnp.float32
    )
    term_key = jnp.einsum(
        "td,tc->dc", normalized_input, grad_key, preferred_element_type=jnp.float32
    )
    term_value = jnp.einsum(
        "td,tc->dc", normalized_input, grad_value, preferred_element_type=jnp.float32
    )
    summed = (
        lax.psum_scatter(
            grad_gain_attn.astype(jnp.bfloat16), "dp", scatter_dimension=0, tiled=True
        ).astype(jnp.float32),
        lax.psum_scatter(
            grad_gain_ffn.astype(jnp.bfloat16), "dp", scatter_dimension=0, tiled=True
        ).astype(jnp.float32),
        lax.psum_scatter(
            term_query.astype(jnp.bfloat16), "dp", scatter_dimension=0, tiled=True
        ).astype(jnp.float32),
        lax.psum_scatter(
            term_key.astype(jnp.bfloat16), "dp", scatter_dimension=0, tiled=True
        ).astype(jnp.float32),
        lax.psum_scatter(
            term_value.astype(jnp.bfloat16), "dp", scatter_dimension=0, tiled=True
        ).astype(jnp.float32),
        lax.psum_scatter(
            term_out.astype(jnp.bfloat16), "dp", scatter_dimension=0, tiled=True
        ).astype(jnp.float32),
    )
    totals = (
        lax.psum(summed[0].astype(jnp.bfloat16), "expert").astype(jnp.float32),
        lax.psum(summed[1].astype(jnp.bfloat16), "expert").astype(jnp.float32),
        lax.psum(summed[2].astype(jnp.bfloat16), "expert").astype(jnp.float32),
        lax.psum(summed[3].astype(jnp.bfloat16), "expert").astype(jnp.float32),
        lax.psum(summed[4].astype(jnp.bfloat16), "expert").astype(jnp.float32),
        lax.psum(summed[5].astype(jnp.bfloat16), "expert").astype(jnp.float32),
    )
    return (
        output_rows,
        grad_rows_in,
        totals[0],
        totals[1],
        totals[2],
        totals[3],
        totals[4],
        totals[5],
        grad_expert_gate,
        grad_expert_up,
        grad_expert_down,
    )


def solution(mesh):
    return jax.shard_map(
        shards,
        mesh=mesh,
        in_specs=(
            P(("dp", "expert"), None),
            P(("dp", "expert"), None),
            P("dp"),
            P("dp"),
            P("dp", None),
            P("dp", None),
            P("dp", None),
            P("dp", None),
            P("dp", "expert", None),
            P("dp", "expert", None),
            P("dp", "expert", None),
            P(("dp", "expert"), None),
            P(("dp", "expert"), None),
            P("dp", None),
            P("dp", None),
        ),
        out_specs=(
            P(("dp", "expert"), None),
            P(("dp", "expert"), None),
            P("dp"),
            P("dp"),
            P("dp", None),
            P("dp", None),
            P("dp", None),
            P("dp", None),
            P("dp", "expert", None),
            P("dp", "expert", None),
            P("dp", "expert", None),
        ),
        check_vma=False,
    )
```

profile of v0, /device:TPU:0, one launch (start us, length us, event | category | flops | bytes accessed | tf_op | source)
XLA Modules:
  0.0 1508.2 jit_solution(5130470908282991859)
XLA Ops:
  12.6 5.2 fusion.115
  17.8 5.2 fusion.118
  25.2 15.6 %all-reduce.9 = (bf16[1536]{0:T(1024)(128)(2,1)S(1)}, bf16[1536]{0:T(1024)(128)(2,1)S(1)}) all-reduce(bf16[1536]{0:T(1024)(128)(2,1)S(1)} %dynamic-update-slice, bf16[1536]{0:T(1024)(128)(2,1)S(1)} %dynamic-update-slice.1), channel_id=1, replica_groups=mesh['dp'=8,'expert'=4] {'dp'}, use_global_device_ids=true, to_apply=%add.4 | all-reduce | flops 3072 | bytes 12288
  48.2 11.1 all-gather
  60.5 5.3 scatter_custom_fusion
  68.1 15.4 %all_gather.47 = bf16[640,512]{1,0:T(8,128)(2,1)S(1)} all-gather(bf16[160,512]{1,0:T(8,128)(2,1)S(1)} %convolution_convert_fusion.5), channel_id=1, replica_groups=mesh['dp'=8,'expert'=4] {'expert'}, dimensions={0}, use_global_device_ids=true | all-gather | bytes 819200 | tf_op jit(solution)/shard_map/all_gather | solution.py:244
  87.4 16.7 %all_gather.49 = bf16[640,512]{1,0:T(8,128)(2,1)S(1)} all-gather(bf16[160,512]{1,0:T(8,128)(2,1)S(1)} %convert_element_type.217), channel_id=1, replica_groups=mesh['dp'=8,'expert'=4] {'expert'}, dimensions={0}, use_global_device_ids=true | all-gather | bytes 819200 | tf_op jit(solution)/shard_map/all_gather | solution.py:243
  107.2 4.3 fusion.125
  119.0 32.4 %while.30 = (s32[]{:T(128)}, bf16[8,160,3,64]{1,3,2,0:T(8,128)(2,1)S(1)}, f32[8,3,160]{2,1,0:T(4,128)}, bf16[8,640,64]{1,2,0:T(8,128)(2,1)}, bf16[8,640,64]{1,2,...) while((s32[]{:T(128)}, ...), condition=%wide.region_8.9_spmd.clone.clone, body=%wide.region_5.8_spmd.clone.sunk.clone | while | flops 81407520 | bytes 4380401 | solution.py:256
  152.2 4.2 multiply_reduce_fusion.3
  157.2 9.6 gather_fusion.3
  166.8 5.6 all-to-all-start
  176.7 19.6 %gather_fusion.5 = bf16[2560,1536]{1,0:T(8,128)(2,1)} fusion(bf16[1281,1536]{1,0:T(8,128)(2,1)} %concatenate.43, s32[3072]{0:T(1024)S(1)} %pad_clamp_fusion), kind=kCustom, calls=%fused_computation.5 | custom fusion | bytes 15738880 | tf_op jit(solution)/shard_map/gather | solution.py:339
  196.3 148.7 %all-to-all-done = bf16[4,5,128,1536]{3,2,1,0:T(8,128)(2,1)} async-done(((bf16[4,5,128,1536]{3,2,1,0:T(8,128)(2,1)}), bf16[4,5,128,1536]{3,2,1,0:T(8,128)(2,1)}, u32[]{:S(2)}, u32[]{:S(2)}) %all-to-all-start) | async-done | bytes 7864352 | tf_op jit(solution)/shard_map/all_to_all | solution.py:292
  345.0 6.0 all-to-all-start.2
  351.0 12.0 fusion.54
  363.1 12.1 fusion.58
  375.2 147.5 %all-to-all-done.2 = bf16[4,5,128,1536]{3,2,1,0:T(8,128)(2,1)} async-done(((bf16[4,5,128,1536]{3,2,1,0:T(8,128)(2,1)}), bf16[4,5,128,1536]{3,2,1,0:T(8,128)(2,1)}, u32[]{:S(2)}, u32[]{:S(2)}) %all-to-all-start.2) | async-done | bytes 7864352 | tf_op jit(solution)/shard_map/all_to_all | solution.py:342
  522.7 13.2 fusion.73
  535.9 12.0 fusion.52
  547.9 13.1 fusion.48
  561.0 7.1 copy.122
  568.1 5.5 all-to-all-start.3
  573.6 11.4 convert_bitcast_fusion
  585.0 7.1 copy.119
  592.1 152.9 %all-to-all-done.3 = bf16[4,5,128,1536]{3,2,1,0:T(8,128)(2,1)} async-done(((bf16[4,5,128,1536]{3,2,1,0:T(8,128)(2,1)}), bf16[4,5,128,1536]{3,2,1,0:T(8,128)(2,1)}, u32[]{:S(2)}, u32[]{:S(2)}) %all-to-all-start.3) | async-done | bytes 7864352 | tf_op jit(solution)/shard_map/all_to_all | solution.py:358
  745.0 5.5 all-to-all-start.1
  750.8 6.8 concatenate.44
  757.5 13.3 gather_fusion.6
  770.8 4.7 convert_reduce_fusion
  775.8 146.0 %all-to-all-done.1 = bf16[4,5,128,1536]{3,2,1,0:T(8,128)(2,1)} async-done(((bf16[4,5,128,1536]{3,2,1,0:T(8,128)(2,1)}), bf16[4,5,128,1536]{3,2,1,0:T(8,128)(2,1)}, u32[]{:S(2)}, u32[]{:S(2)}) %all-to-all-start.1) | async-done | bytes 7864352 | tf_op jit(solution)/shard_map/all_to_all | solution.py:301
  921.8 6.8 concatenate.42
  928.6 13.1 gather_fusion.4
  949.9 63.9 %while.31 = (s32[]{:T(128)}, f32[8,160,3,64]{1,3,2,0:T(8,128)}, bf16[8,640,64]{1,2,0:T(8,128)(2,1)S(1)}, bf16[8,640,64]{1,2,0:T(8,128)(2,1)}, bf16[8,640,64]{1,2...) while((s32[]{:T(128)}, f32[8,160,3,64]{1,3,2,0:T(8,128)}, ...), condition=%wide.region_22.23_spmd.clone.clone, body=%wide.region_20.22_spmd.clone.sunk.clone | while | flops 199751200 | bytes 10605321 | solution.py:391
  1017.3 18.1 %reduce-scatter.10.cloned.1.call-done = bf16[160,512]{1,0:T(8,128)(2,1)} async-done(((bf16[640,512]{1,0:T(8,128)(2,1)}), bf16[160,512]{1,0:T(8,128)(2,1)}) %reduce-scatter.10.cloned.1.call-update) | async-done | bytes 163856 | tf_op jit(solution)/shard_map/reduce_scatter | solution.py:404
  1039.1 20.1 %reduce-scatter.22.cloned.1.call-done = bf16[160,512]{1,0:T(8,128)(2,1)} async-done(((bf16[640,512]{1,0:T(8,128)(2,1)}), bf16[160,512]{1,0:T(8,128)(2,1)}) %reduce-scatter.22.cloned.1.call-update) | async-done | bytes 163856
  1082.6 11.4 fusion.51
  1094.0 11.7 fusion.50
  1105.7 9.7 fusion.49
  1115.4 27.3 %reduce-scatter.16.cloned.1.call-done = bf16[192,512]{1,0:T(8,128)(2,1)} async-done(((bf16[1536,512]{1,0:T(8,128)(2,1)}), bf16[192,512]{1,0:T(8,128)(2,1)}) %reduce-scatter.16.cloned.1.call-update) | async-done | bytes 196624 | tf_op jit(solution)/shard_map/reduce_scatter | solution.py:461
  1142.7 57.2 %reduce-scatter.12.cloned.1.call-done = bf16[192,1536]{1,0:T(8,128)(2,1)} async-done(((bf16[1536,1536]{1,0:T(8,128)(2,1)}), bf16[192,1536]{1,0:T(8,128)(2,1)}) %reduce-scatter.12.cloned.1.call-update) | async-done | bytes 589840 | tf_op jit(solution)/shard_map/reduce_scatter | solution.py:455
  1199.9 57.8 %reduce-scatter.18.cloned.1.call-done = bf16[192,1536]{1,0:T(8,128)(2,1)} async-done(((bf16[1536,1536]{1,0:T(8,128)(2,1)}), bf16[192,1536]{1,0:T(8,128)(2,1)}) %reduce-scatter.18.cloned.1.call-update) | async-done | bytes 589840 | tf_op jit(solution)/shard_map/reduce_scatter | solution.py:464
  1257.9 20.0 %pad_maximum_fusion = bf16[1536,15,512]{0,2,1:T(8,128)(2,1)} fusion(bf16[1536,5,512]{0,2,1:T(8,128)(2,1)} %fusion.51, bf16[1536,5,512]{0,2,1:T(8,128)(2,1)} %fusion.50, bf16[1536,5,512]{0,2,1:T(8,128)(2,1)} %fusion.49), kind=kLoop, calls=%fused_computation.69 | loop fusion | flops 23592960 | bytes 47185920 | tf_op jit(solution)/shard_map/concatenate | solution.py:369
  1277.9 32.3 %copy.133 = bf16[1536,15,512]{2,1,0:T(8,128)(2,1)} copy(bf16[1536,15,512]{0,2,1:T(8,128)(2,1)} %pad_maximum_fusion) | data formatting | bytes 47185920 | tf_op jit(solution)/shard_map/concatenate | solution.py:369
  1318.1 13.7 all-reduce.8
  1332.0 11.6 all-reduce.10
  1354.2 135.6 %reduce-scatter.20.cloned.1.call-done = bf16[192,15,512]{2,1,0:T(8,128)(2,1)} async-done(((bf16[1536,15,512]{2,1,0:T(8,128)(2,1)}), bf16[192,15,512]{2,1,0:T(8,128)(2,1)}) %reduce-scatter.20.cloned.1.call-update) | async-done | bytes 2949136 | tf_op jit(solution)/shard_map/reduce_scatter | solution.py:368
  1489.8 4.4 fusion.131
  (346 shorter events, 197.6 us)
Async XLA Ops:
  7.2 16.2 %copy-start.36 = (u32[32]{0:T(128)S(1)}, u32[32]{0:T(128)}, u32[]{:S(2)}) copy-start(u32[32]{0:T(128)} %constant.179) | copy-start | bytes 388
  7.2 15.8 %copy-start.32 = (s32[160,8]{0,1:T(8,128)S(1)}, s32[160,8]{0,1:T(8,128)}, u32[]{:S(2)}) copy-start(s32[160,8]{0,1:T(8,128)} %param.30) | copy-start | bytes 15364
  7.2 17.5 %copy-start.37 = (bf16[192]{0:T(256)(128)(2,1)S(1)}, bf16[192]{0:T(256)(128)(2,1)}, u32[]{:S(2)}) copy-start(bf16[192]{0:T(256)(128)(2,1)} %param.21) | copy-start | bytes 1156
  7.2 17.8 %copy-start.38 = (bf16[192]{0:T(256)(128)(2,1)S(1)}, bf16[192]{0:T(256)(128)(2,1)}, u32[]{:S(2)}) copy-start(bf16[192]{0:T(256)(128)(2,1)} %param.22) | copy-start | bytes 1156
  7.2 33.6 %copy-start = (bf16[160,1536]{1,0:T(8,128)(2,1)S(1)}, bf16[160,1536]{1,0:T(8,128)(2,1)}, u32[]{:S(2)}) copy-start(bf16[160,1536]{1,0:T(8,128)(2,1)} %param.19) | copy-start | bytes 1474564
  7.2 34.4 %copy-start.39 = (s32[1,3]{1,0:T(1,128)S(1)}, s32[1,3]{1,0:T(1,128)}, u32[]{:S(2)}) copy-start(s32[1,3]{1,0:T(1,128)} %param.32) | copy-start | bytes 40
  7.2 34.4 %copy-start.40 = (s32[1,3]{1,0:T(1,128)S(1)}, s32[1,3]{1,0:T(1,128)}, u32[]{:S(2)}) copy-start(s32[1,3]{1,0:T(1,128)} %param.33) | copy-start | bytes 40
  7.3 58.9 %all-gather.9.cloned.1.call-start = ((), (), s32[]{:S(2)}) async-start(), calls=%async_computation.11 | async-start | bytes 1769472 | tf_op jit(solution)/shard_map/all_gather | solution.py:196
  8.0 76.6 %all-gather.11.cloned.1.call-start = ((), (), s32[]{:S(2)}) async-start(), calls=%async_computation.12 | async-start | bytes 1769472 | tf_op jit(solution)/shard_map/all_gather | solution.py:195
  8.7 98.5 %all-gather.13.cloned.1.call-start = ((), (), s32[]{:S(2)}) async-start(), calls=%async_computation.13 | async-start | bytes 5308416 | tf_op jit(solution)/shard_map/all_gather | solution.py:194
  9.5 141.9 %all-gather.15.cloned.1.call-start = ((), (), s32[]{:S(2)}) async-start(), calls=%async_computation.14 | async-start | bytes 5308416 | tf_op jit(solution)/shard_map/all_gather | solution.py:197
  10.0 341.0 %all-gather.19.cloned.1.call-start = ((), (), s32[]{:S(2)}) async-start(), calls=%async_computation.16 | async-start | bytes 8847360 | tf_op jit(solution)/shard_map/all_gather | solution.py:201
  10.6 352.5 %all-gather.17.cloned.1.call-start = ((), (), s32[]{:S(2)}) async-start(), calls=%async_computation.15 | async-start | bytes 8847360 | tf_op jit(solution)/shard_map/all_gather | solution.py:200
  40.8 66.4 %copy-start.21 = (f32[1536]{0:T(1024)}, f32[1536]{0:T(1024)S(1)}, u32[]{:S(2)}) copy-start(f32[1536]{0:T(1024)S(1)} %convert_element_type.212) | copy-start | bytes 18436
  41.6 65.6 %copy-start.28 = (f32[160]{0:T(256)}, f32[160]{0:T(256)S(1)}, u32[]{:S(2)}) copy-start(f32[160]{0:T(256)S(1)} %get-tuple-element.316) | copy-start | bytes 1924
  66.1 47.0 %copy-start.7 = (f32[160,32]{1,0:T(8,128)}, f32[160,32]{1,0:T(8,128)S(1)}, u32[]{:S(2)}) copy-start(f32[160,32]{1,0:T(8,128)S(1)} %get-tuple-element.313) | copy-start | bytes 61444
  66.1 47.0 %copy-start.9 = (f32[160,32]{1,0:T(8,128)}, f32[160,32]{1,0:T(8,128)S(1)}, u32[]{:S(2)}) copy-start(f32[160,32]{1,0:T(8,128)S(1)} %get-tuple-element.314) | copy-start | bytes 61444
  151.4 5.8 copy-start.2
  151.4 5.8 copy-start.24
  151.4 5.8 copy-start.26
  166.8 6.4 copy-start.33
  166.8 6.6 copy-start.11
  166.8 178.2 %all-to-all-start = ((bf16[4,5,128,1536]{3,2,1,0:T(8,128)(2,1)}), bf16[4,5,128,1536]{3,2,1,0:T(8,128)(2,1)}, u32[]{:S(2)}, u32[]{:S(2)}) async-start(bf16[4,5,128,1536]{3,2,1,0:T(8,128)(2,1)} %bitcast.347), calls=%async_computation | async-start | bytes 15728640 | tf_op jit(solution)/shard_map/all_to_all | solution.py:292
  172.4 350.3 %all-gather.21.cloned.1.call-start = ((), (), s32[]{:S(2)}) async-start(), calls=%async_computation.17 | async-start | bytes 8847360 | tf_op jit(solution)/shard_map/all_gather | solution.py:202
  345.0 177.8 %all-to-all-start.2 = ((bf16[4,5,128,1536]{3,2,1,0:T(8,128)(2,1)}), bf16[4,5,128,1536]{3,2,1,0:T(8,128)(2,1)}, u32[]{:S(2)}, u32[]{:S(2)}) async-start(bf16[4,5,128,1536]{3,2,1,0:T(8,128)(2,1)} %bitcast.348), calls=%async_computation.2 | async-start | bytes 15728640 | tf_op jit(solution)/shard_map/all_to_all | solution.py:342
  535.9 12.0 copy-start.6
  568.1 176.9 %all-to-all-start.3 = ((bf16[4,5,128,1536]{3,2,1,0:T(8,128)(2,1)}), bf16[4,5,128,1536]{3,2,1,0:T(8,128)(2,1)}, u32[]{:S(2)}, u32[]{:S(2)}) async-start(bf16[4,5,128,1536]{3,2,1,0:T(8,128)(2,1)} %copy.122), calls=%async_computation.3 | async-start | bytes 15728640 | tf_op jit(solution)/shard_map/all_to_all | solution.py:358
  592.1 158.6 %copy-start.31 = (s32[1280]{0:T(1024)S(1)}, s32[1280]{0:T(1024)}, u32[]{:S(2)}) copy-start(s32[1280]{0:T(1024)} %copy-done.30) | copy-start | bytes 15364
  745.0 176.8 %all-to-all-start.1 = ((bf16[4,5,128,1536]{3,2,1,0:T(8,128)(2,1)}), bf16[4,5,128,1536]{3,2,1,0:T(8,128)(2,1)}, u32[]{:S(2)}, u32[]{:S(2)}) async-start(bf16[4,5,128,1536]{3,2,1,0:T(8,128)(2,1)} %copy.119), calls=%async_computation.1 | async-start | bytes 15728640 | tf_op jit(solution)/shard_map/all_to_all | solution.py:301
  750.5 284.8 %reduce-scatter.10.cloned.1.call-start = ((), (), s32[]{:S(2)}) async-start(), calls=%async_computation.18 | async-start | bytes 819200 | tf_op jit(solution)/shard_map/reduce_scatter | solution.py:404
  1013.8 22.6 %copy-start.8 = (f32[160,32]{1,0:T(8,128)S(1)}, f32[160,32]{1,0:T(8,128)}, u32[]{:S(2)}) copy-start(f32[160,32]{1,0:T(8,128)} %copy-done.7) | copy-start | bytes 61444
  1013.8 22.6 %copy-start.10 = (f32[160,32]{1,0:T(8,128)S(1)}, f32[160,32]{1,0:T(8,128)}, u32[]{:S(2)}) copy-start(f32[160,32]{1,0:T(8,128)} %copy-done.9) | copy-start | bytes 61444
  1013.8 23.4 %copy-start.1 = (bf16[160,1536]{1,0:T(8,128)(2,1)S(1)}, bf16[160,1536]{1,0:T(8,128)(2,1)}, u32[]{:S(2)}) copy-start(bf16[160,1536]{1,0:T(8,128)(2,1)} %param.19) | copy-start | bytes 1474564
  1013.8 23.3 %copy-start.22 = (f32[1536]{0:T(1024)S(1)}, f32[1536]{0:T(1024)}, u32[]{:S(2)}) copy-start(f32[1536]{0:T(1024)} %copy-done.21) | copy-start | bytes 18436
  1013.8 23.3 %copy-start.29 = (f32[160]{0:T(256)S(1)}, f32[160]{0:T(256)}, u32[]{:S(2)}) copy-start(f32[160]{0:T(256)} %copy-done.28) | copy-start | bytes 1924
  1015.0 44.3 %reduce-scatter.22.cloned.1.call-start = ((), (), s32[]{:S(2)}) async-start(), calls=%async_computation.24 | async-start | bytes 819200
  1017.2 98.2 %reduce-scatter.14.cloned.1.call-start = ((), (), s32[]{:S(2)}) async-start(), calls=%async_computation.20 | async-start | bytes 1769472 | tf_op jit(solution)/shard_map/reduce_scatter | solution.py:458
  1037.2 24.8 %copy-start.14 = (bf16[160,512]{1,0:T(8,128)(2,1)}, bf16[160,512]{1,0:T(8,128)(2,1)S(1)}, u32[]{:S(2)}) copy-start(bf16[160,512]{1,0:T(8,128)(2,1)S(1)} %convert_element_type.247) | copy-start | bytes 491524
  1037.2 24.9 %copy-start.13 = (f32[8,160,3,64]{1,3,2,0:T(8,128)S(1)}, f32[8,160,3,64]{1,3,2,0:T(8,128)}, u32[]{:S(2)}) copy-start(f32[8,160,3,64]{1,3,2,0:T(8,128)} %get-tuple-element.105) | copy-start | bytes 2949124
  1039.1 103.7 %reduce-scatter.16.cloned.1.call-start = ((), (), s32[]{:S(2)}) async-start(), calls=%async_computation.21 | async-start | bytes 1769472 | tf_op jit(solution)/shard_map/reduce_scatter | solution.py:461
  1062.0 137.9 %reduce-scatter.12.cloned.1.call-start = ((), (), s32[]{:S(2)}) async-start(), calls=%async_computation.19 | async-start | bytes 5308416 | tf_op jit(solution)/shard_map/reduce_scatter | solution.py:455
  1077.4 180.3 %reduce-scatter.18.cloned.1.call-start = ((), (), s32[]{:S(2)}) async-start(), calls=%async_computation.22 | async-start | bytes 5308416 | tf_op jit(solution)/shard_map/reduce_scatter | solution.py:464
  1082.2 263.9 %all-reduce.14.cloned.1.call-start = ((), (), s32[]{:S(2)}) async-start(), calls=%async_computation.25 | async-start | bytes 3145728 | tf_op jit(solution)/shard_map/psum | solution.py:471
  1094.0 11.7 copy-start.5
  1257.7 232.1 %reduce-scatter.20.cloned.1.call-start = ((), (), s32[]{:S(2)}) async-start(), calls=%async_computation.23 | async-start | bytes 28311552 | tf_op jit(solution)/shard_map/reduce_scatter | solution.py:368
  1310.9 6.3 copy-start.12
  1310.9 6.3 copy-start.23
  1315.1 29.7 %copy-start.34 = (f32[160]{0:T(256)S(1)}, f32[160]{0:T(256)}, u32[]{:S(2)}) copy-start(f32[160]{0:T(256)} %get-tuple-element.315) | copy-start | bytes 1924
  (12 other events, 40.3 us)
Sparse Core Ops, SparseCore 0:
  10.0 28.5 all-gather.8
  40.5 25.8 all-gather.10
  68.3 38.9 all-gather.12
  109.0 38.9 all-gather.14
  149.7 52.1 all-gather.18
  203.7 52.1 all-gather.16
  257.8 52.1 all-gather.20
  1015.1 20.1 reduce-scatter.9
  1038.2 21.0 reduce-scatter.21
  1063.0 37.3 reduce-scatter.13
  1104.2 38.4 reduce-scatter.15
  1146.0 53.8 reduce-scatter.11
  1203.7 53.8 reduce-scatter.17
  1260.1 70.2 all-reduce.13
  1333.9 155.9 reduce-scatter.19
where the time goes:
time: 1520 us; the launch traced here: 1510 us
  waiting for transfers between devices  918 us (60%)
  matrix products  222 us (15%)
  local copies, waits for them, and re-layouts  172 us (11%)
  blocking collectives  84.2 us (6%)
  other arithmetic  70.6 us (5%)
  starting transfers between devices  23.8 us (2%)
  between operations  16.5 us (1%)
    all_to_all x1, waiting for transfers between devices, shards(): lax.all_to_all(grad_rows, 'expert', split_axis=0, concat_axis=0, tiled=True)  153 us
    all_to_all x1, waiting for transfers between devices, shards(): lax.all_to_all(outgoing, 'expert', split_axis=0, concat_axis=0, tiled=True)  149 us
    all_to_all x1, waiting for transfers between devices, shards(): lax.all_to_all(grad_outgoing, 'expert', split_axis=0, concat_axis=0, tile...  148 us
    all_to_all x1, waiting for transfers between devices, shards(): lax.all_to_all(produced, 'expert', split_axis=0, concat_axis=0, tiled=True)  146 us
    reduce_scatter x1, waiting for transfers between devices, shards(): lax.psum_scatter(jnp.concatenate([part_gate, part_up, part_down], axis=1)...  136 us
    reduce_scatter x1, waiting for transfers between devices, shards(): lax.psum_scatter(term_out.astype(jnp.bfloat16), 'dp', scatter_dimension=0...  57.8 us
    reduce_scatter x1, waiting for transfers between devices, shards(): lax.psum_scatter(term_query.astype(jnp.bfloat16), 'dp', scatter_dimension...  57.2 us
    concatenate x1, local copies, waits for them, and re-layouts, shards(): jnp.concatenate([part_gate, part_up, part_down], axis=1)  32.3 us
  transfers between devices with their start and end apart: 19, of which 11 were waited for; matrix products, arithmetic and copies ran while one was open for 21% of the time, Pallas kernels for 0%

commit v1 on v0

v1 whole, which is shorter than its diff:
```python
import functools

import jax
import jax.numpy as jnp
from jax import lax
from jax.sharding import PartitionSpec as P

QUERY_HEADS = 24
KEY_VALUE_HEADS = 8
HEAD_SIZE = 64
TOP = 8

epsilon = 1e-06
rope_base = 10000.0
score_scale = 0.015625
branch_scale = 0.22
F32 = jnp.float32
BF16 = jnp.bfloat16


def layout(lengths_row, order_row, span):
    seqs = lengths_row.shape[0]
    slot_ids = jnp.arange(seqs, dtype=jnp.int32)
    picked = jnp.sum(
        jnp.where(order_row[:, None] == slot_ids[None, :], lengths_row[None, :], 0), axis=1
    )
    before = slot_ids[:, None] >= slot_ids[None, :]
    seq_ends = jnp.sum(jnp.where(before, picked[None, :], 0), axis=1)
    place = jnp.arange(span, dtype=jnp.int32)
    passed = place[:, None] >= seq_ends[None, :]
    segment = jnp.sum(passed.astype(jnp.int32), axis=1)
    start = jnp.sum(jnp.where(passed, picked[None, :], 0), axis=1)
    return segment, (place - start).astype(F32)


def rotation(position):
    half = HEAD_SIZE // 2
    frequency = rope_base ** (-(jnp.arange(half, dtype=F32) * (2.0 / HEAD_SIZE)))
    angles = position[:, None] * frequency[None, :]
    return jnp.cos(angles), jnp.sin(angles)


def rotate(rows, cosine, sine, back=False):
    t = rows.shape[0]
    heads = rows.reshape(t, -1, 2, HEAD_SIZE // 2)
    a, b = heads[:, :, 0], heads[:, :, 1]
    c, s = cosine[:, None, :], sine[:, None, :]
    if back:
        s = -s
    return jnp.stack([a * c - b * s, b * c + a * s], axis=2).reshape(t, -1)


def dot(a, b):
    return jnp.dot(a, b, preferred_element_type=F32)


def dot_nt(a, b):
    return jnp.einsum("tc,dc->td", a, b, preferred_element_type=F32)


def dot_tn(a, b):
    return jnp.einsum("td,tc->dc", a, b, preferred_element_type=F32)


def rms_factor(rows):
    return lax.rsqrt(jnp.mean(rows * rows, axis=-1, keepdims=True) + epsilon)


def norm_back(rows, factor, gain, grad):
    scaled = gain * grad
    return factor * scaled - rows * (factor * factor * factor) * jnp.mean(
        scaled * rows, axis=-1, keepdims=True
    )


def gather(x, axis):
    return lax.all_gather(x, axis, axis=0, tiled=True)


def scatter(x, axis):
    return lax.psum_scatter(x.astype(BF16), axis, scatter_dimension=0, tiled=True).astype(F32)


def attend_forward(q, k, v, allowed):
    scores = jnp.einsum("irh,jh->rij", q, k, preferred_element_type=F32) * score_scale
    scores = jnp.where(allowed[None], scores, -1e30)
    peak = jnp.max(scores, axis=-1, keepdims=True)
    exponent = jnp.exp(scores - peak)
    total = jnp.sum(exponent, axis=-1, keepdims=True)
    probs = exponent / total
    return jnp.einsum("rij,jh->irh", probs.astype(BF16), v, preferred_element_type=F32), probs


def attend_backward(q, k, v, probs, grad, allowed):
    grad_probs = jnp.einsum("irh,jh->rij", grad, v, preferred_element_type=F32)
    inner = jnp.sum(probs * grad_probs, axis=-1, keepdims=True)
    grad_scores = (probs * (grad_probs - inner)).astype(BF16)
    grad_q = jnp.einsum("rij,jh->irh", grad_scores, k, preferred_element_type=F32) * score_scale
    grad_k = jnp.einsum("rij,irh->jh", grad_scores, q, preferred_element_type=F32) * score_scale
    grad_v = jnp.einsum("rij,irh->jh", probs.astype(BF16), grad, preferred_element_type=F32)
    return grad_q, grad_k, grad_v


def shards(
    tokens,
    cotangent,
    gain_attn,
    gain_ffn,
    w_query,
    key_weight,
    value_weight,
    w_out,
    expert_gate,
    expert_up,
    expert_down,
    expert_ids,
    gates,
    lengths,
    order,
):
    rows, width = tokens.shape
    members = lax.axis_size("expert")
    member = lax.axis_index("expert")
    span = rows * members
    own_experts, ff = expert_gate.shape[1], expert_gate.shape[2]
    capacity = rows * TOP // own_experts
    q_cols = w_query.shape[1] // members
    kv_cols = key_weight.shape[1] // members
    kv_heads = kv_cols // HEAD_SIZE
    repeat = QUERY_HEADS // KEY_VALUE_HEADS

    def mine(weight, cols):
        return lax.dynamic_slice_in_dim(weight, member * cols, cols, axis=1)

    tokens_all = gather(tokens, "expert").astype(F32)
    packed = jnp.concatenate(
        [
            mine(w_query, q_cols),
            mine(key_weight, kv_cols),
            mine(value_weight, kv_cols),
            mine(w_out, q_cols),
            gain_attn[:, None],
            gain_ffn[:, None],
            jnp.zeros((gain_attn.shape[0], 126), BF16),
        ],
        axis=1,
    )
    packed_all = gather(packed, "dp")
    qkv_cols = q_cols + 2 * kv_cols
    w_qkv = packed_all[:, :qkv_cols]
    wo = packed_all[:, qkv_cols : qkv_cols + q_cols]
    gain_one = packed_all[:, qkv_cols + q_cols].astype(F32)
    gain_two = packed_all[:, qkv_cols + q_cols + 1].astype(F32)
    gate_all = gather(expert_gate.reshape(-1, own_experts * ff), "dp")
    up_all = gather(expert_up.reshape(-1, own_experts * ff), "dp")
    down_all = gather(expert_down.reshape(-1, own_experts * ff), "dp")
    ids_all = gather(expert_ids, "expert")
    gates_all = gather(gates, "expert")
    cot_all = gather(cotangent, "expert")

    segment, position = layout(lengths[0], order[0], span)
    cosine, sine = rotation(position)
    place = jnp.arange(span, dtype=jnp.int32)
    allowed = (segment[:, None] == segment[None, :]) & (place[None, :] <= place[:, None])
    factor_one = rms_factor(tokens_all)
    normed_attn = (tokens_all * factor_one * gain_one).astype(BF16)
    qkv = dot(normed_attn, w_qkv)
    qk = rotate(qkv[:, : q_cols + kv_cols], cosine, sine).astype(BF16)
    v = qkv[:, q_cols + kv_cols :].astype(BF16)
    q_heads = jnp.moveaxis(qk[:, :q_cols].reshape(span, kv_heads, repeat, HEAD_SIZE), 1, 0)
    k_heads = jnp.moveaxis(qk[:, q_cols:].reshape(span, kv_heads, HEAD_SIZE), 1, 0)
    v_heads = jnp.moveaxis(v.reshape(span, kv_heads, HEAD_SIZE), 1, 0)
    attended, probs = jax.vmap(functools.partial(attend_forward, allowed=allowed))(
        q_heads, k_heads, v_heads
    )
    attended = jnp.moveaxis(attended, 0, 1).reshape(span, q_cols).astype(BF16)
    attn_out = scatter(dot_nt(attended, wo), "expert")
    residual = tokens.astype(F32) + branch_scale * attn_out
    factor_two = rms_factor(residual)
    normed_all = gather((residual * factor_two * gain_two).astype(BF16), "expert")

    expert_of = member * own_experts + jnp.arange(own_experts, dtype=jnp.int32)
    named = ids_all[None, :, :] == expert_of[:, None, None]
    chosen = jnp.any(named, axis=2)
    weight = jnp.sum(jnp.where(named, gates_all[None], 0.0), axis=2)
    upto = (place[:, None] <= place[None, :]).astype(BF16)
    slot = dot(chosen.astype(BF16), upto).astype(jnp.int32) - 1
    slots = jnp.arange(capacity, dtype=jnp.int32)
    picks = chosen[:, None, :] & (slot[:, None, :] == slots[None, :, None])
    pick = picks.astype(BF16)
    slot_weight = jnp.sum(jnp.where(picks, weight[:, None, :], 0.0), axis=2)
    mixture = jnp.zeros((span, width), F32)
    grad_normed = jnp.zeros((span, width), F32)
    expert_grads = []
    for e in range(own_experts):
        cols = slice(e * ff, (e + 1) * ff)
        w_gate, w_up, w_down = gate_all[:, cols], up_all[:, cols], down_all[:, cols]
        here = pick[e]
        gate_col = slot_weight[e][:, None]
        received = dot(here, normed_all).astype(BF16)
        pre_gate, pre_up = dot(received, w_gate), dot(received, w_up)
        sig = jax.nn.sigmoid(pre_gate)
        silu = pre_gate * sig
        activ = (silu * pre_up).astype(BF16)
        produced = (gate_col * dot_nt(activ, w_down)).astype(BF16)
        mixture = mixture + dot_tn(here, produced)
        grad_out = (gate_col * (branch_scale * dot(here, cot_all))).astype(BF16)
        grad_activ = dot(grad_out, w_down)
        grad_gate = (grad_activ * pre_up * sig * (1.0 + pre_gate * (1.0 - sig))).astype(BF16)
        grad_up = (grad_activ * silu).astype(BF16)
        grad_pair = (dot_nt(grad_gate, w_gate) + dot_nt(grad_up, w_up)).astype(BF16)
        grad_normed = grad_normed + dot_tn(here, grad_pair)
        expert_grads.append(
            (dot_tn(received, grad_gate), dot_tn(received, grad_up), dot_tn(grad_out, activ))
        )
    output = (residual + branch_scale * scatter(mixture, "expert")).astype(BF16)
    summed = [
        scatter(jnp.stack([one[i] for one in expert_grads], axis=1), "dp") for i in range(3)
    ]

    grad_norm_own = scatter(grad_normed, "expert")
    gain_two_part = jnp.sum(grad_norm_own * residual * factor_two, axis=0)
    grad_residual = cotangent.astype(F32) + norm_back(
        residual, factor_two, gain_two, grad_norm_own
    )
    grad_attn_out = gather((branch_scale * grad_residual).astype(BF16), "expert")
    term_out = dot_tn(grad_attn_out, attended)
    grad_attended = dot(grad_attn_out, wo).astype(BF16)
    grad_heads = jnp.moveaxis(grad_attended.reshape(span, kv_heads, repeat, HEAD_SIZE), 1, 0)
    grad_q, grad_k, grad_v = jax.vmap(functools.partial(attend_backward, allowed=allowed))(
        q_heads, k_heads, v_heads, probs, grad_heads
    )
    grad_qk = jnp.concatenate(
        [
            jnp.moveaxis(grad_q, 0, 1).reshape(span, q_cols),
            jnp.moveaxis(grad_k, 0, 1).reshape(span, kv_cols),
        ],
        axis=1,
    )
    grad_qkv = jnp.concatenate(
        [
            rotate(grad_qk, cosine, sine, back=True).astype(BF16),
            jnp.moveaxis(grad_v, 0, 1).reshape(span, kv_cols).astype(BF16),
        ],
        axis=1,
    )
    grad_norm_part = dot_nt(grad_qkv, w_qkv)
    gain_one_part = jnp.sum(grad_norm_part * tokens_all * factor_one, axis=0)
    term_qkv = dot_tn(normed_attn, grad_qkv)
    packed_grads = jnp.concatenate(
        [
            term_qkv,
            term_out,
            gain_one_part[:, None],
            gain_two_part[:, None],
            jnp.zeros((width, 126), F32),
        ],
        axis=1,
    )
    packed_own = scatter(packed_grads, "dp").astype(BF16)
    per_member = lax.all_gather(packed_own, "expert", axis=0).astype(F32)

    def columns(first, cols):
        part = per_member[:, :, first : first + cols]
        return jnp.moveaxis(part, 0, 1).reshape(part.shape[1], -1)

    grad_norm_attn = scatter(grad_norm_part, "expert")
    own_tokens = tokens.astype(F32)
    grad_tokens = grad_residual + norm_back(
        own_tokens, rms_factor(own_tokens), gain_one, grad_norm_attn
    )
    gains = jnp.sum(per_member[:, :, qkv_cols + q_cols :], axis=0)
    return (
        output,
        grad_tokens,
        gains[:, 0],
        gains[:, 1],
        columns(0, q_cols),
        columns(q_cols, kv_cols),
        columns(q_cols + kv_cols, kv_cols),
        columns(qkv_cols, q_cols),
        summed[0],
        summed[1],
        summed[2],
    )


def solution(mesh):
    both = P(("dp", "expert"), None)
    row, rows = P("dp"), P("dp", None)
    experts = P("dp", "expert", None)
    return jax.shard_map(
        shards,
        mesh=mesh,
        in_specs=(both, both, row, row, rows, rows, rows, rows)
        + (experts, experts, experts, both, both, rows, rows),
        out_specs=(both, both, row, row, rows, rows, rows, rows, experts, experts, experts),
        check_vma=False,
    )
```

time: 1520 us -> 1030 us (0.68)
  waiting for transfers between devices: 918 us -> 694 us
  local copies, waits for them, and re-layouts: 172 us -> 44.2 us
  blocking collectives: 84.2 us -> 27.1 us
  other arithmetic: 70.6 us -> 40.3 us
  matrix products: 222 us -> 196 us
  starting transfers between devices: 23.8 us -> 1.33 us
    all_to_all x4 -> x0, waiting for transfers between devices: 595 us -> none  [the longest x1 153 us: shards(): lax.all_to_all(grad_rows, 'expert', split_axis=0, concat_axis=0, tiled=True)]
    all_gather x7 -> x9, waiting for transfers between devices: 2.12 us -> 328 us  [the longest x8 288 us: gather(): return lax.all_gather(x, axis, axis=0, tiled=True)]
    reduce_scatter x6 -> x8, waiting for transfers between devices: 296 us -> 364 us  [scatter(): lax.psum_scatter(x.astype(BF16), axis, scatter_dimension=0, tiled=True)]
    gather x9 -> x0, local copies, waits for them, and re-layouts: 61.9 us -> none  [the longest x1 19.6 us: shards(): jnp.concatenate([grad_pairs, zero_row], axis=0)[pair_table]]
    dot_general x79 -> x67, matrix products: 222 us -> 190 us  [the longest x27 91.9 us: dot_tn(): return jnp.einsum('td,tc->dc', a, b, preferred_element_type=F32)]
    unnamed x2 -> x0, blocking collectives: 29.3 us -> none
    concatenate x5 -> x2, local copies, waits for them, and re-layouts: 48.1 us -> 19.2 us  [the longest x1 18.3 us: shards(): jnp.concatenate([term_qkv, term_out, gain_one_part[:, None], gain_two_par...]
    all_to_all x4 -> x0, starting transfers between devices: 22.7 us -> none  [the longest x1 6.02 us: shards(): lax.all_to_all(grad_outgoing, 'expert', split_axis=0, concat_axis=0, tile...]
  transfers between devices with their start and end apart: 19 -> 17, of which waited for: 11 -> 16; matrix products, arithmetic and copies ran while one was open for 21% -> 13% of each run, Pallas kernels for 0% -> 0%
where the time goes in v1:
time: 1030 us; the launch traced here: 1020 us
  waiting for transfers between devices  694 us (67%)
  matrix products  196 us (19%)
  local copies, waits for them, and re-layouts  44.2 us (4%)
  other arithmetic  40.3 us (4%)
  blocking collectives  27.1 us (3%)
  between operations  15.4 us (1%)
    reduce_scatter x8, waiting for transfers between devices, scatter(): lax.psum_scatter(x.astype(BF16), axis, scatter_dimension=0, tiled=True)  364 us
    all_gather x8, waiting for transfers between devices, gather(): return lax.all_gather(x, axis, axis=0, tiled=True)  288 us
    dot_general x27, matrix products, dot_tn(): return jnp.einsum('td,tc->dc', a, b, preferred_element_type=F32)  91.9 us
    dot_general x28, matrix products, dot(): return jnp.dot(a, b, preferred_element_type=F32)  59.1 us
    all_gather x1, waiting for transfers between devices, shards(): per_member = lax.all_gather(packed_own, 'expert', axis=0).astype(F32)  39.1 us
    all_gather x2, blocking collectives, gather(): return lax.all_gather(x, axis, axis=0, tiled=True)  27.1 us
  transfers between devices with their start and end apart: 17, of which 16 were waited for; matrix products, arithmetic and copies ran while one was open for 13% of the time, Pallas kernels for 0%

profile of v1, /device:TPU:0, one launch (start us, length us, event | category | flops | bytes accessed | tf_op | source)
XLA Modules:
  0.0 1017.9 jit_solution(8621647131437678482)
XLA Ops:
  14.1 41.8 %all-gather.13.cloned.1.call-done = bf16[640,1536]{1,0:T(8,128)(2,1)} async-done(((bf16[160,1536]{1,0:T(8,128)(2,1)}), bf16[640,1536]{1,0:T(8,128)(2,1)}) %all-gather.13.cloned.1.call-update) | async-done | bytes 1966096 | tf_op jit(solution)/shard_map/all_gather | solution.py:77
  57.9 33.3 %all-gather.15.cloned.1.call-done = bf16[1536,1152]{1,0:T(8,128)(2,1)} async-done(((bf16[192,1152]{1,0:T(8,128)(2,1)}), bf16[1536,1152]{1,0:T(8,128)(2,1)}) %all-gather.15.cloned.1.call-update) | async-done | bytes 3538960 | tf_op jit(solution)/shard_map/all_gather | solution.py:77
  92.8 4.0 fusion.65
  97.3 6.0 fusion.194
  103.3 4.7 fusion.143
  108.1 4.0 convolution_convert_fusion.1
  112.8 41.0 %reduce-scatter.11.cloned.1.call-done = bf16[160,1536]{1,0:T(8,128)(2,1)} async-done(((bf16[640,1536]{1,0:T(8,128)(2,1)}), bf16[160,1536]{1,0:T(8,128)(2,1)}) %reduce-scatter.11.cloned.1.call-update) | async-done | bytes 491536 | tf_op jit(solution)/shard_map/reduce_scatter | solution.py:81
  163.9 13.4 %all-gather.1 = s32[4,160,8]{1,2,0:T(8,128)S(1)} all-gather(s32[1,160,8]{1,2,0:T(8,128)S(1)} %bitcast.318), channel_id=1, replica_groups=mesh['dp'=8,'expert'=4] {'expert'}, dimensions={0}, use_global_device_ids=true | all-gather | bytes 25600 | tf_op jit(solution)/shard_map/all_gather | solution.py:77
  177.4 13.6 %all-gather.2 = f32[4,160,8]{1,2,0:T(8,128)S(1)} all-gather(f32[1,160,8]{1,2,0:T(8,128)S(1)} %bitcast.319), channel_id=1, replica_groups=mesh['dp'=8,'expert'=4] {'expert'}, dimensions={0}, use_global_device_ids=true | all-gather | bytes 25600 | tf_op jit(solution)/shard_map/all_gather | solution.py:77
  193.0 6.1 all-gather.25.cloned.1.call-done
  199.1 3.4 fusion.58
  209.3 34.2 %all-gather.17.cloned.1.call-done = bf16[640,1536]{1,0:T(8,128)(2,1)} async-done(((bf16[160,1536]{1,0:T(8,128)(2,1)}), bf16[640,1536]{1,0:T(8,128)(2,1)}) %all-gather.17.cloned.1.call-update) | async-done | bytes 1966096 | tf_op jit(solution)/shard_map/all_gather | solution.py:77
  251.9 44.9 %all-gather.21.cloned.1.call-done = bf16[1536,2560]{1,0:T(8,128)(2,1)} async-done(((bf16[192,2560]{1,0:T(8,128)(2,1)}), bf16[1536,2560]{1,0:T(8,128)(2,1)}) %all-gather.21.cloned.1.call-update) | async-done | bytes 7864336 | tf_op jit(solution)/shard_map/all_gather | solution.py:77
  299.6 51.9 %all-gather.19.cloned.1.call-done = bf16[1536,2560]{1,0:T(8,128)(2,1)} async-done(((bf16[192,2560]{1,0:T(8,128)(2,1)}), bf16[1536,2560]{1,0:T(8,128)(2,1)}) %all-gather.19.cloned.1.call-update) | async-done | bytes 7864336 | tf_op jit(solution)/shard_map/all_gather | solution.py:77
  372.6 33.5 %all-gather.23.cloned.1.call-done = bf16[1536,2560]{1,0:T(8,128)(2,1)} async-done(((bf16[192,2560]{1,0:T(8,128)(2,1)}), bf16[1536,2560]{1,0:T(8,128)(2,1)}) %all-gather.23.cloned.1.call-update) | async-done | bytes 7864336 | tf_op jit(solution)/shard_map/all_gather | solution.py:77
  406.2 3.3 multiply_convert_fusion.8
  414.2 3.3 fusion.115
  427.5 5.0 fusion.120
  432.5 5.0 fusion.123
  437.5 5.0 fusion.129
  442.5 4.5 fusion.126
  447.0 9.3 add_convert_fusion
  456.4 41.6 %reduce-scatter.15.cloned.1.call-done = bf16[160,1536]{1,0:T(8,128)(2,1)} async-done(((bf16[640,1536]{1,0:T(8,128)(2,1)}), bf16[160,1536]{1,0:T(8,128)(2,1)}) %reduce-scatter.15.cloned.1.call-update) | async-done | bytes 491536 | tf_op jit(solution)/shard_map/reduce_scatter | solution.py:81
  502.6 42.7 %all-gather.27.cloned.1.call-done = bf16[640,1536]{1,0:T(8,128)(2,1)} async-done(((bf16[160,1536]{1,0:T(8,128)(2,1)}), bf16[640,1536]{1,0:T(8,128)(2,1)}) %all-gather.27.cloned.1.call-update) | async-done | bytes 1966096 | tf_op jit(solution)/shard_map/all_gather | solution.py:77
  545.3 3.2 convolution_convert_fusion.23
  548.5 6.3 fusion.152
  554.8 4.5 fusion.1
  559.3 10.1 fusion.3
  569.5 4.2 fusion.149
  577.2 3.2 fusion.12
  582.5 3.1 convolution_convert_fusion
  585.7 18.3 %concatenate.16 = bf16[1536,1152]{0,1:T(8,128)(2,1)} concatenate(bf16[1536,640]{0,1:T(8,128)(2,1)} %convolution_convert_fusion, bf16[1536,384]{0,1:T(8,128)(2,1)} %convolution_convert_fusion.17, bf16[1536,1]{0,1:T(2,128)(2,1)S(1)} %broadcast_in_dim.142, bf16[1536,1]{0,1:T(2,128)(2,1)S(1)} %broadcast_in_dim.143, bf16[1536,126]{0,1:T(8,128)(2,1)S(1)} %broadcast_in_dim.144), dimensions={1} | concatenate | bytes 7077888 | tf_op jit(solution)/shard_map/concatenate | solution.py:250
  603.9 5.8 copy.114
  610.7 4.5 fusion.138
  615.2 4.7 fusion.141
  619.9 4.7 fusion.135
  624.6 4.6 fusion.132
  629.1 9.3 add_convert_fusion.1
  638.5 3.0 fusion.35
  649.6 3.0 fusion.25
  660.6 3.0 fusion.15
  671.4 29.7 %reduce-scatter.17.cloned.1.call-done = bf16[160,1536]{1,0:T(8,128)(2,1)} async-done(((bf16[640,1536]{1,0:T(8,128)(2,1)}), bf16[160,1536]{1,0:T(8,128)(2,1)}) %reduce-scatter.17.cloned.1.call-update) | async-done | bytes 491536 | tf_op jit(solution)/shard_map/reduce_scatter | solution.py:81
  702.3 42.3 %reduce-scatter.13.cloned.1.call-done = bf16[160,1536]{1,0:T(8,128)(2,1)} async-done(((bf16[640,1536]{1,0:T(8,128)(2,1)}), bf16[160,1536]{1,0:T(8,128)(2,1)}) %reduce-scatter.13.cloned.1.call-update) | async-done | bytes 491536 | tf_op jit(solution)/shard_map/reduce_scatter | solution.py:81
  744.7 3.1 fusion.171
  747.8 68.9 %reduce-scatter.23.cloned.1.call-done = bf16[192,5,512]{2,0,1:T(8,128)(2,1)} async-done(((bf16[1536,5,512]{2,0,1:T(8,128)(2,1)}), bf16[192,5,512]{2,0,1:T(8,128)(2,1)}) %reduce-scatter.23.cloned.1.call-update) | async-done | bytes 983056 | tf_op jit(solution)/shard_map/reduce_scatter | solution.py:81
  819.4 70.3 %reduce-scatter.21.cloned.1.call-done = bf16[192,5,512]{2,0,1:T(8,128)(2,1)} async-done(((bf16[1536,5,512]{2,0,1:T(8,128)(2,1)}), bf16[192,5,512]{2,0,1:T(8,128)(2,1)}) %reduce-scatter.21.cloned.1.call-update) | async-done | bytes 983056 | tf_op jit(solution)/shard_map/reduce_scatter | solution.py:81
  892.4 70.0 %reduce-scatter.19.cloned.1.call-done = bf16[192,5,512]{2,0,1:T(8,128)(2,1)} async-done(((bf16[1536,5,512]{2,0,1:T(8,128)(2,1)}), bf16[192,5,512]{2,0,1:T(8,128)(2,1)}) %reduce-scatter.19.cloned.1.call-update) | async-done | bytes 983056 | tf_op jit(solution)/shard_map/reduce_scatter | solution.py:81
  965.2 39.1 %all-gather.29.cloned.1.call-done = bf16[768,1152]{1,0:T(8,128)(2,1)} async-done(((bf16[192,1152]{1,0:T(8,128)(2,1)}), bf16[768,1152]{1,0:T(8,128)(2,1)}) %all-gather.29.cloned.1.call-update) | async-done | bytes 1769488 | tf_op jit(solution)/shard_map/all_gather | solution.py:261
  (352 shorter events, 128.2 us)
Async XLA Ops:
  7.2 48.7 %all-gather.13.cloned.1.call-start = ((), (), s32[]{:S(2)}) async-start(), calls=%async_computation.8 | async-start | bytes 2457600 | tf_op jit(solution)/shard_map/all_gather | solution.py:77
  7.9 83.3 %all-gather.15.cloned.1.call-start = ((), (), s32[]{:S(2)}) async-start(), calls=%async_computation.9 | async-start | bytes 3981312 | tf_op jit(solution)/shard_map/all_gather | solution.py:77
  12.3 141.5 %reduce-scatter.11.cloned.1.call-start = ((), (), s32[]{:S(2)}) async-start(), calls=%async_computation.10 | async-start | bytes 2457600 | tf_op jit(solution)/shard_map/reduce_scatter | solution.py:81
  57.9 38.9 %copy-start.60 = (f32[640]{0:T(1024)}, f32[640]{0:T(1024)S(1)}, u32[]{:S(2)}) copy-start(f32[640]{0:T(1024)S(1)} %add_rsqrt_fusion) | copy-start | bytes 7684
  96.8 6.5 copy-start.37
  108.1 46.9 %copy-start.65 = (bf16[2,64,3,640]{3,1,2,0:T(8,128)(2,1)}, bf16[2,64,3,640]{3,1,2,0:T(8,128)(2,1)S(1)}, u32[]{:S(2)}) copy-start(bf16[2,64,3,640]{3,1,2,0:T(8,128)(2,1)S(1)} %fusion.143) | copy-start | bytes 1474564
  108.1 45.6 %copy-start.1 = (bf16[160,1536]{1,0:T(8,128)(2,1)S(1)}, bf16[160,1536]{1,0:T(8,128)(2,1)}, u32[]{:S(2)}) copy-start(bf16[160,1536]{1,0:T(8,128)(2,1)} %param.15) | copy-start | bytes 1474564
  112.1 45.6 %copy-start.10 = (bf16[192,5,512]{2,0,1:T(8,128)(2,1)S(1)}, bf16[192,5,512]{2,0,1:T(8,128)(2,1)}, u32[]{:S(2)}) copy-start(bf16[192,5,512]{2,0,1:T(8,128)(2,1)} %param.24) | copy-start | bytes 2949124
  112.1 87.0 %all-gather.25.cloned.1.call-start = ((), (), s32[]{:S(2)}) async-start(), calls=%async_computation.16 | async-start | bytes 2457600 | tf_op jit(solution)/shard_map/all_gather | solution.py:77
  112.7 130.8 %all-gather.17.cloned.1.call-start = ((), (), s32[]{:S(2)}) async-start(), calls=%async_computation.11 | async-start | bytes 2457600 | tf_op jit(solution)/shard_map/all_gather | solution.py:77
  157.7 139.1 %all-gather.21.cloned.1.call-start = ((), (), s32[]{:S(2)}) async-start(), calls=%async_computation.13 | async-start | bytes 8847360 | tf_op jit(solution)/shard_map/all_gather | solution.py:77
  159.7 191.8 %all-gather.19.cloned.1.call-start = ((), (), s32[]{:S(2)}) async-start(), calls=%async_computation.12 | async-start | bytes 8847360 | tf_op jit(solution)/shard_map/all_gather | solution.py:77
  161.8 15.6 %copy-start.58 = (f32[160,8]{0,1:T(8,128)S(1)}, f32[160,8]{0,1:T(8,128)}, u32[]{:S(2)}) copy-start(f32[160,8]{0,1:T(8,128)} %param.27) | copy-start | bytes 15364
  161.8 244.4 %all-gather.23.cloned.1.call-start = ((), (), s32[]{:S(2)}) async-start(), calls=%async_computation.14 | async-start | bytes 8847360 | tf_op jit(solution)/shard_map/all_gather | solution.py:77
  163.8 334.1 %reduce-scatter.15.cloned.1.call-start = ((), (), s32[]{:S(2)}) async-start(), calls=%async_computation.17 | async-start | bytes 2457600 | tf_op jit(solution)/shard_map/reduce_scatter | solution.py:81
  192.3 11.9 %copy-start.47 = (f32[1,256]{1,0:T(1,128)}, f32[1,256]{1,0:T(1,128)S(1)}, u32[]{:S(2)}) copy-start(f32[1,256]{1,0:T(1,128)S(1)} %get-tuple-element.48) | copy-start | bytes 3076
  192.3 11.9 %copy-start.49 = (f32[1,256]{1,0:T(1,128)}, f32[1,256]{1,0:T(1,128)S(1)}, u32[]{:S(2)}) copy-start(f32[1,256]{1,0:T(1,128)S(1)} %get-tuple-element.49) | copy-start | bytes 3076
  192.3 11.9 %copy-start.51 = (f32[1,256]{1,0:T(1,128)}, f32[1,256]{1,0:T(1,128)S(1)}, u32[]{:S(2)}) copy-start(f32[1,256]{1,0:T(1,128)S(1)} %get-tuple-element.50) | copy-start | bytes 3076
  192.4 11.9 %copy-start.53 = (f32[1,256]{1,0:T(1,128)}, f32[1,256]{1,0:T(1,128)S(1)}, u32[]{:S(2)}) copy-start(f32[1,256]{1,0:T(1,128)S(1)} %get-tuple-element.52) | copy-start | bytes 3076
  192.4 11.9 %copy-start.55 = (f32[1,256]{1,0:T(1,128)}, f32[1,256]{1,0:T(1,128)S(1)}, u32[]{:S(2)}) copy-start(f32[1,256]{1,0:T(1,128)S(1)} %get-tuple-element.51) | copy-start | bytes 3076
  246.0 105.5 %copy-start.68 = (bf16[256,1536]{1,0:T(8,128)(2,1)}, bf16[256,1536]{1,0:T(8,128)(2,1)S(1)}, u32[]{:S(2)}) copy-start(bf16[256,1536]{1,0:T(8,128)(2,1)S(1)} %convolution_convert_fusion.18) | copy-start | bytes 2359300
  246.8 110.5 %copy-start.70 = (bf16[256,1536]{1,0:T(8,128)(2,1)}, bf16[256,1536]{1,0:T(8,128)(2,1)S(1)}, u32[]{:S(2)}) copy-start(bf16[256,1536]{1,0:T(8,128)(2,1)S(1)} %convolution_convert_fusion.19) | copy-start | bytes 2359300
  351.5 8.6 copy-start.4
  368.5 37.7 %copy-start.85 = (bf16[256,1536]{1,0:T(8,128)(2,1)S(1)}, bf16[256,1536]{1,0:T(8,128)(2,1)}, u32[]{:S(2)}) copy-start(bf16[256,1536]{1,0:T(8,128)(2,1)} %fusion.55) | copy-start | bytes 2359300
  406.2 6.4 copy-start.3
  409.4 33.0 %copy-start.16 = (bf16[256,512]{1,0:T(8,128)(2,1)}, bf16[256,512]{1,0:T(8,128)(2,1)S(1)}, u32[]{:S(2)}) copy-start(bf16[256,512]{1,0:T(8,128)(2,1)S(1)} %get-tuple-element.34) | copy-start | bytes 786436
  412.6 6.5 slice-start.3
  447.0 50.9 %copy-start.2 = (bf16[160,1536]{1,0:T(8,128)(2,1)S(1)}, bf16[160,1536]{1,0:T(8,128)(2,1)}, u32[]{:S(2)}) copy-start(bf16[160,1536]{1,0:T(8,128)(2,1)} %reduce-scatter.11.cloned.1.call-done) | copy-start | bytes 1474564
  447.0 50.9 %copy-start.40 = (f32[160]{0:T(256)S(1)}, f32[160]{0:T(256)}, u32[]{:S(2)}) copy-start(f32[160]{0:T(256)} %copy-done.39) | copy-start | bytes 1924
  456.3 43.8 %copy-start.5 = (bf16[160,1536]{1,0:T(8,128)(2,1)S(1)}, bf16[160,1536]{1,0:T(8,128)(2,1)}, u32[]{:S(2)}) copy-start(bf16[160,1536]{1,0:T(8,128)(2,1)} %param.16) | copy-start | bytes 1474564
  456.3 43.8 %copy-start.43 = (f32[160]{0:T(256)S(1)}, f32[160]{0:T(256)}, u32[]{:S(2)}) copy-start(f32[160]{0:T(256)} %get-tuple-element.58) | copy-start | bytes 1924
  456.3 89.0 %all-gather.27.cloned.1.call-start = ((), (), s32[]{:S(2)}) async-start(), calls=%async_computation.18 | async-start | bytes 2457600 | tf_op jit(solution)/shard_map/all_gather | solution.py:77
  502.3 46.1 %copy-start.42 = (f32[2,3,640]{2,1,0:T(4,128)S(1)}, f32[2,3,640]{2,1,0:T(4,128)}, u32[]{:S(2)}) copy-start(f32[2,3,640]{2,1,0:T(4,128)} %copy-done.41) | copy-start | bytes 46084
  502.3 168.5 %reduce-scatter.25.cloned.1.call-start = ((), (), s32[]{:S(2)}) async-start(), calls=%async_computation.24 | async-start | bytes 3981312 | tf_op jit(solution)/shard_map/reduce_scatter | solution.py:81
  545.3 9.5 slice-start
  548.4 6.3 slice-start.1
  548.4 6.3 slice-start.2
  548.4 6.3 copy-start.38
  559.3 10.1 copy-start.9
  609.8 91.3 %reduce-scatter.17.cloned.1.call-start = ((), (), s32[]{:S(2)}) async-start(), calls=%async_computation.19 | async-start | bytes 2457600 | tf_op jit(solution)/shard_map/reduce_scatter | solution.py:81
  610.4 134.3 %reduce-scatter.13.cloned.1.call-start = ((), (), s32[]{:S(2)}) async-start(), calls=%async_computation.15 | async-start | bytes 2457600 | tf_op jit(solution)/shard_map/reduce_scatter | solution.py:81
  638.5 178.1 %reduce-scatter.23.cloned.1.call-start = ((), (), s32[]{:S(2)}) async-start(), calls=%async_computation.22 | async-start | bytes 8847360 | tf_op jit(solution)/shard_map/reduce_scatter | solution.py:81
  648.6 241.0 %reduce-scatter.21.cloned.1.call-start = ((), (), s32[]{:S(2)}) async-start(), calls=%async_computation.21 | async-start | bytes 8847360 | tf_op jit(solution)/shard_map/reduce_scatter | solution.py:81
  659.7 302.7 %reduce-scatter.19.cloned.1.call-start = ((), (), s32[]{:S(2)}) async-start(), calls=%async_computation.20 | async-start | bytes 8847360 | tf_op jit(solution)/shard_map/reduce_scatter | solution.py:81
  670.7 73.9 %copy-start.6 = (bf16[160,1536]{1,0:T(8,128)(2,1)S(1)}, bf16[160,1536]{1,0:T(8,128)(2,1)}, u32[]{:S(2)}) copy-start(bf16[160,1536]{1,0:T(8,128)(2,1)} %reduce-scatter.15.cloned.1.call-done) | copy-start | bytes 1474564
  670.7 73.9 %copy-start.44 = (f32[160]{0:T(256)S(1)}, f32[160]{0:T(256)}, u32[]{:S(2)}) copy-start(f32[160]{0:T(256)} %get-tuple-element.58) | copy-start | bytes 1924
  670.7 73.9 %copy-start.46 = (f32[160]{0:T(256)S(1)}, f32[160]{0:T(256)}, u32[]{:S(2)}) copy-start(f32[160]{0:T(256)} %copy-done.45) | copy-start | bytes 1924
  670.8 333.5 %all-gather.29.cloned.1.call-start = ((), (), s32[]{:S(2)}) async-start(), calls=%async_computation.23 | async-start | bytes 2211840 | tf_op jit(solution)/shard_map/all_gather | solution.py:261
  (71 other events, 238.4 us)
Sparse Core Ops, SparseCore 0:
  9.6 46.2 all-gather.12
  58.3 32.7 all-gather.14
  112.2 41.4 reduce-scatter.10
  155.2 43.9 all-gather.24
  201.1 42.3 all-gather.16
  245.8 50.9 all-gather.20
  299.3 52.1 all-gather.18
  354.0 52.1 all-gather.22
  456.4 41.4 reduce-scatter.14
  502.4 42.7 all-gather.26
  609.9 46.9 reduce-scatter.24
  659.6 41.4 reduce-scatter.16
  704.0 40.6 reduce-scatter.12
  748.0 68.6 reduce-scatter.22
  820.3 69.3 reduce-scatter.20
  893.0 69.4 reduce-scatter.18
  963.9 40.2 all-gather.28

commit v2 on v1

--- a/solution.py
+++ b/solution.py
@@ -3,6 +3,8 @@
 import jax
 import jax.numpy as jnp
 from jax import lax
+from jax.experimental import pallas as pl
+from jax.experimental.pallas import tpu as pltpu
 from jax.sharding import PartitionSpec as P
 
 QUERY_HEADS = 24
@@ -16,6 +18,8 @@
 branch_scale = 0.22
 F32 = jnp.float32
 BF16 = jnp.bfloat16
+MESH = pl.DeviceIdType.MESH
+VMEM_LIMIT = 58 * 2**20
 
 
 def layout(lengths_row, order_row, span):
@@ -79,6 +83,489 @@
 
 def scatter(x, axis):
     return lax.psum_scatter(x.astype(BF16), axis, scatter_dimension=0, tiled=True).astype(F32)
+
+
+class Links:
+    def __init__(self, send, recv, local, members):
+        self.send, self.recv, self.local = send, recv, local
+        self.remotes = self.locals = 0
+        self.members = members
+        self.d, self.z = lax.axis_index("dp"), lax.axis_index("expert")
+        d = self.d
+        core, x, y = d % 2, (d // 2) % 2, d // 4
+        self.core = core
+        self.sib = d + 1 - 2 * core
+        self.x = d + 2 - 4 * x
+        self.y = d + 4 - 8 * y
+        self.diag = self.x + 4 - 8 * y
+        self.waiting = []
+
+    def other(self, d):
+        return d + 1 - 2 * self.core
+
+    def greet(self):
+        barrier = pltpu.get_barrier_semaphore()
+        last = self.members - 1
+
+        def hello(d, z):
+            pl.semaphore_signal(barrier, inc=1, device_id=(d, z), device_id_type=MESH)
+
+        for d in (self.sib, self.x, self.y):
+            hello(d, self.z)
+        pl.when(self.z > 0)(lambda: hello(self.d, self.z - 1))
+        pl.when(self.z < last)(lambda: hello(self.d, self.z + 1))
+        ends = (self.z == 0).astype(jnp.int32) + (self.z == last).astype(jnp.int32)
+        pl.semaphore_wait(barrier, 5 - ends)
+
+    def remote(self, src, dst, to):
+        k = self.remotes
+        self.remotes += 1
+        return pltpu.make_async_remote_copy(
+            src_ref=src,
+            dst_ref=dst,
+            send_sem=self.send.at[k],
+            recv_sem=self.recv.at[k],
+            device_id=to,
+            device_id_type=MESH,
+        )
+
+    def push(self, src, dst, d):
+        copy = self.remote(src, dst, (d, self.z))
+        copy.start()
+        self.waiting.append(copy.wait_send)
+        return copy
+
+    def move(self, src, dst):
+        k = self.locals
+        self.locals += 1
+        copy = pltpu.make_async_copy(src, dst, self.local.at[k])
+        copy.start()
+        return copy
+
+    def finish(self):
+        for wait in self.waiting:
+            wait()
+
+
+def run(order, **chains):
+    for name in order:
+        next(chains[name], None)
+    chains = list(chains.values())
+    while chains:
+        for chain in list(chains):
+            try:
+                next(chain)
+            except StopIteration:
+                chains.remove(chain)
+
+
+def line_gather(links, own, full):
+    z, last = links.z, links.members - 1
+    local = links.move(own, full.at[z])
+    right, left = (links.d, z + 1), (links.d, z - 1)
+    to_right, to_left = [], []
+    for s in range(last):
+        at_r, at_l = jnp.maximum(z - s, 0), jnp.minimum(z + s, last)
+        to_right.append(links.remote(own if s == 0 else full.at[at_r], full.at[at_r], right))
+        to_left.append(links.remote(own if s == 0 else full.at[at_l], full.at[at_l], left))
+    for s in range(last):
+        send_r, send_l = (z < last) & (z >= s), (z > 0) & (z + s <= last)
+        pl.when(send_r)(to_right[s].start)
+        pl.when(send_l)(to_left[s].start)
+        yield
+        pl.when((z > 0) & (z - 1 >= s))(to_right[s].wait_recv)
+        pl.when((z < last) & (z + 1 + s <= last))(to_left[s].wait_recv)
+    for s in range(last):
+        send_r, send_l = (z < last) & (z >= s), (z > 0) & (z + s <= last)
+        pl.when(send_r)(to_right[s].wait_send)
+        pl.when(send_l)(to_left[s].wait_send)
+    local.wait()
+
+
+def add_rows(target, other, step=16):
+    rows = target.shape[0]
+
+    @pl.loop(0, rows // step)
+    def _(i):
+        at = pl.ds(pl.multiple_of(i * step, step), step)
+        target[at] = (target[at].astype(F32) + other[at].astype(F32)).astype(target.dtype)
+
+
+def line_scatter(links, part, acc, from_left, from_right):
+    z, last = links.z, links.members - 1
+    links.move(part, acc).wait()
+    to_right = {o: links.remote(acc.at[o], from_left.at[o], (links.d, z + 1)) for o in range(1, last + 1)}
+    to_left = {o: links.remote(acc.at[o], from_right.at[o], (links.d, z - 1)) for o in range(last)}
+
+    def pass_right(o):
+        @pl.when(z > 0)
+        def _():
+            to_right[o].wait_recv()
+            add_rows(acc.at[o], from_left.at[o])
+
+        to_right[o].start()
+
+    def pass_left(o):
+        @pl.when(z < last)
+        def _():
+            to_left[o].wait_recv()
+            add_rows(acc.at[o], from_right.at[o])
+
+        to_left[o].start()
+
+    @pl.when(z == 0)
+    def _():
+        from_left[0] = jnp.zeros(from_left.shape[1:], from_left.dtype)
+
+    @pl.when(z == last)
+    def _():
+        from_right[last] = jnp.zeros(from_right.shape[1:], from_right.dtype)
+
+    for j in range(last):
+        pl.when(z < last - j)(functools.partial(pass_right, last - j))
+        pl.when(z > j)(functools.partial(pass_left, j))
+        yield
+    for o in range(last + 1):
+
+        @pl.when(z == o)
+        def _(o=o):
+            if o > 0:
+                to_right[o].wait_recv()
+            if o < last:
+                to_left[o].wait_recv()
+
+    for o in range(last + 1):
+        if o > 0:
+            pl.when(z < o)(to_right[o].wait_send)
+        if o < last:
+            pl.when(z > o)(to_left[o].wait_send)
+
+
+def plane_gather(links, own, full):
+    half = own.shape[0] // 2
+    first, second = pl.ds(0, half), pl.ds(half, half)
+    me = links.d
+    local = links.move(own, full.at[me])
+    by_x, by_y = {}, {}
+    for by, d, h in ((by_y, links.y, first), (by_x, links.x, second), (by_x, links.x, first), (by_y, links.y, second)):
+        by[h.start // half] = links.push(own.at[h], full.at[me, h], d)
+    to_sib = [links.push(own, full.at[me], links.sib)]
+
+    def share(d, h):
+        to_sib.append(links.push(full.at[d, h], full.at[d, h], links.sib))
+
+    yield
+    by_y[0].wait_recv()
+    over_x = links.push(full.at[links.y, first], full.at[links.y, first], links.x)
+    share(links.y, first)
+    by_x[1].wait_recv()
+    over_y = links.push(full.at[links.x, second], full.at[links.x, second], links.y)
+    share(links.x, second)
+    yield
+    by_x[0].wait_recv()
+    share(links.x, first)
+    by_y[1].wait_recv()
+    share(links.y, second)
+    yield
+    over_x.wait_recv()
+    share(links.diag, first)
+    over_y.wait_recv()
+    share(links.diag, second)
+    yield
+    for copy in to_sib:
+        copy.wait_recv()
+    local.wait()
+
+
+def plane_scatter(links, part, mine, theirs, mid_x, mid_y, end_x, end_y):
+    half = part.shape[1] // 2
+    first, second = pl.ds(0, half), pl.ds(half, half)
+    chips = (links.d, links.x, links.y, links.diag)
+    from_sib, load = {}, {}
+    for k in (3, 1, 2, 0):
+        from_sib[k] = links.push(part.at[links.other(chips[k])], theirs.at[k], links.sib)
+        load[k] = links.move(part.at[chips[k]], mine.at[k])
+    yield
+    for k in (3, 1, 2):
+        load[k].wait()
+        from_sib[k].wait_recv()
+        add_rows(mine.at[k], theirs.at[k])
+        if k == 3:
+            to_mid_x = links.push(mine.at[3, first], mid_x, links.x)
+            to_mid_y = links.push(mine.at[3, second], mid_y, links.y)
+        if k == 1:
+            to_end_x = links.push(mine.at[1, first], end_x.at[first], links.x)
+        if k == 2:
+            to_end_y = links.push(mine.at[2, second], end_y.at[second], links.y)
+    yield
+    to_mid_y.wait_recv()
+    add_rows(mine.at[1, second], mid_y)
+    rest_x = links.push(mine.at[1, second], end_x.at[second], links.x)
+    to_mid_x.wait_recv()
+    add_rows(mine.at[2, first], mid_x)
+    rest_y = links.push(mine.at[2, first], end_y.at[first], links.y)
+    yield
+    load[0].wait()
+    from_sib[0].wait_recv()
+    to_end_x.wait_recv()
+    to_end_y.wait_recv()
+    rest_x.wait_recv()
+    rest_y.wait_recv()
+
+
+def plane_scratch(rows, cols):
+    return [
+        pltpu.VMEM((4, rows, cols), BF16),
+        pltpu.VMEM((4, rows, cols), BF16),
+        pltpu.VMEM((rows // 2, cols), BF16),
+        pltpu.VMEM((rows // 2, cols), BF16),
+        pltpu.VMEM((rows, cols), BF16),
+        pltpu.VMEM((rows, cols), BF16),
+    ]
+
+
+def plane_result(mine, theirs, end_x, end_y, out, step=16):
+    @pl.loop(0, out.shape[0] // step)
+    def _(i):
+        at = pl.ds(pl.multiple_of(i * step, step), step)
+        own = mine[0, at].astype(F32) + theirs[0, at].astype(F32)
+        out[at] = (own + end_x[at].astype(F32) + end_y[at].astype(F32)).astype(out.dtype)
+
+
+def line_result(z, acc, from_left, from_right, at):
+    return (
+        acc[z, at].astype(F32) + from_left[z, at].astype(F32) + from_right[z, at].astype(F32)
+    )
+
+
+ANY = pl.BlockSpec(memory_space=pl.ANY)
+VMEM = pl.BlockSpec(memory_space=pltpu.VMEM)
+
+
+def comm_call(kernel, name, number, members, remotes, locals_, in_specs, out_specs, out_shape, scratch):
+    return pl.pallas_call(
+        functools.partial(kernel, members),
+        out_shape=out_shape,
+        in_specs=in_specs,
+        out_specs=out_specs,
+        scratch_shapes=[
+            pltpu.SemaphoreType.DMA((remotes,)),
+            pltpu.SemaphoreType.DMA((remotes,)),
+            pltpu.SemaphoreType.DMA((locals_,)),
+            *scratch,
+        ],
+        compiler_params=pltpu.CompilerParams(
+            collective_id=number, has_side_effects=True, vmem_limit_bytes=VMEM_LIMIT
+        ),
+        name=name,
+    )
+
+
+def sds(shape, dtype):
+    return jax.ShapeDtypeStruct(shape, dtype)
+
+
+def first_kernel(members, tokens, cot, route, pack, gate, tokens_all, cot_all, route_all, pack_all, gate_all, send, recv, local):
+    links = Links(send, recv, local, members)
+    links.greet()
+    run(
+        "trpgtrptrtrgcpgcpgcpc",
+        t=line_gather(links, tokens, tokens_all),
+        r=line_gather(links, route, route_all),
+        p=plane_gather(links, pack, pack_all),
+        g=plane_gather(links, gate, gate_all),
+        c=line_gather(links, cot, cot_all),
+    )
+    links.finish()
+
+
+def first_phase(members, tokens, cot, route, pack, gate):
+    many = lambda a, n: sds((n, *a.shape), a.dtype)
+    return comm_call(
+        first_kernel, "phase_one", 1, members, 60, 8, [ANY] * 5, [ANY] * 5,
+        [many(tokens, members), many(cot, members), many(route, members), many(pack, 8), many(gate, 8)], [],
+    )(tokens, cot, route, pack, gate)
+
+
+def second_kernel(members, part, tokens, gain, up, down, residual, normed_all, up_all, down_all, send, recv, local, acc, from_left, from_right, normed):
+    links = Links(send, recv, local, members)
+    links.greet()
+
+    def chain():
+        yield from line_scatter(links, part, acc, from_left, from_right)
+
+        @pl.loop(0, tokens.shape[0] // 16)
+        def _(i):
+            at = pl.ds(pl.multiple_of(i * 16, 16), 16)
+            here = tokens[at].astype(F32) + branch_scale * line_result(links.z, acc, from_left, from_right, at)
+            residual[at] = here
+            normed[at] = (here * rms_factor(here) * gain[...]).astype(BF16)
+
+        yield from line_gather(links, normed, normed_all)
+
+    run(
+        "zudzzzzudududzud",
+        z=chain(),
+        u=plane_gather(links, up, up_all),
+        d=plane_gather(links, down, down_all),
+    )
+    links.finish()
+
+
+def second_phase(members, part, tokens, gain, up, down):
+    rows, width = tokens.shape
+    blocks = pltpu.VMEM((members, rows, width), BF16)
+    return comm_call(
+        second_kernel, "phase_two", 2, members, 60, 8,
+        [ANY, VMEM, VMEM, ANY, ANY], [VMEM, ANY, ANY, ANY],
+        [
+            sds((rows, width), F32),
+            sds((members, rows, width), BF16),
+            sds((8, *up.shape), BF16),
+            sds((8, *down.shape), BF16),
+        ],
+        [blocks, blocks, blocks, pltpu.VMEM((rows, width), BF16)],
+    )(part, tokens, gain, up, down)
+
+
+def third_kernel(members, part, residual, cot, gain, gate, up, grad_residual, gain_part, out_all, gate_out, up_out, send, recv, local, acc, from_left, from_right, grad_out, *rest):
+    links = Links(send, recv, local, members)
+    links.greet()
+    for_gate, for_up = rest[:6], rest[6:]
+
+    def chain():
+        yield from line_scatter(links, part, acc, from_left, from_right)
+        gain_part[...] = jnp.zeros(gain_part.shape, F32)
+
+        @pl.loop(0, residual.shape[0] // 16)
+        def _(i):
+            at = pl.ds(pl.multiple_of(i * 16, 16), 16)
+            grad = line_result(links.z, acc, from_left, from_right, at)
+            here = residual[at]
+            factor = rms_factor(here)
+            gain_part[...] += jnp.sum(grad * here * factor, axis=0, keepdims=True)
+            total = cot[at].astype(F32) + norm_back(here, factor, gain[...], grad)
+            grad_residual[at] = total
+            grad_out[at] = (branch_scale * total).astype(BF16)
+
+        yield from line_gather(links, grad_out, out_all)
+
+    run(
+        "zguguzzzguzgu",
+        z=chain(),
+        g=plane_scatter(links, gate, *for_gate),
+        u=plane_scatter(links, up, *for_up),
+    )
+    plane_result(for_gate[0], for_gate[1], for_gate[4], for_gate[5], gate_out)
+    plane_result(for_up[0], for_up[1], for_up[4], for_up[5], up_out)
+    links.finish()
+
+
+def third_phase(members, part, residual, cot, gain, gate, up):
+    rows, width = cot.shape
+    blocks = pltpu.VMEM((members, rows, width), BF16)
+    return comm_call(
+        third_kernel, "phase_three", 3, members, 60, 16,
+        [ANY, VMEM, VMEM, VMEM, ANY, ANY], [VMEM, VMEM, ANY, VMEM, VMEM],
+        [
+            sds((rows, width), F32),
+            sds((1, width), F32),
+            sds((members, rows, width), BF16),
+            sds(gate.shape[1:], F32),
+            sds(up.shape[1:], F32),
+        ],
+        [blocks, blocks, blocks, pltpu.VMEM((rows, width), BF16)]
+        + plane_scratch(*gate.shape[1:])
+        + plane_scratch(*up.shape[1:]),
+    )(part, residual, cot, gain, gate, up)
+
+
+def fourth_kernel(members, part, grad_residual, tokens, gain, pack, down, grad_tokens, pack_all, down_out, send, recv, local, acc, from_left, from_right, pack_own, *rest):
+    links = Links(send, recv, local, members)
+    links.greet()
+    for_pack, for_down = rest[:6], rest[6:]
+
+    def pack_chain():
+        yield from plane_scatter(links, pack, *for_pack)
+        plane_result(for_pack[0], for_pack[1], for_pack[4], for_pack[5], pack_own)
+        yield from line_gather(links, pack_own, pack_all)
+
+    run(
+        "zpdpdzppppzdpppd",
+        p=pack_chain(),
+        z=line_scatter(links, part, acc, from_left, from_right),
+        d=plane_scatter(links, down, *for_down),
+    )
+
+    @pl.loop(0, tokens.shape[0] // 16)
+    def _(i):
+        at = pl.ds(pl.multiple_of(i * 16, 16), 16)
+        grad = line_result(links.z, acc, from_left, from_right, at)
+        here = tokens[at].astype(F32)
+        grad_tokens[at] = grad_residual[at] + norm_back(here, rms_factor(here), gain[...], grad)
+
+    plane_result(for_down[0], for_down[1], for_down[4], for_down[5], down_out)
+    links.finish()
+
+
+def fourth_phase(members, part, grad_residual, tokens, gain, pack, down):
+    rows, width = tokens.shape
+    blocks = pltpu.VMEM((members, rows, width), BF16)
+    return comm_call(
+        fourth_kernel, "phase_four", 4, members, 60, 16,
+        [ANY, VMEM, VMEM, VMEM, ANY, ANY], [VMEM, ANY, VMEM],
+        [
+            sds((rows, width), F32),
+            sds((members, *pack.shape[1:]), BF16),
+            sds(down.shape[1:], F32),
+        ],
+        [blocks, blocks, blocks, pltpu.VMEM(pack.shape[1:], BF16)]
+        + plane_scratch(*pack.shape[1:])
+        + plane_scratch(*down.shape[1:]),
+    )(part, grad_residual, tokens, gain, pack, down)
+
+
+def all_blocks(x, axis):
+    return lax.all_gather(x, axis, axis=0)
+
+
+def plain_first(members, tokens, cot, route, pack, gate):
+    return (
+        all_blocks(tokens, "expert"),
+        all_blocks(cot, "expert"),
+        all_blocks(route, "expert"),
+        all_blocks(pack, "dp"),
+        all_blocks(gate, "dp"),
+    )
+
+
+def line_sum(part):
+    return scatter(part.reshape(-1, part.shape[2]), "expert")
+
+
+def plain_second(members, part, tokens, gain, up, down):
+    residual = tokens.astype(F32) + branch_scale * line_sum(part)
+    normed = (residual * rms_factor(residual) * gain).astype(BF16)
+    return residual, all_blocks(normed, "expert"), all_blocks(up, "dp"), all_blocks(down, "dp")
+
+
+def plane_sum(part):
+    return scatter(part.reshape(-1, part.shape[2]), "dp")
+
+
+def plain_third(members, part, residual, cot, gain, gate, up):
+    grad = line_sum(part)
+    factor = rms_factor(residual)
+    gain_part = jnp.sum(grad * residual * factor, axis=0, keepdims=True)
+    total = cot.astype(F32) + norm_back(residual, factor, gain, grad)
+    out_all = all_blocks((branch_scale * total).astype(BF16), "expert")
+    return total, gain_part, out_all, plane_sum(gate), plane_sum(up)
+
+
+def plain_fourth(members, part, grad_residual, tokens, gain, pack, down):
+    here = tokens.astype(F32)
+    grad_tokens = grad_residual + norm_back(here, rms_factor(here), gain, line_sum(part))
+    return grad_tokens, all_blocks(plane_sum(pack).astype(BF16), "expert"), plane_sum(down)
 
 
 def attend_forward(q, k, v, allowed):
@@ -132,8 +619,13 @@
     def mine(weight, cols):
         return lax.dynamic_slice_in_dim(weight, member * cols, cols, axis=1)
 
-    tokens_all = gather(tokens, "expert").astype(F32)
-    packed = jnp.concatenate(
+    devices = lax.axis_size("dp")
+    phases = (plain_first, plain_second, plain_third, plain_fourth)
+    if devices == 8 and rows % 16 == 0 and width % (32 * devices) == 0:
+        phases = (first_phase, second_phase, third_phase, fourth_phase)
+    phases = [functools.partial(phase, members) for phase in phases]
+
+    pack = jnp.concatenate(
         [
             mine(w_query, q_cols),
             mine(key_weight, kv_cols),
@@ -145,18 +637,21 @@
         ],
         axis=1,
     )
-    packed_all = gather(packed, "dp")
+    route = jnp.concatenate([expert_ids.astype(F32), gates], axis=1)
+    tokens_all, cot_all, route_all, pack_all, gate_all = phases[0](
+        tokens, cotangent, route, pack, expert_gate.reshape(-1, own_experts * ff)
+    )
+    tokens_all = tokens_all.reshape(span, width).astype(F32)
+    cot_all = cot_all.reshape(span, width)
+    route_all = route_all.reshape(span, 2 * TOP)
+    ids_all, gates_all = route_all[:, :TOP].astype(jnp.int32), route_all[:, TOP:]
+    pack_all = pack_all.reshape(width, -1)
+    gate_all = gate_all.reshape(width, -1)
     qkv_cols = q_cols + 2 * kv_cols
-    w_qkv = packed_all[:, :qkv_cols]
-    wo = packed_all[:, qkv_cols : qkv_cols + q_cols]
-    gain_one = packed_all[:, qkv_cols + q_cols].astype(F32)
-    gain_two = packed_all[:, qkv_cols + q_cols + 1].astype(F32)
-    gate_all = gather(expert_gate.reshape(-1, own_experts * ff), "dp")
-    up_all = gather(expert_up.reshape(-1, own_experts * ff), "dp")
-    down_all = gather(expert_down.reshape(-1, own_experts * ff), "dp")
-    ids_all = gather(expert_ids, "expert")
-    gates_all = gather(gates, "expert")
-    cot_all = gather(cotangent, "expert")
+    w_qkv = pack_all[:, :qkv_cols]
+    wo = pack_all[:, qkv_cols : qkv_cols + q_cols]
+    gain_one = pack_all[:, qkv_cols + q_cols].astype(F32)[None]
+    gain_two = pack_all[:, qkv_cols + q_cols + 1].astype(F32)[None]
 
     segment, position = layout(lengths[0], order[0], span)
     cosine, sine = rotation(position)
@@ -174,10 +669,16 @@
         q_heads, k_heads, v_heads
     )
     attended = jnp.moveaxis(attended, 0, 1).reshape(span, q_cols).astype(BF16)
-    attn_out = scatter(dot_nt(attended, wo), "expert")
-    residual = tokens.astype(F32) + branch_scale * attn_out
-    factor_two = rms_factor(residual)
-    normed_all = gather((residual * factor_two * gain_two).astype(BF16), "expert")
+    attn_part = dot_nt(attended, wo).astype(BF16).reshape(members, rows, width)
+    residual, normed_all, up_all, down_all = phases[1](
+        attn_part,
+        tokens,
+        gain_two,
+        expert_up.reshape(-1, own_experts * ff),
+        expert_down.reshape(-1, own_experts * ff),
+    )
+    normed_all = normed_all.reshape(span, width)
+    up_all, down_all = up_all.reshape(width, -1), down_all.reshape(width, -1)
 
     expert_of = member * own_experts + jnp.arange(own_experts, dtype=jnp.int32)
     named = ids_all[None, :, :] == expert_of[:, None, None]
@@ -214,16 +715,22 @@
             (dot_tn(received, grad_gate), dot_tn(received, grad_up), dot_tn(grad_out, activ))
         )
     output = (residual + branch_scale * scatter(mixture, "expert")).astype(BF16)
-    summed = [
-        scatter(jnp.stack([one[i] for one in expert_grads], axis=1), "dp") for i in range(3)
+    by_kind = [
+        jnp.concatenate([one[i].astype(BF16) for one in expert_grads], axis=1).reshape(
+            devices, -1, own_experts * ff
+        )
+        for i in range(3)
     ]
 
-    grad_norm_own = scatter(grad_normed, "expert")
-    gain_two_part = jnp.sum(grad_norm_own * residual * factor_two, axis=0)
-    grad_residual = cotangent.astype(F32) + norm_back(
-        residual, factor_two, gain_two, grad_norm_own
-    )
-    grad_attn_out = gather((branch_scale * grad_residual).astype(BF16), "expert")
+    grad_residual, gain_two_part, grad_attn_out, sum_gate, sum_up = phases[2](
+        grad_normed.astype(BF16).reshape(members, rows, width),
+        residual,
+        cotangent,
+        gain_two,
+        by_kind[0],
+        by_kind[1],
+    )
+    grad_attn_out = grad_attn_out.reshape(span, width)
     term_out = dot_tn(grad_attn_out, attended)
     grad_attended = dot(grad_attn_out, wo).astype(BF16)
     grad_heads = jnp.moveaxis(grad_attended.reshape(span, kv_heads, repeat, HEAD_SIZE), 1, 0)
@@ -252,23 +759,25 @@
             term_qkv,
             term_out,
             gain_one_part[:, None],
-            gain_two_part[:, None],
+            gain_two_part.reshape(-1, 1),
             jnp.zeros((width, 126), F32),
         ],
         axis=1,
     )
-    packed_own = scatter(packed_grads, "dp").astype(BF16)
-    per_member = lax.all_gather(packed_own, "expert", axis=0).astype(F32)
+    grad_tokens, per_member, sum_down = phases[3](
+        grad_norm_part.astype(BF16).reshape(members, rows, width),
+        grad_residual,
+        tokens,
+        gain_one,
+        packed_grads.astype(BF16).reshape(devices, -1, packed_grads.shape[1]),
+        by_kind[2],
+    )
+    per_member = per_member.astype(F32)
 
     def columns(first, cols):
         part = per_member[:, :, first : first + cols]
         return jnp.moveaxis(part, 0, 1).reshape(part.shape[1], -1)
 
-    grad_norm_attn = scatter(grad_norm_part, "expert")
-    own_tokens = tokens.astype(F32)
-    grad_tokens = grad_residual + norm_back(
-        own_tokens, rms_factor(own_tokens), gain_one, grad_norm_attn
-    )
     gains = jnp.sum(per_member[:, :, qkv_cols + q_cols :], axis=0)
     return (
         output,
@@ -279,9 +788,9 @@
         columns(q_cols, kv_cols),
         columns(q_cols + kv_cols, kv_cols),
         columns(qkv_cols, q_cols),
-        summed[0],
-        summed[1],
-        summed[2],
+        sum_gate.reshape(-1, own_experts, ff),
+        sum_up.reshape(-1, own_experts, ff),
+        sum_down.reshape(-1, own_experts, ff),
     )
 
 

time: 1030 us -> 770 us (0.75)
  waiting for transfers between devices: 694 us -> 0.02 us
  Pallas kernels: 0 us -> 432 us
  local copies, waits for them, and re-layouts: 44.2 us -> 82.1 us
  blocking collectives: 27.1 us -> 0 us
  other arithmetic: 40.3 us -> 23.8 us
    pallas_call x0 -> x4, Pallas kernels: none -> 432 us  [the longest x1 125 us: third_phase(): comm_call(third_kernel, 'phase_three', 3, members, 60, 16, [ANY, VMEM, VM...]
    reduce_scatter x8 -> x1, waiting for transfers between devices: 364 us -> 0.01 us  [scatter(): lax.psum_scatter(x.astype(BF16), axis, scatter_dimension=0, tiled=True)]
    all_gather x9 -> x0, waiting for transfers between devices: 328 us -> none  [the longest x8 288 us: gather(): return lax.all_gather(x, axis, axis=0, tiled=True)]
    concatenate x0 -> x4, local copies, waits for them, and re-layouts: none -> 32.4 us  [the longest x3 31.7 us: shards(): jnp.concatenate([one[i].astype(BF16) for one in expert_grads], axis=1)]
    all_gather x2 -> x0, blocking collectives: 27.1 us -> none  [gather(): return lax.all_gather(x, axis, axis=0, tiled=True)]
  transfers between devices with their start and end apart: 17 -> 1, of which waited for: 16 -> 0; matrix products, arithmetic and copies ran while one was open for 13% -> 25% of each run, Pallas kernels for 0% -> 32%
where the time goes in v2:
time: 770 us; the launch traced here: 759 us
  Pallas kernels  432 us (56%)
  matrix products  205 us (27%)
  local copies, waits for them, and re-layouts  82.1 us (11%)
  other arithmetic  23.8 us (3%)
  between operations  15.2 us (2%)
    pallas_call x1, Pallas kernels, third_phase(): comm_call(third_kernel, 'phase_three', 3, members, 60, 16, [ANY, VMEM, VM...  125 us
    pallas_call x1, Pallas kernels, fourth_phase(): comm_call(fourth_kernel, 'phase_four', 4, members, 60, 16, [ANY, VMEM, VM...  118 us
    pallas_call x1, Pallas kernels, second_phase(): comm_call(second_kernel, 'phase_two', 2, members, 60, 8, [ANY, VMEM, VMEM...  109 us
    dot_general x27, matrix products, dot_tn(): return jnp.einsum('td,tc->dc', a, b, preferred_element_type=F32)  98 us
    pallas_call x1, Pallas kernels, first_phase(): comm_call(first_kernel, 'phase_one', 1, members, 60, 8, [ANY] * 5, [ANY]...  80.8 us
    dot_general x28, matrix products, dot(): return jnp.dot(a, b, preferred_element_type=F32)  55.1 us
    concatenate x3, local copies, waits for them, and re-layouts, shards(): jnp.concatenate([one[i].astype(BF16) for one in expert_grads], axis=1)  31.7 us
    dot_general x7, matrix products, dot_nt(): return jnp.einsum('tc,dc->td', a, b, preferred_element_type=F32)  23.9 us
  transfers between devices with their start and end apart: 1, of which 0 were waited for; matrix products, arithmetic and copies ran while one was open for 25% of the time, Pallas kernels for 32%

profile of v2, /device:TPU:0, one launch (start us, length us, event | category | flops | bytes accessed | tf_op | source)
XLA Modules:
  0.0 758.7 jit_solution(1652535431927920710)
XLA Ops:
  16.5 80.8 %phase_one.1 = (bf16[4,160,1536]{2,1,0:T(8,128)(2,1)}, bf16[4,160,1536]{2,1,0:T(8,128)(2,1)}, f32[4,160,16]{2,1,0:T(8,128)}, bf16[8,192,1152]{2,1,0:T(8,128)(2,1)}, bf16[8,192,2560]{2,1,0:T(8,128)(2,1)}) custom-call(bf16[160,1536]{1,0:T(8,128)(2,1)} %tokens.5, bf16[160,1536]{1,0:T(8,128)(2,1)} %cot.3, f32[160,16]{1,0:T(8,128)} %copy.157.route, ...), custom_call_target="tpu_custom_call" | custom-call | tf_op jit(solution)/shard_map/phase_one/pallas_call | solution.py:384
  115.8 6.0 fusion.168
  121.8 4.7 fusion.128
  126.6 4.0 convolution_convert_fusion
  130.5 108.6 %phase_two.1 = (f32[160,1536]{1,0:T(8,128)}, bf16[4,160,1536]{2,1,0:T(8,128)(2,1)}, bf16[8,192,2560]{2,1,0:T(8,128)(2,1)}, bf16[8,192,2560]{2,1,0:T(8,128)(2,1)}) custom-call(bf16[4,160,1536]{2,1,0:T(8,128)(2,1)} %bitcast.309, bf16[160,1536]{1,0:T(8,128)(2,1)} %tokens.5, f32[1,1536]{1,0:T(1,128)} %bitcast_convert_fusion.gain, bf16[192,2560]{1,0:T(8,128)(2,1)} %copy.164.up, ...), custom_call_target="tpu_custom_call" | custom-call | tf_op jit(solution)/shard_map/phase_two/pallas_call | solution.py:418
  242.5 3.4 fusion.58
  245.9 2.9 fusion.62
  250.2 2.9 fusion.72
  264.8 3.3 fusion.43
  276.8 4.9 fusion.123
  281.8 3.3 multiply_convert_fusion.8
  285.1 4.4 fusion.126
  289.5 3.3 multiply_convert_fusion.4
  292.9 4.6 fusion.120
  297.4 3.4 multiply_convert_fusion.2
  300.9 4.5 fusion.117
  305.4 3.4 multiply_convert_fusion
  308.8 8.8 %add_convert_fusion.1 = bf16[640,1536]{1,0:T(8,128)(2,1)} fusion(f32[640,1536]{1,0:T(8,128)} %fusion.117, f32[640,1536]{1,0:T(8,128)} %fusion.120, f32[640,1536]{1,0:T(8,128)} %fusion.126, f32[640,1536]{1,0:T(8,128)} %fusion.123, bf16[256,512]{1,0:T(8,128)(2,1)S(1)} %get-tuple-element.119, bf16[1536,2560]{1,0:T(8,128)(2,1)} %bitcast.286, ...), kind=kOutput, calls=%fused_computation.22 | convolution fusion | flops 911671296 | bytes 19694592 | tf_op jit(solution)/shard_map/td,tc->dc/dot_general | solution.py:66
  317.6 2.9 fusion.18
  320.5 3.4 fusion.100
  325.7 3.3 fusion.90
  328.9 3.2 fusion.80
  334.2 3.2 fusion.60
  339.2 5.2 fusion.114
  344.4 5.0 fusion.111
  349.4 2.9 fusion.22
  352.3 5.0 fusion.108
  357.4 3.0 fusion.21
  360.3 4.6 fusion.105
  365.0 3.0 fusion.20
  369.8 10.4 %copy.169 = bf16[1536,2560]{1,0:T(8,128)(2,1)} copy(bf16[1536,2560]{0,1:T(8,128)(2,1)} %fusion.19) | data formatting | bytes 15728640 | tf_op jit(solution)/shard_map/concatenate | solution.py:719
  380.2 3.1 fusion.27
  388.7 10.8 %copy.168 = bf16[1536,2560]{1,0:T(8,128)(2,1)} copy(bf16[1536,2560]{0,1:T(8,128)(2,1)} %fusion.24) | data formatting | bytes 15728640 | tf_op jit(solution)/shard_map/concatenate | solution.py:719
  399.4 8.7 %add_convert_fusion = bf16[640,1536]{1,0:T(8,128)(2,1)} fusion(f32[640,1536]{1,0:T(8,128)} %fusion.105, f32[640,1536]{1,0:T(8,128)} %fusion.108, f32[640,1536]{1,0:T(8,128)} %fusion.114, f32[640,1536]{1,0:T(8,128)} %fusion.111, f32[256,1536]{1,0:T(8,128)S(1)} %copy-done.5, bf16[256,512]{1,0:T(8,128)(2,1)S(1)} %copy-done.31, ...), kind=kOutput, calls=%fused_computation.21 | convolution fusion | flops 911671296 | bytes 21266432 | tf_op jit(solution)/shard_map/td,tc->dc/dot_general | solution.py:66
  408.2 125.0 %phase_three.1 = (f32[160,1536]{1,0:T(8,128)}, f32[1,1536]{1,0:T(1,128)}, bf16[4,160,1536]{2,1,0:T(8,128)(2,1)}, f32[192,2560]{1,0:T(8,128)}, f32[192,2560]{1,0:T(8,128)}) custom-call(bf16[4,160,1536]{2,1,0:T(8,128)(2,1)} %bitcast.299, f32[160,1536]{1,0:T(8,128)} %get-tuple-element.30.residual, bf16[160,1536]{1,0:T(8,128)(2,1)} %cot.3, ...), custom_call_target="tpu_custom_call" | custom-call | tf_op jit(solution)/shard_map/phase_three/pallas_call | solution.py:467
  533.1 3.2 convolution_convert_fusion.23
  536.3 5.6 fusion.135
  542.0 4.6 fusion.1
  549.0 3.1 fusion.17
  555.6 10.2 %fusion.3 = bf16[2,3,640,640]{2,3,1,0:T(8,128)(2,1)} fusion(f32[2,640,640,3]{2,1,3,0:T(8,128)} %get-tuple-element.145, f32[2,3,640]{2,1,0:T(4,128)S(1)} %get-tuple-element.144, f32[2,3,640,640]{2,3,1,0:T(8,128)} %get-tuple-element.143, f32[2,3,640]{2,1,0:T(4,128)S(1)} %copy-done.51), kind=kLoop, calls=%fused_computation.5 | loop fusion | flops 9830400 | bytes 24606720 | tf_op jit(solution)/shard_map/vmap()/convert_element_type | solution.py:584
  567.6 10.5 %copy.180 = bf16[1536,2560]{1,0:T(8,128)(2,1)} copy(bf16[1536,2560]{0,1:T(8,128)(2,1)} %fusion.14) | data formatting | bytes 15728640 | tf_op jit(solution)/shard_map/concatenate | solution.py:719
  589.4 3.4 convolution_multiply_fusion.10
  592.8 4.0 fusion.134
  599.1 4.8 fusion.12
  604.7 3.9 convolution_convert_fusion.22
  608.6 4.3 convolution_convert_fusion.21
  613.0 6.7 concatenate.38.pack
  620.3 117.9 %phase_four.1 = (f32[160,1536]{1,0:T(8,128)}, bf16[4,192,1152]{2,1,0:T(8,128)(2,1)}, f32[192,2560]{1,0:T(8,128)}) custom-call(bf16[4,160,1536]{2,1,0:T(8,128)(2,1)} %bitcast.314, f32[160,1536]{1,0:T(8,128)} %get-tuple-element.38.grad_residual, bf16[160,1536]{1,0:T(8,128)(2,1)} %tokens.5, f32[1,1536]{1,0:T(1,128)} %convert_bitcast_fusion.gain, ...), custom_call_target="tpu_custom_call" | custom-call | tf_op jit(solution)/shard_map/phase_four/pallas_call | solution.py:514
  (256 shorter events, 101.4 us)
Async XLA Ops:
  7.2 741.6 %reduce-scatter.2.cloned.1.call-start = ((), (), s32[]{:S(2)}) async-start(), calls=%async_computation.1 | async-start | bytes 2457600 | tf_op jit(solution)/shard_map/reduce_scatter | solution.py:85
  97.3 3.8 copy-start
  101.1 3.8 copy-start.48
  107.8 8.0 %copy-start.40 = (bf16[640,128]{0,1:T(8,128)(2,1)}, bf16[640,128]{0,1:T(8,128)(2,1)S(1)}, u32[]{:S(2)}) copy-start(bf16[640,128]{0,1:T(8,128)(2,1)S(1)} %slice.191) | copy-start | bytes 491524
  107.9 7.9 %copy-start.14 = (bf16[640,384]{0,1:T(8,128)(2,1)}, bf16[640,384]{0,1:T(8,128)(2,1)S(1)}, u32[]{:S(2)}) copy-start(bf16[640,384]{0,1:T(8,128)(2,1)S(1)} %slice.192) | copy-start | bytes 1474564
  107.9 6.2 copy-start.55
  115.8 6.0 copy-start.46
  121.8 4.7 copy-start.50
  126.6 112.6 %copy-start.61 = (bf16[2,64,3,640]{3,1,2,0:T(8,128)(2,1)}, bf16[2,64,3,640]{3,1,2,0:T(8,128)(2,1)S(1)}, u32[]{:S(2)}) copy-start(bf16[2,64,3,640]{3,1,2,0:T(8,128)(2,1)S(1)} %fusion.128) | copy-start | bytes 1474564
  241.7 7.1 copy-start.4
  242.5 7.7 %copy-start.7 = (bf16[256,1536]{1,0:T(8,128)(2,1)}, bf16[256,1536]{1,0:T(8,128)(2,1)S(1)}, u32[]{:S(2)}) copy-start(bf16[256,1536]{1,0:T(8,128)(2,1)S(1)} %convolution_convert_fusion.17) | copy-start | bytes 2359300
  245.9 9.4 %slice-start.3 = ((s8[7864320]{0:T(1024)(128)(4,1)}), s8[4194304]{0:T(1024)(128)(4,1)S(1)}, s32[]{:S(2)}) async-start(s8[7864320]{0:T(1024)(128)(4,1)} %bitcast.294), calls=%async_computation.5 | async-start | bytes 8388608
  250.2 5.1 slice-start.4
  257.5 4.9 copy-start.11
  263.9 4.3 copy-start.57
  272.3 4.5 copy-start.37
  276.8 4.9 copy-start.17
  276.8 48.8 %copy-start.23 = (bf16[256,512]{1,0:T(8,128)(2,1)}, bf16[256,512]{1,0:T(8,128)(2,1)S(1)}, u32[]{:S(2)}) copy-start(bf16[256,512]{1,0:T(8,128)(2,1)S(1)} %get-tuple-element.121) | copy-start | bytes 786436
  292.9 4.6 copy-start.19
  292.9 36.1 %copy-start.24 = (bf16[256,512]{1,0:T(8,128)(2,1)}, bf16[256,512]{1,0:T(8,128)(2,1)S(1)}, u32[]{:S(2)}) copy-start(bf16[256,512]{1,0:T(8,128)(2,1)S(1)} %get-tuple-element.127) | copy-start | bytes 786436
  300.9 4.5 copy-start.21
  320.5 3.4 copy-start.63
  328.9 3.2 copy-start.26
  334.2 3.2 copy-start.44
  380.2 3.1 copy-start.10
  380.2 3.1 copy-start.25
  380.2 4.9 copy-start.8
  380.2 4.9 copy-start.27
  383.3 3.6 copy-start.29
  388.6 10.8 %copy-start.5 = (f32[256,1536]{1,0:T(8,128)S(1)}, f32[256,1536]{1,0:T(8,128)}, u32[]{:S(2)}) copy-start(f32[256,1536]{1,0:T(8,128)} %fusion.60) | copy-start | bytes 4718596
  388.6 10.8 %copy-start.31 = (bf16[256,512]{1,0:T(8,128)(2,1)S(1)}, bf16[256,512]{1,0:T(8,128)(2,1)}, u32[]{:S(2)}) copy-start(bf16[256,512]{1,0:T(8,128)(2,1)} %get-tuple-element.117) | copy-start | bytes 786436
  533.1 3.2 copy-start.51
  533.1 8.8 %slice-start = ((s8[9830400]{0:T(1024)(128)(4,1)}), s8[4194304]{0:T(1024)(128)(4,1)S(1)}, s32[]{:S(2)}) async-start(s8[9830400]{0:T(1024)(128)(4,1)} %bitcast.264), calls=%async_computation.2 | async-start | bytes 8388608
  536.3 5.7 slice-start.1
  536.3 5.7 slice-start.2
  536.3 5.7 copy-start.47
  542.0 4.6 copy-start.3
  546.6 5.4 copy-start.20
  548.9 4.9 copy-start.22
  548.9 4.9 copy-start.35
  555.6 10.2 %copy-start.34 = (bf16[256,1536]{1,0:T(8,128)(2,1)S(1)}, bf16[256,1536]{1,0:T(8,128)(2,1)}, u32[]{:S(2)}) copy-start(bf16[256,1536]{1,0:T(8,128)(2,1)} %fusion.43) | copy-start | bytes 2359300
  567.6 10.5 %copy-start.54 = (f32[1,1536]{1,0:T(1,128)S(1)}, f32[1,1536]{1,0:T(1,128)}, u32[]{:S(2)}) copy-start(f32[1,1536]{1,0:T(1,128)} %get-tuple-element.39) | copy-start | bytes 18436
  567.6 11.4 %copy-start.13 = (bf16[4,160,1536]{2,1,0:T(8,128)(2,1)S(1)}, bf16[4,160,1536]{2,1,0:T(8,128)(2,1)}, u32[]{:S(2)}) copy-start(bf16[4,160,1536]{2,1,0:T(8,128)(2,1)} %get-tuple-element.37) | copy-start | bytes 5898244
  589.4 3.4 copy-start.15
  604.0 4.6 copy-start.12
  613.0 6.7 copy-start.49
  745.3 3.5 copy-start.6
  746.9 3.9 copy-start.33
  (24 other events, 46.6 us)
Sparse Core Ops, SparseCore 0:
  317.7 38.6 reduce-scatter.1

commit v3 on v2

--- a/solution.py
+++ b/solution.py
@@ -193,7 +193,13 @@
 
 def line_scatter(links, part, acc, from_left, from_right):
     z, last = links.z, links.members - 1
-    links.move(part, acc).wait()
+    made = set()
+
+    def make(o):
+        if o not in made:
+            made.add(o)
+            part(o)
+
     to_right = {o: links.remote(acc.at[o], from_left.at[o], (links.d, z + 1)) for o in range(1, last + 1)}
     to_left = {o: links.remote(acc.at[o], from_right.at[o], (links.d, z - 1)) for o in range(last)}
 
@@ -222,8 +228,11 @@
         from_right[last] = jnp.zeros(from_right.shape[1:], from_right.dtype)
 
     for j in range(last):
-        pl.when(z < last - j)(functools.partial(pass_right, last - j))
+        make(last - j)
+        make(j)
+        pl.when((z < last - j) & (2 * z < last))(functools.partial(pass_right, last - j))
         pl.when(z > j)(functools.partial(pass_left, j))
+        pl.when((z < last - j) & (2 * z >= last))(functools.partial(pass_right, last - j))
         yield
     for o in range(last + 1):
 
@@ -365,76 +374,14 @@
     return jax.ShapeDtypeStruct(shape, dtype)
 
 
-def first_kernel(members, tokens, cot, route, pack, gate, tokens_all, cot_all, route_all, pack_all, gate_all, send, recv, local):
-    links = Links(send, recv, local, members)
-    links.greet()
-    run(
-        "trpgtrptrtrgcpgcpgcpc",
-        t=line_gather(links, tokens, tokens_all),
-        r=line_gather(links, route, route_all),
-        p=plane_gather(links, pack, pack_all),
-        g=plane_gather(links, gate, gate_all),
-        c=line_gather(links, cot, cot_all),
-    )
-    links.finish()
-
-
-def first_phase(members, tokens, cot, route, pack, gate):
-    many = lambda a, n: sds((n, *a.shape), a.dtype)
-    return comm_call(
-        first_kernel, "phase_one", 1, members, 60, 8, [ANY] * 5, [ANY] * 5,
-        [many(tokens, members), many(cot, members), many(route, members), many(pack, 8), many(gate, 8)], [],
-    )(tokens, cot, route, pack, gate)
-
-
-def second_kernel(members, part, tokens, gain, up, down, residual, normed_all, up_all, down_all, send, recv, local, acc, from_left, from_right, normed):
-    links = Links(send, recv, local, members)
-    links.greet()
-
-    def chain():
-        yield from line_scatter(links, part, acc, from_left, from_right)
-
-        @pl.loop(0, tokens.shape[0] // 16)
-        def _(i):
-            at = pl.ds(pl.multiple_of(i * 16, 16), 16)
-            here = tokens[at].astype(F32) + branch_scale * line_result(links.z, acc, from_left, from_right, at)
-            residual[at] = here
-            normed[at] = (here * rms_factor(here) * gain[...]).astype(BF16)
-
-        yield from line_gather(links, normed, normed_all)
-
-    run(
-        "zudzzzzudududzud",
-        z=chain(),
-        u=plane_gather(links, up, up_all),
-        d=plane_gather(links, down, down_all),
-    )
-    links.finish()
-
-
-def second_phase(members, part, tokens, gain, up, down):
-    rows, width = tokens.shape
-    blocks = pltpu.VMEM((members, rows, width), BF16)
-    return comm_call(
-        second_kernel, "phase_two", 2, members, 60, 8,
-        [ANY, VMEM, VMEM, ANY, ANY], [VMEM, ANY, ANY, ANY],
-        [
-            sds((rows, width), F32),
-            sds((members, rows, width), BF16),
-            sds((8, *up.shape), BF16),
-            sds((8, *down.shape), BF16),
-        ],
-        [blocks, blocks, blocks, pltpu.VMEM((rows, width), BF16)],
-    )(part, tokens, gain, up, down)
-
-
 def third_kernel(members, part, residual, cot, gain, gate, up, grad_residual, gain_part, out_all, gate_out, up_out, send, recv, local, acc, from_left, from_right, grad_out, *rest):
     links = Links(send, recv, local, members)
     links.greet()
     for_gate, for_up = rest[:6], rest[6:]
 
     def chain():
-        yield from line_scatter(links, part, acc, from_left, from_right)
+        links.move(part, acc).wait()
+        yield from line_scatter(links, lambda o: None, acc, from_left, from_right)
         gain_part[...] = jnp.zeros(gain_part.shape, F32)
 
         @pl.loop(0, residual.shape[0] // 16)
@@ -490,10 +437,11 @@
         plane_result(for_pack[0], for_pack[1], for_pack[4], for_pack[5], pack_own)
         yield from line_gather(links, pack_own, pack_all)
 
+    links.move(part, acc).wait()
     run(
         "zpdpdzppppzdpppd",
         p=pack_chain(),
-        z=line_scatter(links, part, acc, from_left, from_right),
+        z=line_scatter(links, lambda o: None, acc, from_left, from_right),
         d=plane_scatter(links, down, *for_down),
     )
 
@@ -525,6 +473,250 @@
     )(part, grad_residual, tokens, gain, pack, down)
 
 
+def dims(a, b):
+    return (((a,), (b,)), ((), ()))
+
+
+def mm(a, b):
+    return lax.dot_general(a, b, dims(1, 0), preferred_element_type=F32)
+
+
+def mm_nt(a, b):
+    return lax.dot_general(a, b, dims(1, 1), preferred_element_type=F32)
+
+
+def mm_tn(a, b):
+    return lax.dot_general(a, b, dims(0, 0), preferred_element_type=F32)
+
+
+def expert_kernel(capacity, slot_row, slot_col, weight_row, normed, cot, w_gate, w_up, w_down, mixture, grad_normed, d_gate, d_up, d_down, mix_sum, grad_sum):
+    e = pl.program_id(0)
+    span = normed.shape[0]
+
+    @pl.when(e == 0)
+    def _():
+        mix_sum[...] = jnp.zeros(mix_sum.shape, F32)
+        grad_sum[...] = jnp.zeros(grad_sum.shape, F32)
+
+    slots = slot_row[0]
+    picks = slots == lax.broadcasted_iota(jnp.int32, (capacity, span), 0)
+    pick = picks.astype(BF16)
+    gate_col = jnp.sum(jnp.where(picks, weight_row[0], 0.0), axis=1, keepdims=True)
+    put = (slot_col[0] == lax.broadcasted_iota(jnp.int32, (span, capacity), 1)).astype(BF16)
+    received = mm(pick, normed[...]).astype(BF16)
+    pre_gate, pre_up = mm(received, w_gate[...]), mm(received, w_up[...])
+    sig = 1.0 / (1.0 + jnp.exp(-pre_gate))
+    silu = pre_gate * sig
+    activ = (silu * pre_up).astype(BF16)
+    produced = (gate_col * mm_nt(activ, w_down[...])).astype(BF16)
+    mix_sum[...] += mm(put, produced)
+    grad_out = (gate_col * (branch_scale * mm(pick, cot[...]))).astype(BF16)
+    grad_activ = mm(grad_out, w_down[...])
+    grad_gate = (grad_activ * pre_up * (sig * (1.0 + pre_gate * (1.0 - sig)))).astype(BF16)
+    grad_up = (grad_activ * silu).astype(BF16)
+    grad_pair = (mm_nt(grad_gate, w_gate[...]) + mm_nt(grad_up, w_up[...])).astype(BF16)
+    grad_sum[...] += mm(put, grad_pair)
+    d_gate[...] = mm_tn(received, grad_gate).astype(BF16)
+    d_up[...] = mm_tn(received, grad_up).astype(BF16)
+    d_down[...] = mm_tn(grad_out, activ).astype(BF16)
+
+    @pl.when(e == pl.num_programs(0) - 1)
+    def _():
+        mixture[...] = mix_sum[...].astype(BF16)
+        grad_normed[...] = grad_sum[...].astype(BF16)
+
+
+def experts(slot, weight, normed, cot, w_gate, w_up, w_down, ff, capacity):
+    own_experts, span = slot.shape
+    width = normed.shape[1]
+    whole = pl.BlockSpec((span, width), lambda e: (0, 0))
+    column = pl.BlockSpec((width, ff), lambda e: (0, e))
+    row = pl.BlockSpec((1, 1, span), lambda e: (e, 0, 0))
+    grads = jax.ShapeDtypeStruct(w_gate.shape, BF16)
+    rows = jax.ShapeDtypeStruct((span, width), BF16)
+    return pl.pallas_call(
+        functools.partial(expert_kernel, capacity),
+        grid=(own_experts,),
+        in_specs=[row, pl.BlockSpec((1, span, 1), lambda e: (e, 0, 0)), row, whole, whole, column, column, column],
+        out_specs=[whole, whole, column, column, column],
+        out_shape=[rows, rows, grads, grads, grads],
+        scratch_shapes=[pltpu.VMEM((span, width), F32), pltpu.VMEM((span, width), F32)],
+        compiler_params=pltpu.CompilerParams(vmem_limit_bytes=VMEM_LIMIT),
+        name="experts",
+    )(slot[:, None, :], slot[:, :, None], weight[:, None, :], normed, cot, w_gate, w_up, w_down)
+
+
+LANES = 128
+
+
+def lane_ids(rows):
+    return lax.broadcasted_iota(jnp.int32, (rows, LANES), 1)
+
+
+def turn(x, cosine, sine):
+    half = HEAD_SIZE // 2
+    ahead, behind = pltpu.roll(x, LANES - half, axis=1), pltpu.roll(x, half, axis=1)
+    partner = jnp.where(lane_ids(x.shape[0]) % HEAD_SIZE < half, ahead, behind)
+    return x * cosine + partner * sine
+
+
+def spread(block, at, out):
+    low = lane_ids(block.shape[0]) < HEAD_SIZE
+    other = pltpu.roll(block, HEAD_SIZE, axis=1)
+    zero = jnp.zeros_like(block)
+    out[0, 0, at] = jnp.where(low, block, zero).astype(BF16)
+    out[0, 1, at] = jnp.where(low, zero, other).astype(BF16)
+    out[1, 0, at] = jnp.where(low, other, zero).astype(BF16)
+    out[1, 1, at] = jnp.where(low, zero, block).astype(BF16)
+
+
+def attention_setup(seg_row, seg_col, bias):
+    span = bias.shape[0]
+    for b in range(span // LANES):
+        at = pl.ds(b * LANES, LANES)
+        row = b * LANES + lax.broadcasted_iota(jnp.int32, (LANES, span), 0)
+        col = lax.broadcasted_iota(jnp.int32, (LANES, span), 1)
+        ok = (seg_col[at] == seg_row[...]) & (col <= row)
+        bias[at] = jnp.where(ok, 0.0, -1e30)
+
+
+def weight_columns(pack_all, first, cols):
+    return pack_all[:, :, first : first + cols].reshape(-1, cols)
+
+
+def gain_rows(pack_all, first):
+    pick = lax.broadcasted_iota(jnp.int32, (16, LANES), 0) == lax.broadcasted_iota(jnp.int32, (16, LANES), 1)
+    return mm_nt(pick.astype(BF16), weight_columns(pack_all, first, LANES))
+
+
+def attend_steps(qkv, kx, vx, bias, probs, attended):
+    span, blocks = qkv.shape[0], attended.shape[1] // LANES
+    repeat = QUERY_HEADS // KEY_VALUE_HEADS
+    for j in range(blocks):
+        for b in range(span // LANES):
+            at, keys = pl.ds(b * LANES, LANES), (b + 1) * LANES
+            q = qkv[at, j * LANES : (j + 1) * LANES]
+            total = jnp.zeros((LANES, LANES), F32)
+            for half in range(2):
+                h = 2 * j + half
+                kv = h // repeat
+                scores = mm_nt(q, kx[kv, half, :keys]) + bias[at, :keys]
+                peak = jnp.max(scores, axis=1, keepdims=True)
+                exponent = jnp.exp(scores - peak)
+                share = 1.0 / jnp.sum(exponent, axis=1, keepdims=True)
+                low = (exponent * share).astype(BF16)
+                probs[h, at, :keys] = low
+                total += mm(low, vx[kv, half, :keys])
+            attended[at, j * LANES : (j + 1) * LANES] = total.astype(BF16)
+        yield
+
+
+def forward_kernel(
+    members, tokens, cot, route, pack, gate, up, down, seg_row, seg_col, cosine, sine,
+    cot_all, route_all, pack_all, gate_all, up_all, down_all, normed_attn, qkv, kx, vx, probs, attended, residual, normed_all,
+    send, recv, local, tokens_all, bias, acc, from_left, from_right, normed,
+):
+    links = Links(send, recv, local, members)
+    links.greet()
+    rows, width = tokens.shape
+    span = rows * members
+    q_cols = attended.shape[1]
+    qkv_cols = qkv.shape[1]
+
+    def produce(o):
+        acc[o] = mm_nt(attended[o * rows : (o + 1) * rows], weight_columns(pack_all, qkv_cols, q_cols)).astype(BF16)
+
+    def chain():
+        attention_setup(seg_row, seg_col, bias)
+        yield
+        gains = gain_rows(pack_all, qkv_cols + q_cols)
+
+        @pl.loop(0, span // 16)
+        def _(i):
+            here = tokens_all[i // (rows // 16), pl.ds(pl.multiple_of(i % (rows // 16) * 16, 16), 16)].astype(F32)
+            normed_attn[pl.ds(pl.multiple_of(i * 16, 16), 16)] = (here * rms_factor(here) * gains[0:1]).astype(BF16)
+
+        @pl.loop(0, span // LANES)
+        def _(i):
+            at = pl.ds(pl.multiple_of(i * LANES, LANES), LANES)
+            here = mm(normed_attn[at], weight_columns(pack_all, 0, qkv_cols))
+            c, s = cosine[at], sine[at]
+            for j in range(q_cols // LANES):
+                lanes = slice(j * LANES, (j + 1) * LANES)
+                qkv[at, lanes] = (turn(here[:, lanes], c, s).astype(BF16).astype(F32) * score_scale).astype(BF16)
+            key = turn(here[:, q_cols : q_cols + LANES], c, s)
+            value = here[:, q_cols + LANES :]
+            qkv[at, q_cols : q_cols + LANES] = key.astype(BF16)
+            qkv[at, q_cols + LANES :] = value.astype(BF16)
+            spread(key, at, kx)
+            spread(value, at, vx)
+
+        yield
+        yield from attend_steps(qkv, kx, vx, bias, probs, attended)
+        yield from line_scatter(links, produce, acc, from_left, from_right)
+
+        @pl.loop(0, rows // 16)
+        def _(i):
+            at = pl.ds(pl.multiple_of(i * 16, 16), 16)
+            here = tokens[at].astype(F32) + branch_scale * line_result(links.z, acc, from_left, from_right, at)
+            residual[at] = here
+            normed[at] = (here * rms_factor(here) * gains[1:2]).astype(BF16)
+
+        yield from line_gather(links, normed, normed_all)
+
+    run(
+        FORWARD_ORDER,
+        t=line_gather(links, tokens, tokens_all),
+        r=line_gather(links, route, route_all),
+        c=line_gather(links, cot, cot_all),
+        p=plane_gather(links, pack, pack_all),
+        g=plane_gather(links, gate, gate_all),
+        u=plane_gather(links, up, up_all),
+        d=plane_gather(links, down, down_all),
+        a=chain(),
+    )
+    links.finish()
+
+
+FORWARD_ORDER = "trpgatrputrpppdtrcaggacguaucaudcauaddacadada"
+
+
+def forward_phase(members, tokens, cot, route, pack, gate, up, down, seg_row, seg_col, cosine, sine, q_cols, qkv_cols):
+    rows, width = tokens.shape
+    span = rows * members
+    blocks = pltpu.VMEM((members, rows, width), BF16)
+    heads = q_cols // HEAD_SIZE
+    return comm_call(
+        forward_kernel, "forward", 1, members, 100, 16,
+        [VMEM, ANY, ANY, ANY, ANY, ANY, ANY, VMEM, VMEM, VMEM, VMEM],
+        [ANY, ANY, VMEM, ANY, ANY, ANY, VMEM, VMEM, VMEM, VMEM, VMEM, VMEM, VMEM, ANY],
+        [
+            sds((members, rows, width), BF16),
+            sds((members, *route.shape), F32),
+            sds((8, *pack.shape), BF16),
+            sds((8, *gate.shape), BF16),
+            sds((8, *up.shape), BF16),
+            sds((8, *down.shape), BF16),
+            sds((span, width), BF16),
+            sds((span, qkv_cols), BF16),
+            sds((2, 2, span, LANES), BF16),
+            sds((2, 2, span, LANES), BF16),
+            sds((heads, span, span), BF16),
+            sds((span, q_cols), BF16),
+            sds((rows, width), F32),
+            sds((members, rows, width), BF16),
+        ],
+        [
+            blocks,
+            pltpu.VMEM((span, span), F32),
+            blocks,
+            blocks,
+            blocks,
+            pltpu.VMEM((rows, width), BF16),
+        ],
+    )(tokens, cot, route, pack, gate, up, down, seg_row, seg_col, cosine, sine)
+
+
 def all_blocks(x, axis):
     return lax.all_gather(x, axis, axis=0)
 
@@ -588,7 +780,7 @@
     return grad_q, grad_k, grad_v
 
 
-def shards(
+def shards_plain(
     tokens,
     cotangent,
     gain_attn,
@@ -620,10 +812,10 @@
         return lax.dynamic_slice_in_dim(weight, member * cols, cols, axis=1)
 
     devices = lax.axis_size("dp")
-    phases = (plain_first, plain_second, plain_third, plain_fourth)
-    if devices == 8 and rows % 16 == 0 and width % (32 * devices) == 0:
-        phases = (first_phase, second_phase, third_phase, fourth_phase)
-    phases = [functools.partial(phase, members) for phase in phases]
+    phases = [
+        functools.partial(phase, members)
+        for phase in (plain_first, plain_second, plain_third, plain_fourth)
+    ]
 
     pack = jnp.concatenate(
         [
@@ -686,44 +878,15 @@
     weight = jnp.sum(jnp.where(named, gates_all[None], 0.0), axis=2)
     upto = (place[:, None] <= place[None, :]).astype(BF16)
     slot = dot(chosen.astype(BF16), upto).astype(jnp.int32) - 1
-    slots = jnp.arange(capacity, dtype=jnp.int32)
-    picks = chosen[:, None, :] & (slot[:, None, :] == slots[None, :, None])
-    pick = picks.astype(BF16)
-    slot_weight = jnp.sum(jnp.where(picks, weight[:, None, :], 0.0), axis=2)
-    mixture = jnp.zeros((span, width), F32)
-    grad_normed = jnp.zeros((span, width), F32)
-    expert_grads = []
-    for e in range(own_experts):
-        cols = slice(e * ff, (e + 1) * ff)
-        w_gate, w_up, w_down = gate_all[:, cols], up_all[:, cols], down_all[:, cols]
-        here = pick[e]
-        gate_col = slot_weight[e][:, None]
-        received = dot(here, normed_all).astype(BF16)
-        pre_gate, pre_up = dot(received, w_gate), dot(received, w_up)
-        sig = jax.nn.sigmoid(pre_gate)
-        silu = pre_gate * sig
-        activ = (silu * pre_up).astype(BF16)
-        produced = (gate_col * dot_nt(activ, w_down)).astype(BF16)
-        mixture = mixture + dot_tn(here, produced)
-        grad_out = (gate_col * (branch_scale * dot(here, cot_all))).astype(BF16)
-        grad_activ = dot(grad_out, w_down)
-        grad_gate = (grad_activ * pre_up * sig * (1.0 + pre_gate * (1.0 - sig))).astype(BF16)
-        grad_up = (grad_activ * silu).astype(BF16)
-        grad_pair = (dot_nt(grad_gate, w_gate) + dot_nt(grad_up, w_up)).astype(BF16)
-        grad_normed = grad_normed + dot_tn(here, grad_pair)
-        expert_grads.append(
-            (dot_tn(received, grad_gate), dot_tn(received, grad_up), dot_tn(grad_out, activ))
-        )
+    slot = jnp.where(chosen & (slot < capacity), slot, -1)
+    mixture, grad_normed, *by_kind = experts(
+        slot, weight, normed_all, cot_all, gate_all, up_all, down_all, ff, capacity
+    )
     output = (residual + branch_scale * scatter(mixture, "expert")).astype(BF16)
-    by_kind = [
-        jnp.concatenate([one[i].astype(BF16) for one in expert_grads], axis=1).reshape(
-            devices, -1, own_experts * ff
-        )
-        for i in range(3)
-    ]
+    by_kind = [one.reshape(devices, -1, own_experts * ff) for one in by_kind]
 
     grad_residual, gain_two_part, grad_attn_out, sum_gate, sum_up = phases[2](
-        grad_normed.astype(BF16).reshape(members, rows, width),
+        grad_normed.reshape(members, rows, width),
         residual,
         cotangent,
         gain_two,
@@ -794,12 +957,177 @@
     )
 
 
+def shards_fast(
+    tokens,
+    cotangent,
+    gain_attn,
+    gain_ffn,
+    w_query,
+    key_weight,
+    value_weight,
+    w_out,
+    expert_gate,
+    expert_up,
+    expert_down,
+    expert_ids,
+    gates,
+    lengths,
+    order,
+):
+    rows, width = tokens.shape
+    members, devices = lax.axis_size("expert"), lax.axis_size("dp")
+    member = lax.axis_index("expert")
+    span = rows * members
+    own_experts, ff = expert_gate.shape[1], expert_gate.shape[2]
+    capacity = rows * TOP // own_experts
+    q_cols = w_query.shape[1] // members
+    kv_cols = key_weight.shape[1] // members
+    qkv_cols = q_cols + 2 * kv_cols
+    kv_heads = kv_cols // HEAD_SIZE
+    repeat = QUERY_HEADS // KEY_VALUE_HEADS
+
+    def mine(weight, cols):
+        return lax.dynamic_slice_in_dim(weight, member * cols, cols, axis=1)
+
+    pack = jnp.concatenate(
+        [
+            mine(w_query, q_cols),
+            mine(key_weight, kv_cols),
+            mine(value_weight, kv_cols),
+            mine(w_out, q_cols),
+            gain_attn[:, None],
+            gain_ffn[:, None],
+            jnp.zeros((gain_attn.shape[0], 126), BF16),
+        ],
+        axis=1,
+    )
+    route = jnp.concatenate([expert_ids.astype(F32), gates], axis=1)
+    segment, position = layout(lengths[0], order[0], span)
+    cosine, sine = rotation(position)
+    place = jnp.arange(span, dtype=jnp.int32)
+    (
+        cot_all, route_all, pack_all, gate_all, up_all, down_all,
+        normed_attn, qkv, kx, vx, probs, attended, residual, normed_all,
+    ) = forward_phase(
+        members, tokens, cotangent, route, pack,
+        expert_gate.reshape(-1, own_experts * ff),
+        expert_up.reshape(-1, own_experts * ff),
+        expert_down.reshape(-1, own_experts * ff),
+        segment[None, :], segment[:, None],
+        jnp.tile(cosine, (1, 4)),
+        jnp.tile(jnp.concatenate([-sine, sine], axis=1), (1, 2)),
+        q_cols, qkv_cols,
+    )
+    cot_all = cot_all.reshape(span, width)
+    normed_all = normed_all.reshape(span, width)
+    route_all = route_all.reshape(span, 2 * TOP)
+    ids_all, gates_all = route_all[:, :TOP].astype(jnp.int32), route_all[:, TOP:]
+    pack_all = pack_all.reshape(width, -1)
+    gate_all, up_all, down_all = (w.reshape(width, -1) for w in (gate_all, up_all, down_all))
+    w_qkv = pack_all[:, :qkv_cols]
+    wo = pack_all[:, qkv_cols : qkv_cols + q_cols]
+    gain_one = pack_all[:, qkv_cols + q_cols].astype(F32)[None]
+    gain_two = pack_all[:, qkv_cols + q_cols + 1].astype(F32)[None]
+
+    expert_of = member * own_experts + jnp.arange(own_experts, dtype=jnp.int32)
+    named = ids_all[None, :, :] == expert_of[:, None, None]
+    chosen = jnp.any(named, axis=2)
+    weight = jnp.sum(jnp.where(named, gates_all[None], 0.0), axis=2)
+    upto = (place[:, None] <= place[None, :]).astype(BF16)
+    slot = dot(chosen.astype(BF16), upto).astype(jnp.int32) - 1
+    slot = jnp.where(chosen & (slot < capacity), slot, -1)
+    mixture, grad_normed, *by_kind = experts(
+        slot, weight, normed_all, cot_all, gate_all, up_all, down_all, ff, capacity
+    )
+    output = (residual + branch_scale * scatter(mixture, "expert")).astype(BF16)
+    by_kind = [one.reshape(devices, -1, own_experts * ff) for one in by_kind]
+
+    grad_residual, gain_two_part, grad_attn_out, sum_gate, sum_up = third_phase(
+        members,
+        grad_normed.reshape(members, rows, width),
+        residual,
+        cotangent,
+        gain_two,
+        by_kind[0],
+        by_kind[1],
+    )
+    grad_attn_out = grad_attn_out.reshape(span, width)
+    term_out = dot_tn(grad_attn_out, attended)
+    grad_attended = dot(grad_attn_out, wo).astype(BF16)
+    grad_heads = jnp.moveaxis(grad_attended.reshape(span, kv_heads, repeat, HEAD_SIZE), 1, 0)
+    allowed = (segment[:, None] == segment[None, :]) & (place[None, :] <= place[:, None])
+    probs = jnp.where(allowed, probs.astype(F32), 0.0).reshape(kv_heads, repeat, span, span)
+    q_heads = jnp.moveaxis(qkv[:, :q_cols].reshape(span, kv_heads, repeat, HEAD_SIZE), 1, 0) * BF16(64.0)
+    k_heads = jnp.moveaxis(qkv[:, q_cols : q_cols + kv_cols].reshape(span, kv_heads, HEAD_SIZE), 1, 0)
+    v_heads = jnp.moveaxis(qkv[:, q_cols + kv_cols :].reshape(span, kv_heads, HEAD_SIZE), 1, 0)
+    grad_q, grad_k, grad_v = jax.vmap(functools.partial(attend_backward, allowed=allowed))(
+        q_heads, k_heads, v_heads, probs, grad_heads
+    )
+    grad_qk = jnp.concatenate(
+        [
+            jnp.moveaxis(grad_q, 0, 1).reshape(span, q_cols),
+            jnp.moveaxis(grad_k, 0, 1).reshape(span, kv_cols),
+        ],
+        axis=1,
+    )
+    grad_qkv = jnp.concatenate(
+        [
+            rotate(grad_qk, cosine, sine, back=True).astype(BF16),
+            jnp.moveaxis(grad_v, 0, 1).reshape(span, kv_cols).astype(BF16),
+        ],
+        axis=1,
+    )
+    grad_norm_part = dot_nt(grad_qkv, w_qkv)
+    gain_one_part = jnp.sum(grad_norm_part * normed_attn.astype(F32), axis=0) / gain_one[0]
+    term_qkv = dot_tn(normed_attn, grad_qkv)
+    packed_grads = jnp.concatenate(
+        [
+            term_qkv,
+            term_out,
+            gain_one_part[:, None],
+            gain_two_part.reshape(-1, 1),
+            jnp.zeros((width, 126), F32),
+        ],
+        axis=1,
+    )
+    grad_tokens, per_member, sum_down = fourth_phase(
+        members,
+        grad_norm_part.astype(BF16).reshape(members, rows, width),
+        grad_residual,
+        tokens,
+        gain_one,
+        packed_grads.astype(BF16).reshape(devices, -1, packed_grads.shape[1]),
+        by_kind[2],
+    )
+    per_member = per_member.astype(F32)
+
+    def columns(first, cols):
+        part = per_member[:, :, first : first + cols]
+        return jnp.moveaxis(part, 0, 1).reshape(part.shape[1], -1)
+
+    gains = jnp.sum(per_member[:, :, qkv_cols + q_cols :], axis=0)
+    return (
+        output,
+        grad_tokens,
+        gains[:, 0],
+        gains[:, 1],
+        columns(0, q_cols),
+        columns(q_cols, kv_cols),
+        columns(q_cols + kv_cols, kv_cols),
+        columns(qkv_cols, q_cols),
+        sum_gate.reshape(-1, own_experts, ff),
+        sum_up.reshape(-1, own_experts, ff),
+        sum_down.reshape(-1, own_experts, ff),
+    )
+
+
 def solution(mesh):
     both = P(("dp", "expert"), None)
     row, rows = P("dp"), P("dp", None)
     experts = P("dp", "expert", None)
+    fast = mesh.shape["dp"] == 8 and mesh.shape["expert"] == 4
     return jax.shard_map(
-        shards,
+        shards_fast if fast else shards_plain,
         mesh=mesh,
         in_specs=(both, both, row, row, rows, rows, rows, rows)
         + (experts, experts, experts, both, both, rows, rows),

time: 770 us -> 617 us (0.80)
  matrix products: 205 us -> 30.7 us
  Pallas kernels: 432 us -> 473 us
  local copies, waits for them, and re-layouts: 82.1 us -> 66.3 us
    dot_general x27 -> x2, matrix products: 98 us -> 5.43 us  [dot_tn(): return jnp.einsum('td,tc->dc', a, b, preferred_element_type=F32)]
    dot_general x28 -> x2, matrix products: 55.1 us -> 3.21 us  [dot(): return jnp.dot(a, b, preferred_element_type=F32)]
    pallas_call x2, Pallas kernels: 189 us -> 230 us  [the longest x1 189 us: forward_phase(): comm_call(forward_kernel, 'forward', 1, members, 100, 16, [VMEM, ANY, ANY...]
    concatenate x8 -> x5, local copies, waits for them, and re-layouts: 41.4 us -> 9.12 us  [the longest x3 7.49 us: shards_fast(): jnp.concatenate([term_qkv, term_out, gain_one_part[:, None], gain_two_par...]
    dot_general x7 -> x1, matrix products: 23.9 us -> 3.02 us  [dot_nt(): return jnp.einsum('tc,dc->td', a, b, preferred_element_type=F32)]
    reshape x3 -> x4, local copies, waits for them, and re-layouts: 4.05 us -> 15.4 us  [the longest x1 11.3 us: shards_fast(): jnp.where(allowed, probs.astype(F32), 0.0)]
  transfers between devices with their start and end apart: 1 -> 1, of which waited for: 0 -> 0; matrix products, arithmetic and copies ran while one was open for 25% -> 16% of each run, Pallas kernels for 32% -> 40%
where the time goes in v3:
time: 617 us; the launch traced here: 609 us
  Pallas kernels  473 us (77%)
  local copies, waits for them, and re-layouts  66.3 us (11%)
  matrix products  30.7 us (5%)
  other arithmetic  24.5 us (4%)
  between operations  14.9 us (2%)
    pallas_call x1, Pallas kernels, forward_phase(): comm_call(forward_kernel, 'forward', 1, members, 100, 16, [VMEM, ANY, ANY...  189 us
    pallas_call x1, Pallas kernels, third_phase(): comm_call(third_kernel, 'phase_three', 3, members, 60, 16, [ANY, VMEM, VM...  132 us
    pallas_call x1, Pallas kernels, fourth_phase(): comm_call(fourth_kernel, 'phase_four', 4, members, 60, 16, [ANY, VMEM, VM...  111 us
    pallas_call x1, Pallas kernels, experts(): pl.pallas_call(functools.partial(expert_kernel, capacity), grid=(own_expe...  41 us
    unnamed x49, local copies, waits for them, and re-layouts  12.6 us
  transfers between devices with their start and end apart: 1, of which 0 were waited for; matrix products, arithmetic and copies ran while one was open for 16% of the time, Pallas kernels for 40%

profile of v3, /device:TPU:0, one launch (start us, length us, event | category | flops | bytes accessed | tf_op | source)
XLA Modules:
  0.0 609.0 jit_solution(1760937051854997432)
XLA Ops:
  7.3 0.9 select_reduce_fusion.2
  8.4 0.9 broadcast_in_dim.126.seg_col
  11.8 0.9 copy.165.sine
  12.7 0.9 copy.164.cosine
  14.2 1.4 copy.160.gate
  16.2 1.4 copy.161.up
  18.1 1.4 copy.162.down
  20.2 1.0 constant_dynamic-slice_fusion
  21.2 0.8 constant_dynamic-slice_fusion.1
  22.1 0.9 concatenate.27.pack
  23.0 189.1 %forward.1 = (bf16[4,160,1536]{2,1,0:T(8,128)(2,1)}, f32[4,160,16]{2,1,0:T(8,128)}, bf16[8,192,1152]{2,1,0:T(8,128)(2,1)}, bf16[8,192,2560]{2,1,0:T(8,128)(2,1)}...) custom-call(bf16[160,1536]{1,0:T(8,128)(2,1)} %tokens.3, ...), custom_call_target="tpu_custom_call" | custom-call | tf_op jit(solution)/shard_map/forward/pallas_call | solution.py:689
  212.0 1.2 fusion.26
  215.2 1.7 copy.168.slot_col
  216.9 41.0 %experts.1 = (bf16[640,1536]{1,0:T(8,128)(2,1)}, bf16[640,1536]{1,0:T(8,128)(2,1)}, bf16[1536,2560]{1,0:T(8,128)(2,1)}, bf16[1536,2560]{1,0:T(8,128)(2,1)}, bf16[1536,2560]{1,0:T(8,128)(2,1)}) custom-call(s32[5,1,640]{2,1,0:T(1,128)} %broadcast_in_dim.116.slot_row, s32[5,640,1]{2,1,0:T(8,128)} %copy.168.slot_col, f32[5,1,640]{2,1,0:T(1,128)} %broadcast_in_dim.120.weight_row, ...), custom_call_target="tpu_custom_call" | custom-call | tf_op jit(solution)/shard_map/experts/pallas_call | solution.py:537
  258.2 0.8 copy-done.5
  259.8 2.1 fusion.24
  262.7 131.9 %phase_three.1 = (f32[160,1536]{1,0:T(8,128)}, f32[1,1536]{1,0:T(1,128)}, bf16[4,160,1536]{2,1,0:T(8,128)(2,1)}, f32[192,2560]{1,0:T(8,128)}, f32[192,2560]{1,0:T(8,128)}) custom-call(bf16[4,160,1536]{2,1,0:T(8,128)(2,1)} %bitcast.144, f32[160,1536]{1,0:T(8,128)} %get-tuple-element.36.residual, bf16[160,1536]{1,0:T(8,128)(2,1)} %cot.3, ...), custom_call_target="tpu_custom_call" | custom-call | tf_op jit(solution)/shard_map/phase_three/pallas_call | solution.py:414
  394.6 2.8 copy.178
  397.4 3.0 convolution_convert_fusion.2
  400.4 6.8 %convert_select_fusion = f32[6,640,640]{2,1,0:T(8,128)} fusion(bf16[6,640,640]{2,1,0:T(8,128)(2,1)} %get-tuple-element.45, pred[640,640]{1,0:T(8,128)(4,1)S(1)} %fusion.7), kind=kLoop, calls=%fused_computation.5 | loop fusion | flops 4915200 | bytes 15155200 | tf_op jit(solution)/shard_map/jit(_where)/select_n | solution.py:1059
  407.3 11.3 %copy.173 = f32[2,3,640,640]{2,3,1,0:T(8,128)} copy(f32[2,3,640,640]{3,2,1,0:T(8,128)} %bitcast.118) | data formatting | bytes 19660800 | tf_op jit(solution)/shard_map/reshape | solution.py:1059
  418.6 0.8 copy.170
  419.4 0.8 copy.169
  420.5 1.2 copy.199
  421.7 9.0 %fusion = (f32[2,3,640]{2,1,0:T(4,128)S(1)}, f32[2,640,640,3]{2,1,3,0:T(8,128)}) fusion(f32[2,3,640,640]{2,3,1,0:T(8,128)} %copy.173, bf16[2,640,64,1]{1,2,3,0:T(8,128)(2,1)} %bitcast.151, bf16[2,640,3,64]{1,3,2,0:T(8,128)(2,1)S(1)} %bitcast.140), kind=kOutput, calls=%fused_computation.2 | convolution fusion | flops 319484160 | bytes 20331520 | tf_op jit(solution)/shard_map/vmap(irh,jh->rij)/dot_general | solution.py:774
  430.7 10.0 %fusion.2 = bf16[2,3,640,640]{2,3,1,0:T(8,128)(2,1)} fusion(f32[2,3,640,640]{2,3,1,0:T(8,128)} %copy.173, f32[2,640,640,3]{2,1,3,0:T(8,128)} %get-tuple-element.141, f32[2,3,640]{2,1,0:T(4,128)S(1)} %get-tuple-element.140), kind=kLoop, calls=%fused_computation.4 | loop fusion | flops 7372800 | bytes 24591360 | tf_op jit(solution)/shard_map/vmap()/convert_element_type | solution.py:776
  440.7 3.5 convolution_multiply_fusion
  444.5 1.6 fusion.12
  446.3 0.8 copy-done.7
  447.3 4.9 fusion.14
  452.7 3.0 multiply_reduce_fusion
  457.8 3.5 convolution_convert_fusion.1
  461.3 2.0 convolution_convert_fusion
  463.3 6.1 concatenate.34.pack
  469.4 110.6 %phase_four.1 = (f32[160,1536]{1,0:T(8,128)}, bf16[4,192,1152]{2,1,0:T(8,128)(2,1)}, f32[192,2560]{1,0:T(8,128)}) custom-call(bf16[4,160,1536]{2,1,0:T(8,128)(2,1)} %bitcast.137, f32[160,1536]{1,0:T(8,128)} %get-tuple-element.51.grad_residual, bf16[160,1536]{1,0:T(8,128)(2,1)} %tokens.3, f32[1,1536]{1,0:T(1,128)} %get-tuple-element.136.gain, ...), custom_call_target="tpu_custom_call" | custom-call | tf_op jit(solution)/shard_map/phase_four/pallas_call | solution.py:462
  580.1 1.7 convert_element_type.114
  581.9 1.2 copy.200
  583.1 1.2 copy.203
  584.3 0.8 copy.206
  585.1 0.8 copy.207
  585.9 2.0 copy.187
  587.9 1.9 copy.190
  589.9 2.0 copy.185
  591.9 1.9 copy.188
  593.8 2.0 copy.186
  595.9 1.9 copy.189
  598.6 2.2 add_convert_fusion
  600.8 0.9 copy.209
  (83 shorter events, 13.7 us)
Async XLA Ops:
  7.2 6.4 %copy-start.1 = (bf16[192,5,512]{2,0,1:T(8,128)(2,1)S(1)}, bf16[192,5,512]{2,0,1:T(8,128)(2,1)}, u32[]{:S(2)}) copy-start(bf16[192,5,512]{2,0,1:T(8,128)(2,1)} %param.23) | copy-start | bytes 2949124
  7.2 591.4 %reduce-scatter.2.cloned.1.call-start = ((), (), s32[]{:S(2)}) async-start(), calls=%async_computation.1 | async-start | bytes 2457600 | tf_op jit(solution)/shard_map/reduce_scatter | solution.py:85
  11.7 1.0 copy-start.6
  13.6 1.9 copy-start.2
  15.6 1.9 copy-start.3
  17.5 1.9 copy-start.14
  17.5 2.0 copy-start.15
  257.9 1.1 copy-start.5
  407.3 11.3 %copy-start.10 = (bf16[640,128]{1,0:T(8,128)(2,1)S(1)}, bf16[640,128]{1,0:T(8,128)(2,1)}, u32[]{:S(2)}) copy-start(bf16[640,128]{1,0:T(8,128)(2,1)} %get-tuple-element.132) | copy-start | bytes 491524
  407.3 12.2 %copy-start.9 = (bf16[640,128]{1,0:T(8,128)(2,1)S(1)}, bf16[640,128]{1,0:T(8,128)(2,1)}, u32[]{:S(2)}) copy-start(bf16[640,128]{1,0:T(8,128)(2,1)} %get-tuple-element.131) | copy-start | bytes 491524
  430.7 10.0 %copy-start.8 = (bf16[640,128]{0,1:T(8,128)(2,1)S(1)}, bf16[640,128]{0,1:T(8,128)(2,1)}, u32[]{:S(2)}) copy-start(bf16[640,128]{0,1:T(8,128)(2,1)} %copy.169) | copy-start | bytes 491524
  440.7 3.9 copy-start
  446.2 0.9 copy-start.7
  447.3 5.0 copy-start.11
  447.3 5.4 copy-start.17
  452.3 3.5 copy-start.12
  452.7 4.3 copy-start.16
  457.8 3.5 copy-start.13
  457.8 3.5 copy-start.18
  597.8 3.0 copy-start.4
Sparse Core Ops, SparseCore 0:
  258.0 70.9 reduce-scatter.1

commit v4 on v3

--- a/solution.py
+++ b/solution.py
@@ -19,7 +19,7 @@
 F32 = jnp.float32
 BF16 = jnp.bfloat16
 MESH = pl.DeviceIdType.MESH
-VMEM_LIMIT = 58 * 2**20
+VMEM_LIMIT = 60 * 2**20
 
 
 def layout(lengths_row, order_row, span):
@@ -291,30 +291,34 @@
     first, second = pl.ds(0, half), pl.ds(half, half)
     chips = (links.d, links.x, links.y, links.diag)
     from_sib, load = {}, {}
+    held = [part.at[chip] if mine is None else mine.at[k] for k, chip in enumerate(chips)]
     for k in (3, 1, 2, 0):
         from_sib[k] = links.push(part.at[links.other(chips[k])], theirs.at[k], links.sib)
-        load[k] = links.move(part.at[chips[k]], mine.at[k])
+        if mine is not None:
+            load[k] = links.move(part.at[chips[k]], held[k])
     yield
     for k in (3, 1, 2):
-        load[k].wait()
+        if load:
+            load[k].wait()
         from_sib[k].wait_recv()
-        add_rows(mine.at[k], theirs.at[k])
+        add_rows(held[k], theirs.at[k])
         if k == 3:
-            to_mid_x = links.push(mine.at[3, first], mid_x, links.x)
-            to_mid_y = links.push(mine.at[3, second], mid_y, links.y)
+            to_mid_x = links.push(held[3].at[first], mid_x, links.x)
+            to_mid_y = links.push(held[3].at[second], mid_y, links.y)
         if k == 1:
-            to_end_x = links.push(mine.at[1, first], end_x.at[first], links.x)
+            to_end_x = links.push(held[1].at[first], end_x.at[first], links.x)
         if k == 2:
-            to_end_y = links.push(mine.at[2, second], end_y.at[second], links.y)
+            to_end_y = links.push(held[2].at[second], end_y.at[second], links.y)
     yield
     to_mid_y.wait_recv()
-    add_rows(mine.at[1, second], mid_y)
-    rest_x = links.push(mine.at[1, second], end_x.at[second], links.x)
+    add_rows(held[1].at[second], mid_y)
+    rest_x = links.push(held[1].at[second], end_x.at[second], links.x)
     to_mid_x.wait_recv()
-    add_rows(mine.at[2, first], mid_x)
-    rest_y = links.push(mine.at[2, first], end_y.at[first], links.y)
+    add_rows(held[2].at[first], mid_x)
+    rest_y = links.push(held[2].at[first], end_y.at[first], links.y)
     yield
-    load[0].wait()
+    if load:
+        load[0].wait()
     from_sib[0].wait_recv()
     to_end_x.wait_recv()
     to_end_y.wait_recv()
@@ -322,9 +326,8 @@
     rest_y.wait_recv()
 
 
-def plane_scratch(rows, cols):
-    return [
-        pltpu.VMEM((4, rows, cols), BF16),
+def plane_scratch(rows, cols, mine=True):
+    return [pltpu.VMEM((4, rows, cols), BF16)] * mine + [
         pltpu.VMEM((4, rows, cols), BF16),
         pltpu.VMEM((rows // 2, cols), BF16),
         pltpu.VMEM((rows // 2, cols), BF16),
@@ -337,7 +340,7 @@
     @pl.loop(0, out.shape[0] // step)
     def _(i):
         at = pl.ds(pl.multiple_of(i * step, step), step)
-        own = mine[0, at].astype(F32) + theirs[0, at].astype(F32)
+        own = mine[at].astype(F32) + theirs[0, at].astype(F32)
         out[at] = (own + end_x[at].astype(F32) + end_y[at].astype(F32)).astype(out.dtype)
 
 
@@ -403,8 +406,8 @@
         g=plane_scatter(links, gate, *for_gate),
         u=plane_scatter(links, up, *for_up),
     )
-    plane_result(for_gate[0], for_gate[1], for_gate[4], for_gate[5], gate_out)
-    plane_result(for_up[0], for_up[1], for_up[4], for_up[5], up_out)
+    plane_result(for_gate[0].at[0], for_gate[1], for_gate[4], for_gate[5], gate_out)
+    plane_result(for_up[0].at[0], for_up[1], for_up[4], for_up[5], up_out)
     links.finish()
 
 
@@ -425,52 +428,6 @@
         + plane_scratch(*gate.shape[1:])
         + plane_scratch(*up.shape[1:]),
     )(part, residual, cot, gain, gate, up)
-
-
-def fourth_kernel(members, part, grad_residual, tokens, gain, pack, down, grad_tokens, pack_all, down_out, send, recv, local, acc, from_left, from_right, pack_own, *rest):
-    links = Links(send, recv, local, members)
-    links.greet()
-    for_pack, for_down = rest[:6], rest[6:]
-
-    def pack_chain():
-        yield from plane_scatter(links, pack, *for_pack)
-        plane_result(for_pack[0], for_pack[1], for_pack[4], for_pack[5], pack_own)
-        yield from line_gather(links, pack_own, pack_all)
-
-    links.move(part, acc).wait()
-    run(
-        "zpdpdzppppzdpppd",
-        p=pack_chain(),
-        z=line_scatter(links, lambda o: None, acc, from_left, from_right),
-        d=plane_scatter(links, down, *for_down),
-    )
-
-    @pl.loop(0, tokens.shape[0] // 16)
-    def _(i):
-        at = pl.ds(pl.multiple_of(i * 16, 16), 16)
-        grad = line_result(links.z, acc, from_left, from_right, at)
-        here = tokens[at].astype(F32)
-        grad_tokens[at] = grad_residual[at] + norm_back(here, rms_factor(here), gain[...], grad)
-
-    plane_result(for_down[0], for_down[1], for_down[4], for_down[5], down_out)
-    links.finish()
-
-
-def fourth_phase(members, part, grad_residual, tokens, gain, pack, down):
-    rows, width = tokens.shape
-    blocks = pltpu.VMEM((members, rows, width), BF16)
-    return comm_call(
-        fourth_kernel, "phase_four", 4, members, 60, 16,
-        [ANY, VMEM, VMEM, VMEM, ANY, ANY], [VMEM, ANY, VMEM],
-        [
-            sds((rows, width), F32),
-            sds((members, *pack.shape[1:]), BF16),
-            sds(down.shape[1:], F32),
-        ],
-        [blocks, blocks, blocks, pltpu.VMEM(pack.shape[1:], BF16)]
-        + plane_scratch(*pack.shape[1:])
-        + plane_scratch(*down.shape[1:]),
-    )(part, grad_residual, tokens, gain, pack, down)
 
 
 def dims(a, b):
@@ -717,6 +674,181 @@
     )(tokens, cot, route, pack, gate, up, down, seg_row, seg_col, cosine, sine)
 
 
+def attend_back_steps(qkv, kx, vx, probs, grad_attended, cosine, sine, grad_k, grad_v, grad_qkv):
+    span = qkv.shape[0]
+    blocks = grad_attended.shape[1] // LANES
+    repeat = QUERY_HEADS // KEY_VALUE_HEADS
+    grad_k[...] = jnp.zeros(grad_k.shape, F32)
+    grad_v[...] = jnp.zeros(grad_v.shape, F32)
+    for j in range(blocks):
+        lanes = slice(j * LANES, (j + 1) * LANES)
+        for b in range(span // LANES):
+            at, keys = pl.ds(b * LANES, LANES), (b + 1) * LANES
+            q, grad = qkv[at, lanes], grad_attended[at, lanes]
+            total = jnp.zeros((LANES, LANES), F32)
+            for half in range(2):
+                h = 2 * j + half
+                kv = h // repeat
+                low = probs[h, at, :keys]
+                share = low.astype(F32)
+                grad_probs = mm_nt(grad, vx[kv, half, :keys])
+                inner = jnp.sum(share * grad_probs, axis=1, keepdims=True)
+                grad_scores = (share * (grad_probs - inner)).astype(BF16)
+                total += mm(grad_scores, kx[kv, half, :keys])
+                grad_k[kv, half, :keys] += mm_tn(grad_scores, q)
+                grad_v[kv, half, :keys] += mm_tn(low, grad)
+            grad_qkv[at, lanes] = turn(total * score_scale, cosine[at], -sine[at]).astype(BF16)
+        yield
+    first = blocks * LANES
+
+    def fold(parts, at):
+        low = lane_ids(LANES) < HEAD_SIZE
+        same = jnp.where(low, parts[0, 0, at], parts[1, 1, at])
+        crossed = jnp.where(low, parts[1, 0, at], parts[0, 1, at])
+        return same + pltpu.roll(crossed, HEAD_SIZE, axis=1)
+
+    for b in range(span // LANES):
+        at = pl.ds(b * LANES, LANES)
+        grad_qkv[at, first : first + LANES] = turn(fold(grad_k, at), cosine[at], -sine[at]).astype(BF16)
+        grad_qkv[at, first + LANES :] = fold(grad_v, at).astype(BF16)
+
+
+def backward_kernel(
+    members, mixture, residual, grad_out_all, grad_residual, gain_ffn_part, tokens, down, pack_all, normed_attn, qkv, kx, vx, probs, attended, cosine, sine,
+    output, grad_tokens, gains, d_query, d_key, d_value, d_out, d_down,
+    send, recv, local, acc_m, left_m, right_m, acc, from_left, from_right, grad_attended, grad_k, grad_v, grad_qkv, gain_part,
+    for_w_out, for_w_qkv, own_out, own_qkv, all_out, all_qkv, *rest,
+):
+    links = Links(send, recv, local, members)
+    links.greet()
+    rows, width = tokens.shape
+    q_cols, qkv_cols = attended.shape[1], qkv.shape[1]
+    kv_cols = (qkv_cols - q_cols) // 2
+    with_out, with_qkv, with_down = rest[:5], rest[5:10], rest[10:]
+    pairs = for_w_out.shape[0] // 2
+    step = width // pairs
+    row_gains = gain_rows(pack_all, qkv_cols + q_cols)
+
+    def out_chain():
+        for i in range(pairs):
+            term = mm_tn(grad_out_all[:, i * step : (i + 1) * step], attended[...])
+            for_w_out[2 * i : 2 * i + 2] = term.astype(BF16).reshape(2, step // 2, q_cols)
+        yield from plane_scatter(links, for_w_out, None, *with_out)
+        plane_result(for_w_out.at[links.d], with_out[0], with_out[3], with_out[4], own_out)
+        yield from line_gather(links, own_out, all_out)
+
+    def produce(o):
+        at = slice(o * rows, (o + 1) * rows)
+        part = mm_nt(grad_qkv[at], weight_columns(pack_all, 0, qkv_cols))
+        gain_part[...] += jnp.sum(part * normed_attn[at].astype(F32), axis=0, keepdims=True)
+        acc[o] = part.astype(BF16)
+
+    def chain():
+        wo = weight_columns(pack_all, qkv_cols, q_cols)
+
+        @pl.loop(0, grad_attended.shape[0] // LANES)
+        def _(i):
+            at = pl.ds(pl.multiple_of(i * LANES, LANES), LANES)
+            grad_attended[at] = mm(grad_out_all[at], wo).astype(BF16)
+
+        yield
+        yield from attend_back_steps(qkv, kx, vx, probs, grad_attended, cosine, sine, grad_k, grad_v, grad_qkv)
+        gain_part[...] = jnp.zeros(gain_part.shape, F32)
+        yield from line_scatter(links, produce, acc, from_left, from_right)
+
+        @pl.loop(0, rows // 16)
+        def _(i):
+            at = pl.ds(pl.multiple_of(i * 16, 16), 16)
+            grad = line_result(links.z, acc, from_left, from_right, at)
+            here = tokens[at].astype(F32)
+            grad_tokens[at] = grad_residual[at] + norm_back(here, rms_factor(here), row_gains[0:1], grad)
+
+    def qkv_chain():
+        for i in range(pairs):
+            term = mm_tn(normed_attn[:, i * step : (i + 1) * step], grad_qkv[...])
+            for_w_qkv[2 * i : 2 * i + 2, :, :qkv_cols] = term.astype(BF16).reshape(2, step // 2, qkv_cols)
+        which = lax.broadcasted_iota(jnp.int32, (16, width), 0)
+        both = jnp.where(which == 0, gain_part[...] / row_gains[0:1], jnp.where(which == 1, gain_ffn_part[...], 0.0))
+        pick = lax.broadcasted_iota(jnp.int32, (16, LANES), 0) == lax.broadcasted_iota(jnp.int32, (16, LANES), 1)
+        columns = mm_tn(both.astype(BF16), pick.astype(BF16))
+        for_w_qkv[:, :, qkv_cols:] = columns.astype(BF16).reshape(2 * pairs, step // 2, LANES)
+        yield from plane_scatter(links, for_w_qkv, None, *with_qkv)
+        plane_result(for_w_qkv.at[links.d], with_qkv[0], with_qkv[3], with_qkv[4], own_qkv)
+        yield from line_gather(links, own_qkv, all_qkv)
+
+    def mixture_chain():
+        links.move(mixture, acc_m).wait()
+        yield from line_scatter(links, lambda o: None, acc_m, left_m, right_m)
+
+        @pl.loop(0, rows // 16)
+        def _(i):
+            at = pl.ds(pl.multiple_of(i * 16, 16), 16)
+            here = residual[at] + branch_scale * line_result(links.z, acc_m, left_m, right_m, at)
+            output[at] = here.astype(BF16)
+
+    run(
+        BACKWARD_ORDER,
+        m=mixture_chain(),
+        d=plane_scatter(links, down, *with_down),
+        o=out_chain(),
+        a=chain(),
+        q=qkv_chain(),
+    )
+    plane_result(with_down[0].at[0], with_down[1], with_down[4], with_down[5], d_down)
+    for m in range(members):
+        d_out[:, m * q_cols : (m + 1) * q_cols] = all_out[m].astype(F32)
+        d_query[:, m * q_cols : (m + 1) * q_cols] = all_qkv[m, :, :q_cols].astype(F32)
+        d_key[:, m * kv_cols : (m + 1) * kv_cols] = all_qkv[m, :, q_cols : q_cols + kv_cols].astype(F32)
+        d_value[:, m * kv_cols : (m + 1) * kv_cols] = all_qkv[m, :, q_cols + kv_cols : qkv_cols].astype(F32)
+    gains[...] = sum(all_qkv[m, :, qkv_cols:].astype(F32) for m in range(members))
+    links.finish()
+
+
+BACKWARD_ORDER = "mododmaoaomaodmaodaoaqaqaoqaq"
+
+
+def backward_phase(members, mixture, residual, grad_out_all, grad_residual, gain_ffn_part, tokens, down, pack_all, normed_attn, qkv, kx, vx, probs, attended, cosine, sine):
+    rows, width = tokens.shape
+    span, q_cols = attended.shape
+    qkv_cols = qkv.shape[1]
+    kv_cols = (qkv_cols - q_cols) // 2
+    devices, own = down.shape[:2]
+    line = [pltpu.VMEM((members, rows, width), BF16)] * 3
+    return comm_call(
+        backward_kernel, "backward", 4, members, 100, 32,
+        [ANY, VMEM, VMEM, VMEM, VMEM, VMEM, ANY] + [VMEM] * 9,
+        [VMEM] * 8,
+        [
+            sds((rows, width), BF16),
+            sds((rows, width), F32),
+            sds((own, LANES), F32),
+            sds((own, members * q_cols), F32),
+            sds((own, members * kv_cols), F32),
+            sds((own, members * kv_cols), F32),
+            sds((own, members * q_cols), F32),
+            sds(down.shape[1:], F32),
+        ],
+        [
+            *line,
+            *line,
+            pltpu.VMEM((span, q_cols), BF16),
+            pltpu.VMEM((2, 2, span, LANES), F32),
+            pltpu.VMEM((2, 2, span, LANES), F32),
+            pltpu.VMEM((span, qkv_cols), BF16),
+            pltpu.VMEM((1, width), F32),
+            pltpu.VMEM((devices, own, q_cols), BF16),
+            pltpu.VMEM((devices, own, qkv_cols + LANES), BF16),
+            pltpu.VMEM((own, q_cols), BF16),
+            pltpu.VMEM((own, qkv_cols + LANES), BF16),
+            pltpu.VMEM((members, own, q_cols), BF16),
+            pltpu.VMEM((members, own, qkv_cols + LANES), BF16),
+            *plane_scratch(own, q_cols, False),
+            *plane_scratch(own, qkv_cols + LANES, False),
+            *plane_scratch(*down.shape[1:]),
+        ],
+    )(mixture, residual, grad_out_all, grad_residual, gain_ffn_part, tokens, down, pack_all, normed_attn, qkv, kx, vx, probs, attended, cosine, sine)
+
+
 def all_blocks(x, axis):
     return lax.all_gather(x, axis, axis=0)
 
@@ -983,8 +1115,6 @@
     q_cols = w_query.shape[1] // members
     kv_cols = key_weight.shape[1] // members
     qkv_cols = q_cols + 2 * kv_cols
-    kv_heads = kv_cols // HEAD_SIZE
-    repeat = QUERY_HEADS // KEY_VALUE_HEADS
 
     def mine(weight, cols):
         return lax.dynamic_slice_in_dim(weight, member * cols, cols, axis=1)
@@ -1004,6 +1134,8 @@
     route = jnp.concatenate([expert_ids.astype(F32), gates], axis=1)
     segment, position = layout(lengths[0], order[0], span)
     cosine, sine = rotation(position)
+    cosine = jnp.tile(cosine, (1, 4))
+    sine = jnp.tile(jnp.concatenate([-sine, sine], axis=1), (1, 2))
     place = jnp.arange(span, dtype=jnp.int32)
     (
         cot_all, route_all, pack_all, gate_all, up_all, down_all,
@@ -1014,20 +1146,15 @@
         expert_up.reshape(-1, own_experts * ff),
         expert_down.reshape(-1, own_experts * ff),
         segment[None, :], segment[:, None],
-        jnp.tile(cosine, (1, 4)),
-        jnp.tile(jnp.concatenate([-sine, sine], axis=1), (1, 2)),
+        cosine, sine,
         q_cols, qkv_cols,
     )
     cot_all = cot_all.reshape(span, width)
     normed_all = normed_all.reshape(span, width)
     route_all = route_all.reshape(span, 2 * TOP)
     ids_all, gates_all = route_all[:, :TOP].astype(jnp.int32), route_all[:, TOP:]
-    pack_all = pack_all.reshape(width, -1)
     gate_all, up_all, down_all = (w.reshape(width, -1) for w in (gate_all, up_all, down_all))
-    w_qkv = pack_all[:, :qkv_cols]
-    wo = pack_all[:, qkv_cols : qkv_cols + q_cols]
-    gain_one = pack_all[:, qkv_cols + q_cols].astype(F32)[None]
-    gain_two = pack_all[:, qkv_cols + q_cols + 1].astype(F32)[None]
+    gain_two = pack_all[:, :, qkv_cols + q_cols + 1].astype(F32).reshape(1, width)
 
     expert_of = member * own_experts + jnp.arange(own_experts, dtype=jnp.int32)
     named = ids_all[None, :, :] == expert_of[:, None, None]
@@ -1039,7 +1166,6 @@
     mixture, grad_normed, *by_kind = experts(
         slot, weight, normed_all, cot_all, gate_all, up_all, down_all, ff, capacity
     )
-    output = (residual + branch_scale * scatter(mixture, "expert")).astype(BF16)
     by_kind = [one.reshape(devices, -1, own_experts * ff) for one in by_kind]
 
     grad_residual, gain_two_part, grad_attn_out, sum_gate, sum_up = third_phase(
@@ -1051,73 +1177,32 @@
         by_kind[0],
         by_kind[1],
     )
-    grad_attn_out = grad_attn_out.reshape(span, width)
-    term_out = dot_tn(grad_attn_out, attended)
-    grad_attended = dot(grad_attn_out, wo).astype(BF16)
-    grad_heads = jnp.moveaxis(grad_attended.reshape(span, kv_heads, repeat, HEAD_SIZE), 1, 0)
-    allowed = (segment[:, None] == segment[None, :]) & (place[None, :] <= place[:, None])
-    probs = jnp.where(allowed, probs.astype(F32), 0.0).reshape(kv_heads, repeat, span, span)
-    q_heads = jnp.moveaxis(qkv[:, :q_cols].reshape(span, kv_heads, repeat, HEAD_SIZE), 1, 0) * BF16(64.0)
-    k_heads = jnp.moveaxis(qkv[:, q_cols : q_cols + kv_cols].reshape(span, kv_heads, HEAD_SIZE), 1, 0)
-    v_heads = jnp.moveaxis(qkv[:, q_cols + kv_cols :].reshape(span, kv_heads, HEAD_SIZE), 1, 0)
-    grad_q, grad_k, grad_v = jax.vmap(functools.partial(attend_backward, allowed=allowed))(
-        q_heads, k_heads, v_heads, probs, grad_heads
-    )
-    grad_qk = jnp.concatenate(
-        [
-            jnp.moveaxis(grad_q, 0, 1).reshape(span, q_cols),
-            jnp.moveaxis(grad_k, 0, 1).reshape(span, kv_cols),
-        ],
-        axis=1,
-    )
-    grad_qkv = jnp.concatenate(
-        [
-            rotate(grad_qk, cosine, sine, back=True).astype(BF16),
-            jnp.moveaxis(grad_v, 0, 1).reshape(span, kv_cols).astype(BF16),
-        ],
-        axis=1,
-    )
-    grad_norm_part = dot_nt(grad_qkv, w_qkv)
-    gain_one_part = jnp.sum(grad_norm_part * normed_attn.astype(F32), axis=0) / gain_one[0]
-    term_qkv = dot_tn(normed_attn, grad_qkv)
-    packed_grads = jnp.concatenate(
-        [
-            term_qkv,
-            term_out,
-            gain_one_part[:, None],
-            gain_two_part.reshape(-1, 1),
-            jnp.zeros((width, 126), F32),
-        ],
-        axis=1,
-    )
-    grad_tokens, per_member, sum_down = fourth_phase(
+    (
+        output, grad_tokens, gains, d_query, d_key, d_value, d_out, d_down,
+    ) = backward_phase(
         members,
-        grad_norm_part.astype(BF16).reshape(members, rows, width),
+        mixture.reshape(members, rows, width),
+        residual,
+        grad_attn_out.reshape(span, width),
         grad_residual,
+        gain_two_part,
         tokens,
-        gain_one,
-        packed_grads.astype(BF16).reshape(devices, -1, packed_grads.shape[1]),
         by_kind[2],
-    )
-    per_member = per_member.astype(F32)
-
-    def columns(first, cols):
-        part = per_member[:, :, first : first + cols]
-        return jnp.moveaxis(part, 0, 1).reshape(part.shape[1], -1)
-
-    gains = jnp.sum(per_member[:, :, qkv_cols + q_cols :], axis=0)
+        pack_all,
+        normed_attn, qkv, kx, vx, probs, attended, cosine, sine,
+    )
     return (
         output,
         grad_tokens,
         gains[:, 0],
         gains[:, 1],
-        columns(0, q_cols),
-        columns(q_cols, kv_cols),
-        columns(q_cols + kv_cols, kv_cols),
-        columns(qkv_cols, q_cols),
+        d_query,
+        d_key,
+        d_value,
+        d_out,
         sum_gate.reshape(-1, own_experts, ff),
         sum_up.reshape(-1, own_experts, ff),
-        sum_down.reshape(-1, own_experts, ff),
+        d_down.reshape(-1, own_experts, ff),
     )
 
 

time: 617 us -> 544 us (0.88)
  matrix products: 30.7 us -> 0.2 us
  local copies, waits for them, and re-layouts: 66.3 us -> 38.4 us
  other arithmetic: 24.5 us -> 3.08 us
  Pallas kernels: 473 us -> 494 us
  between operations: 14.9 us -> 1.09 us
    pallas_call x1, Pallas kernels: 111 us -> 153 us  [backward_phase(): comm_call(backward_kernel, 'backward', 4, members, 100, 32, [ANY, VMEM, V...]
    dot_general x7 -> x0, matrix products: 27.5 us -> none  [the longest x1 9.02 us: attend_backward(): grad_probs = jnp.einsum('irh,jh->rij', grad, v, preferred_element_type=F32)]
    pallas_call x1, Pallas kernels: 132 us -> 111 us  [third_phase(): comm_call(third_kernel, 'phase_three', 3, members, 60, 16, [ANY, VMEM, VM...]
    reshape x5 -> x0, local copies, waits for them, and re-layouts: 15.2 us -> none  [the longest x1 11.3 us: shards_fast(): jnp.where(allowed, probs.astype(F32), 0.0)]
    convert_element_type x4 -> x1, other arithmetic: 14.5 us -> 1.36 us  [shards_fast(): pack_all[:, :, qkv_cols + q_cols + 1].astype(F32).reshape(1, width)]
    concatenate x3 -> x0, local copies, waits for them, and re-layouts: 7.49 us -> none  [shards_fast(): jnp.concatenate([term_qkv, term_out, gain_one_part[:, None], gain_two_par...]
    select_n x1 -> x0, other arithmetic: 6.85 us -> none  [shards_fast(): jnp.where(allowed, probs.astype(F32), 0.0)]
    unnamed x49 -> x35, local copies, waits for them, and re-layouts: 12.6 us -> 14.2 us
  transfers between devices with their start and end apart: 1 -> 0, of which waited for: 0 -> 0; matrix products, arithmetic and copies ran while one was open for 16% -> 0% of each run, Pallas kernels for 40% -> 0%
where the time goes in v4:
time: 544 us; the launch traced here: 536 us
  Pallas kernels  494 us (91%)
  local copies, waits for them, and re-layouts  38.4 us (7%)
    pallas_call x1, Pallas kernels, forward_phase(): comm_call(forward_kernel, 'forward', 1, members, 100, 16, [VMEM, ANY, ANY...  189 us
    pallas_call x1, Pallas kernels, backward_phase(): comm_call(backward_kernel, 'backward', 4, members, 100, 32, [ANY, VMEM, V...  153 us
    pallas_call x1, Pallas kernels, third_phase(): comm_call(third_kernel, 'phase_three', 3, members, 60, 16, [ANY, VMEM, VM...  111 us
    pallas_call x1, Pallas kernels, experts(): pl.pallas_call(functools.partial(expert_kernel, capacity), grid=(own_expe...  40.9 us
    unnamed x35, local copies, waits for them, and re-layouts  14.2 us

profile of v4, /device:TPU:0, one launch (start us, length us, event | category | flops | bytes accessed | tf_op | source)
XLA Modules:
  0.0 536.4 jit_solution(17188839414495456509)
XLA Ops:
  0.6 1.0 constant_dynamic-slice_fusion
  1.7 0.8 constant_dynamic-slice_fusion.1
  2.5 0.7 broadcast_in_dim.100
  3.3 0.7 broadcast_in_dim.101
  4.0 0.9 concatenate.10.pack
  4.9 0.9 select_reduce_fusion.2
  5.8 0.1 select_reduce_fusion.1
  5.9 0.1 select_reduce_fusion
  6.0 0.4 fusion.4
  6.5 0.9 copy.112.sine
  7.4 0.9 copy.111.cosine
  8.3 0.9 broadcast_in_dim.102.seg_col
  9.2 0.6 broadcast_in_dim.91.seg_row
  9.8 0.6 copy.103
  10.3 1.4 copy.107.gate
  11.7 0.6 copy.104
  12.3 1.4 copy.108.up
  13.7 0.6 copy.105
  14.2 1.4 copy.109.down
  15.6 0.7 copy.106.route
  16.4 189.2 %forward.1 = (bf16[4,160,1536]{2,1,0:T(8,128)(2,1)}, f32[4,160,16]{2,1,0:T(8,128)}, bf16[8,192,1152]{2,1,0:T(8,128)(2,1)}, bf16[8,192,2560]{2,1,0:T(8,128)(2,1)}...) custom-call(bf16[160,1536]{1,0:T(8,128)(2,1)} %tokens.3, ...), custom_call_target="tpu_custom_call" | custom-call | tf_op jit(solution)/shard_map/forward/pallas_call | solution.py:646
  205.5 1.2 fusion.5
  206.8 0.1 copy.124
  206.9 0.1 copy.114
  207.0 0.1 fusion.3
  207.2 0.6 broadcast_in_dim.99.weight_row
  207.8 0.1 compare_reduce_fusion
  207.9 0.2 and_select_fusion
  208.1 1.7 copy.115.slot_col
  209.8 0.6 broadcast_in_dim.95.slot_row
  210.4 40.9 %experts.1 = (bf16[640,1536]{1,0:T(8,128)(2,1)}, bf16[640,1536]{1,0:T(8,128)(2,1)}, bf16[1536,2560]{1,0:T(8,128)(2,1)}, bf16[1536,2560]{1,0:T(8,128)(2,1)}, bf16[1536,2560]{1,0:T(8,128)(2,1)}) custom-call(s32[5,1,640]{2,1,0:T(1,128)} %broadcast_in_dim.95.slot_row, s32[5,640,1]{2,1,0:T(8,128)} %copy.115.slot_col, f32[5,1,640]{2,1,0:T(1,128)} %broadcast_in_dim.99.weight_row, ...), custom_call_target="tpu_custom_call" | custom-call | tf_op jit(solution)/shard_map/experts/pallas_call | solution.py:494
  251.4 1.4 convert_reduce_fusion
  252.7 0.7 reshape.163.gain
  253.4 110.8 %phase_three.1 = (f32[160,1536]{1,0:T(8,128)}, f32[1,1536]{1,0:T(1,128)}, bf16[4,160,1536]{2,1,0:T(8,128)(2,1)}, f32[192,2560]{1,0:T(8,128)}, f32[192,2560]{1,0:T(8,128)}) custom-call(bf16[4,160,1536]{2,1,0:T(8,128)(2,1)} %bitcast.40, f32[160,1536]{1,0:T(8,128)} %get-tuple-element.50.residual, bf16[160,1536]{1,0:T(8,128)(2,1)} %cot.3, ...), custom_call_target="tpu_custom_call" | custom-call | tf_op jit(solution)/shard_map/phase_three/pallas_call | solution.py:417
  364.3 152.6 %backward.1 = (bf16[160,1536]{1,0:T(8,128)(2,1)}, f32[160,1536]{1,0:T(8,128)}, f32[192,128]{1,0:T(8,128)}, f32[192,1536]{1,0:T(8,128)}, f32[192,512]{1,0:T(8,128...) custom-call(bf16[4,160,1536]{2,1,0:T(8,128)(2,1)} %bitcast.38, ...), custom_call_target="tpu_custom_call" | custom-call | tf_op jit(solution)/shard_map/backward/pallas_call | solution.py:817
  516.8 2.0 copy.120
  518.9 1.9 copy.123
  520.8 0.8 slice_reduce_fusion
  521.6 2.0 copy.118
  523.6 1.9 copy.121
  525.6 2.0 copy.119
  527.6 1.9 copy.122
  529.5 0.8 copy.131
  530.3 2.3 copy.132
  532.6 1.0 copy.133
  533.6 0.7 copy.134
  534.4 0.7 copy.135
  535.1 1.0 copy.136
  (32 shorter events, 0.1 us)
Async XLA Ops:
  4.0 5.7 %copy-start.2 = (bf16[192,5,512]{2,0,1:T(8,128)(2,1)S(1)}, bf16[192,5,512]{2,0,1:T(8,128)(2,1)}, u32[]{:S(2)}) copy-start(bf16[192,5,512]{2,0,1:T(8,128)(2,1)} %param.23) | copy-start | bytes 2949124
  9.8 1.9 copy-start.3
  11.7 1.9 copy-start.4
  13.6 1.9 copy-start.9
  13.6 2.0 copy-start.10
  518.9 1.9 copy-start.8
  527.6 1.9 copy-start.5
  529.5 3.0 copy-start.1
  530.3 3.3 copy-start.7
  532.6 1.8 copy-start.6
  532.6 2.5 copy-start

commit v5 on v4

--- a/solution.py
+++ b/solution.py
@@ -401,7 +401,7 @@
         yield from line_gather(links, grad_out, out_all)
 
     run(
-        "zguguzzzguzgu",
+        "uuzzuzgzgzguz",
         z=chain(),
         g=plane_scatter(links, gate, *for_gate),
         u=plane_scatter(links, up, *for_up),
@@ -635,7 +635,7 @@
     links.finish()
 
 
-FORWARD_ORDER = "trpgatrputrpppdtrcaggacguaucaudcauaddacadada"
+FORWARD_ORDER = "tpptdatpppctpatacpadrpgatcaacdparuagrrttcr"
 
 
 def forward_phase(members, tokens, cot, route, pack, gate, up, down, seg_row, seg_col, cosine, sine, q_cols, qkv_cols):
@@ -804,7 +804,7 @@
     links.finish()
 
 
-BACKWARD_ORDER = "mododmaoaomaodmaodaoaqaqaoqaq"
+BACKWARD_ORDER = "amoadmmadaaaoqoqoqaoaq"
 
 
 def backward_phase(members, mixture, residual, grad_out_all, grad_residual, gain_ffn_part, tokens, down, pack_all, normed_attn, qkv, kx, vx, probs, attended, cosine, sine):

time: 544 us -> 433 us (0.80)
  Pallas kernels: 494 us -> 381 us
    pallas_call x1, Pallas kernels: 189 us -> 137 us  [forward_phase(): comm_call(forward_kernel, 'forward', 1, members, 100, 16, [VMEM, ANY, ANY...]
    pallas_call x1, Pallas kernels: 153 us -> 117 us  [backward_phase(): comm_call(backward_kernel, 'backward', 4, members, 100, 32, [ANY, VMEM, V...]
    pallas_call x1, Pallas kernels: 111 us -> 85.8 us  [third_phase(): comm_call(third_kernel, 'phase_three', 3, members, 60, 16, [ANY, VMEM, VM...]
where the time goes in v5:
time: 433 us; the launch traced here: 424 us
  Pallas kernels  381 us (88%)
  local copies, waits for them, and re-layouts  38.4 us (9%)
    pallas_call x1, Pallas kernels, forward_phase(): comm_call(forward_kernel, 'forward', 1, members, 100, 16, [VMEM, ANY, ANY...  137 us
    pallas_call x1, Pallas kernels, backward_phase(): comm_call(backward_kernel, 'backward', 4, members, 100, 32, [ANY, VMEM, V...  117 us
    pallas_call x1, Pallas kernels, third_phase(): comm_call(third_kernel, 'phase_three', 3, members, 60, 16, [ANY, VMEM, VM...  85.8 us
    pallas_call x1, Pallas kernels, experts(): pl.pallas_call(functools.partial(expert_kernel, capacity), grid=(own_expe...  41 us
    unnamed x35, local copies, waits for them, and re-layouts  14.2 us

profile of v5, /device:TPU:0, one launch (start us, length us, event | category | flops | bytes accessed | tf_op | source)
XLA Modules:
  0.0 424.3 jit_solution(15544192366996670796)
XLA Ops:
  0.6 1.0 constant_dynamic-slice_fusion
  1.7 0.8 constant_dynamic-slice_fusion.1
  2.5 0.7 broadcast_in_dim.100
  3.3 0.7 broadcast_in_dim.101
  4.0 0.9 concatenate.10.pack
  4.9 0.9 select_reduce_fusion.2
  5.8 0.1 select_reduce_fusion.1
  5.9 0.1 select_reduce_fusion
  6.0 0.4 fusion.4
  6.5 0.9 copy.112.sine
  7.4 0.9 copy.111.cosine
  8.3 0.9 broadcast_in_dim.102.seg_col
  9.2 0.6 broadcast_in_dim.91.seg_row
  9.8 0.6 copy.103
  10.3 1.4 copy.107.gate
  11.7 0.6 copy.104
  12.3 1.4 copy.108.up
  13.7 0.6 copy.105
  14.2 1.4 copy.109.down
  15.6 0.7 copy.106.route
  16.4 137.2 %forward.1 = (bf16[4,160,1536]{2,1,0:T(8,128)(2,1)}, f32[4,160,16]{2,1,0:T(8,128)}, bf16[8,192,1152]{2,1,0:T(8,128)(2,1)}, bf16[8,192,2560]{2,1,0:T(8,128)(2,1)}...) custom-call(bf16[160,1536]{1,0:T(8,128)(2,1)} %tokens.3, ...), custom_call_target="tpu_custom_call" | custom-call | tf_op jit(solution)/shard_map/forward/pallas_call | solution.py:646
  153.5 1.2 fusion.5
  154.8 0.1 copy.124
  154.9 0.1 copy.114
  155.0 0.1 fusion.3
  155.2 0.6 broadcast_in_dim.99.weight_row
  155.8 0.1 compare_reduce_fusion
  155.9 0.2 and_select_fusion
  156.1 1.7 copy.115.slot_col
  157.8 0.6 broadcast_in_dim.95.slot_row
  158.4 41.0 %experts.1 = (bf16[640,1536]{1,0:T(8,128)(2,1)}, bf16[640,1536]{1,0:T(8,128)(2,1)}, bf16[1536,2560]{1,0:T(8,128)(2,1)}, bf16[1536,2560]{1,0:T(8,128)(2,1)}, bf16[1536,2560]{1,0:T(8,128)(2,1)}) custom-call(s32[5,1,640]{2,1,0:T(1,128)} %broadcast_in_dim.95.slot_row, s32[5,640,1]{2,1,0:T(8,128)} %copy.115.slot_col, f32[5,1,640]{2,1,0:T(1,128)} %broadcast_in_dim.99.weight_row, ...), custom_call_target="tpu_custom_call" | custom-call | tf_op jit(solution)/shard_map/experts/pallas_call | solution.py:494
  199.4 1.4 convert_reduce_fusion
  200.7 0.7 reshape.163.gain
  201.4 85.8 %phase_three.1 = (f32[160,1536]{1,0:T(8,128)}, f32[1,1536]{1,0:T(1,128)}, bf16[4,160,1536]{2,1,0:T(8,128)(2,1)}, f32[192,2560]{1,0:T(8,128)}, f32[192,2560]{1,0:T(8,128)}) custom-call(bf16[4,160,1536]{2,1,0:T(8,128)(2,1)} %bitcast.40, f32[160,1536]{1,0:T(8,128)} %get-tuple-element.50.residual, bf16[160,1536]{1,0:T(8,128)(2,1)} %cot.3, ...), custom_call_target="tpu_custom_call" | custom-call | tf_op jit(solution)/shard_map/phase_three/pallas_call | solution.py:417
  287.2 117.4 %backward.1 = (bf16[160,1536]{1,0:T(8,128)(2,1)}, f32[160,1536]{1,0:T(8,128)}, f32[192,128]{1,0:T(8,128)}, f32[192,1536]{1,0:T(8,128)}, f32[192,512]{1,0:T(8,128...) custom-call(bf16[4,160,1536]{2,1,0:T(8,128)(2,1)} %bitcast.38, ...), custom_call_target="tpu_custom_call" | custom-call | tf_op jit(solution)/shard_map/backward/pallas_call | solution.py:817
  404.6 2.0 copy.120
  406.7 1.9 copy.123
  408.6 0.8 slice_reduce_fusion
  409.4 2.0 copy.118
  411.4 1.9 copy.121
  413.3 2.0 copy.119
  415.4 1.9 copy.122
  417.3 0.8 copy.131
  418.1 2.3 copy.132
  420.4 1.0 copy.133
  421.4 0.7 copy.134
  422.1 0.7 copy.135
  422.9 1.0 copy.136
  (32 shorter events, 0.1 us)
Async XLA Ops:
  4.0 5.7 %copy-start.2 = (bf16[192,5,512]{2,0,1:T(8,128)(2,1)S(1)}, bf16[192,5,512]{2,0,1:T(8,128)(2,1)}, u32[]{:S(2)}) copy-start(bf16[192,5,512]{2,0,1:T(8,128)(2,1)} %param.23) | copy-start | bytes 2949124
  9.8 1.9 copy-start.3
  11.7 1.9 copy-start.4
  13.6 1.9 copy-start.9
  13.6 2.0 copy-start.10
  406.7 1.9 copy-start.8
  415.4 1.9 copy-start.5
  417.3 3.0 copy-start.1
  418.1 3.3 copy-start.7
  420.4 1.8 copy-start.6
  420.4 2.5 copy-start

commit v6 on v5

--- a/solution.py
+++ b/solution.py
@@ -19,6 +19,7 @@
 F32 = jnp.float32
 BF16 = jnp.bfloat16
 MESH = pl.DeviceIdType.MESH
+LANES = 128
 VMEM_LIMIT = 60 * 2**20
 
 
@@ -248,6 +249,93 @@
             pl.when(z < o)(to_right[o].wait_send)
         if o < last:
             pl.when(z > o)(to_left[o].wait_send)
+
+
+def line_sum_gather(links, part, acc, from_left, from_right, finish, own, full, parts=2):
+    z, last = links.z, links.members - 1
+    rows = own.shape[0] // parts
+    spans = [pl.ds(h * rows, rows) for h in range(parts)]
+    right, left = (links.d, z + 1), (links.d, z - 1)
+    sum_r, sum_l, go_r, go_l, local = {}, {}, {}, {}, []
+    for h, span in enumerate(spans):
+        for o in range(last + 1):
+            if o > 0:
+                sum_r[h, o] = links.remote(acc.at[o, span], from_left.at[o, span], right)
+            if o < last:
+                sum_l[h, o] = links.remote(acc.at[o, span], from_right.at[o, span], left)
+        for s in range(last):
+            at_r, at_l = jnp.maximum(z - s, 0), jnp.minimum(z + s, last)
+            here_r, here_l = full.at[at_r, span], full.at[at_l, span]
+            go_r[h, s] = links.remote(own.at[span] if s == 0 else here_r, here_r, right)
+            go_l[h, s] = links.remote(own.at[span] if s == 0 else here_l, here_l, left)
+
+    def pass_right(h, o):
+        @pl.when(z > 0)
+        def _():
+            sum_r[h, o].wait_recv()
+            add_rows(acc.at[o, spans[h]], from_left.at[o, spans[h]])
+
+        sum_r[h, o].start()
+
+    def pass_left(h, o):
+        @pl.when(z < last)
+        def _():
+            sum_l[h, o].wait_recv()
+            add_rows(acc.at[o, spans[h]], from_right.at[o, spans[h]])
+
+        sum_l[h, o].start()
+
+    def send(h, s):
+        pl.when((z < last) & (z >= s))(go_r[h, s].start)
+        pl.when((z > 0) & (z + s <= last))(go_l[h, s].start)
+
+    @pl.when(z == 0)
+    def _():
+        from_left[0] = jnp.zeros(from_left.shape[1:], from_left.dtype)
+
+    @pl.when(z == last)
+    def _():
+        from_right[last] = jnp.zeros(from_right.shape[1:], from_right.dtype)
+
+    made = set()
+    for j in range(last):
+        for o in (last - j, j):
+            if o not in made:
+                made.add(o)
+                part(o)
+        for h in range(parts):
+            pl.when((z < last - j) & (2 * z < last))(functools.partial(pass_right, h, last - j))
+            pl.when(z > j)(functools.partial(pass_left, h, j))
+            pl.when((z < last - j) & (2 * z >= last))(functools.partial(pass_right, h, last - j))
+            yield
+    for h in range(parts):
+        for o in range(last + 1):
+            if o > 0:
+                pl.when(z == o)(sum_r[h, o].wait_recv)
+            if o < last:
+                pl.when(z == o)(sum_l[h, o].wait_recv)
+        finish(h * rows, rows)
+        send(h, 0)
+        local.append(links.move(own.at[spans[h]], full.at[z, spans[h]]))
+        yield
+    for s in range(last):
+        for h in range(parts):
+            pl.when((z > 0) & (z - 1 >= s))(go_r[h, s].wait_recv)
+            pl.when((z < last) & (z + 1 + s <= last))(go_l[h, s].wait_recv)
+            if s + 1 < last:
+                send(h, s + 1)
+            yield
+    for h in range(parts):
+        for o in range(last + 1):
+            if o > 0:
+                pl.when(z < o)(sum_r[h, o].wait_send)
+            if o < last:
+                pl.when(z > o)(sum_l[h, o].wait_send)
+        for s in range(last):
+            pl.when((z < last) & (z >= s))(go_r[h, s].wait_send)
+            pl.when((z > 0) & (z + s <= last))(go_l[h, s].wait_send)
+    for copy in local:
+        copy.wait()
 
 
 def plane_gather(links, own, full):
@@ -337,11 +425,17 @@
 
 
 def plane_result(mine, theirs, end_x, end_y, out, step=16):
-    @pl.loop(0, out.shape[0] // step)
+    @pl.loop(0, out.shape[-2] // step)
     def _(i):
         at = pl.ds(pl.multiple_of(i * step, step), step)
         own = mine[at].astype(F32) + theirs[0, at].astype(F32)
-        out[at] = (own + end_x[at].astype(F32) + end_y[at].astype(F32)).astype(out.dtype)
+        total = (own + end_x[at].astype(F32) + end_y[at].astype(F32)).astype(out.dtype)
+        if len(out.shape) == 2:
+            out[at] = total
+        else:
+            cols = out.shape[2]
+            for e in range(out.shape[0]):
+                out[e, at] = total[:, e * cols : (e + 1) * cols]
 
 
 def line_result(z, acc, from_left, from_right, at):
@@ -382,26 +476,27 @@
     links.greet()
     for_gate, for_up = rest[:6], rest[6:]
 
-    def chain():
-        links.move(part, acc).wait()
-        yield from line_scatter(links, lambda o: None, acc, from_left, from_right)
-        gain_part[...] = jnp.zeros(gain_part.shape, F32)
-
-        @pl.loop(0, residual.shape[0] // 16)
+    def finish(first, count):
+        @pl.loop(0, count // 16)
         def _(i):
-            at = pl.ds(pl.multiple_of(i * 16, 16), 16)
+            at = pl.ds(pl.multiple_of(first + i * 16, 16), 16)
             grad = line_result(links.z, acc, from_left, from_right, at)
             here = residual[at]
             factor = rms_factor(here)
             gain_part[...] += jnp.sum(grad * here * factor, axis=0, keepdims=True)
-            total = cot[at].astype(F32) + norm_back(here, factor, gain[...], grad)
+            total = cot[at].astype(F32) + norm_back(here, factor, gain[1:2], grad)
             grad_residual[at] = total
             grad_out[at] = (branch_scale * total).astype(BF16)
 
-        yield from line_gather(links, grad_out, out_all)
+    def chain():
+        links.move(part, acc).wait()
+        gain_part[...] = jnp.zeros(gain_part.shape, F32)
+        yield from line_sum_gather(
+            links, lambda o: None, acc, from_left, from_right, finish, grad_out, out_all
+        )
 
     run(
-        "uuzzuzgzgzguz",
+        "uuzuzzgzzgzzzzzzg",
         z=chain(),
         g=plane_scatter(links, gate, *for_gate),
         u=plane_scatter(links, up, *for_up),
@@ -411,18 +506,18 @@
     links.finish()
 
 
-def third_phase(members, part, residual, cot, gain, gate, up):
+def third_phase(members, own_experts, part, residual, cot, gain, gate, up):
     rows, width = cot.shape
     blocks = pltpu.VMEM((members, rows, width), BF16)
     return comm_call(
-        third_kernel, "phase_three", 3, members, 60, 16,
+        third_kernel, "phase_three", 3, members, 80, 16,
         [ANY, VMEM, VMEM, VMEM, ANY, ANY], [VMEM, VMEM, ANY, VMEM, VMEM],
         [
             sds((rows, width), F32),
             sds((1, width), F32),
             sds((members, rows, width), BF16),
-            sds(gate.shape[1:], F32),
-            sds(up.shape[1:], F32),
+            sds((own_experts, gate.shape[1], gate.shape[2] // own_experts), F32),
+            sds((own_experts, up.shape[1], up.shape[2] // own_experts), F32),
         ],
         [blocks, blocks, blocks, pltpu.VMEM((rows, width), BF16)]
         + plane_scratch(*gate.shape[1:])
@@ -430,6 +525,10 @@
     )(part, residual, cot, gain, gate, up)
 
 
+def lane_ids(rows):
+    return lax.broadcasted_iota(jnp.int32, (rows, LANES), 1)
+
+
 def dims(a, b):
     return (((a,), (b,)), ((), ()))
 
@@ -446,7 +545,12 @@
     return lax.dot_general(a, b, dims(0, 0), preferred_element_type=F32)
 
 
-def expert_kernel(capacity, slot_row, slot_col, weight_row, normed, cot, w_gate, w_up, w_down, mixture, grad_normed, d_gate, d_up, d_down, mix_sum, grad_sum):
+def first_lanes():
+    same = lax.broadcasted_iota(jnp.int32, (16, LANES), 0) == lax.broadcasted_iota(jnp.int32, (16, LANES), 1)
+    return same.astype(BF16)
+
+
+def expert_kernel(capacity, own_experts, route, normed, cot, w_gate, w_up, w_down, mixture, grad_normed, d_gate, d_up, d_down, mix_sum, grad_sum, slot_cols, weight_cols, slot_rows):
     e = pl.program_id(0)
     span = normed.shape[0]
 
@@ -454,12 +558,34 @@
     def _():
         mix_sum[...] = jnp.zeros(mix_sum.shape, F32)
         grad_sum[...] = jnp.zeros(grad_sum.shape, F32)
-
-    slots = slot_row[0]
-    picks = slots == lax.broadcasted_iota(jnp.int32, (capacity, span), 0)
-    pick = picks.astype(BF16)
-    gate_col = jnp.sum(jnp.where(picks, weight_row[0], 0.0), axis=1, keepdims=True)
-    put = (slot_col[0] == lax.broadcasted_iota(jnp.int32, (span, capacity), 1)).astype(BF16)
+        lane = lane_ids(LANES)
+        name = (lax.axis_index("expert") * own_experts + lane).astype(F32)
+        name = jnp.where(lane < own_experts, name, -1.0)
+        upto = (lane <= lax.broadcasted_iota(jnp.int32, (LANES, LANES), 0)).astype(BF16)
+        before = jnp.zeros((1, LANES), F32)
+        for b in range(span // LANES):
+            at = pl.ds(b * LANES, LANES)
+            chosen, weight = jnp.zeros((LANES, LANES), F32), jnp.zeros((LANES, LANES), F32)
+            for k in range(TOP):
+                named = route[at, k : k + 1] == name
+                chosen = jnp.where(named, 1.0, chosen)
+                weight = jnp.where(named, route[at, TOP + k : TOP + k + 1], weight)
+            slot = mm(upto, chosen.astype(BF16)) + (before - 1.0)
+            slot_cols[at] = jnp.where((chosen > 0.0) & (slot < capacity), slot, -1.0)
+            weight_cols[at] = weight
+            before = before + jnp.sum(chosen, axis=0, keepdims=True)
+        slot_rows[...] = mm_nt(first_lanes(), slot_cols[...].astype(BF16))
+
+    def column(values):
+        return jnp.sum(jnp.where(lane_ids(span) == e, values[...], 0.0), axis=1, keepdims=True)
+
+    slots = lax.broadcasted_iota(jnp.int32, (capacity, span), 0).astype(F32)
+    pick = (slot_rows[pl.ds(e, 1)] == slots).astype(BF16)
+    puts = column(slot_cols) == lax.broadcasted_iota(jnp.int32, (span, capacity), 1).astype(F32)
+    put = puts.astype(BF16)
+    gate_row = jnp.sum(jnp.where(puts, column(weight_cols), 0.0), axis=0, keepdims=True)
+    same = lax.broadcasted_iota(jnp.int32, (capacity, capacity), 0) == lax.broadcasted_iota(jnp.int32, (capacity, capacity), 1)
+    gate_col = jnp.sum(jnp.where(same, gate_row, 0.0), axis=1, keepdims=True)
     received = mm(pick, normed[...]).astype(BF16)
     pre_gate, pre_up = mm(received, w_gate[...]), mm(received, w_up[...])
     sig = 1.0 / (1.0 + jnp.exp(-pre_gate))
@@ -483,31 +609,29 @@
         grad_normed[...] = grad_sum[...].astype(BF16)
 
 
-def experts(slot, weight, normed, cot, w_gate, w_up, w_down, ff, capacity):
-    own_experts, span = slot.shape
-    width = normed.shape[1]
+def experts(own_experts, capacity, route, normed, cot, w_gate, w_up, w_down):
+    span, width = normed.shape
+    ff = w_gate.shape[1] // own_experts
     whole = pl.BlockSpec((span, width), lambda e: (0, 0))
     column = pl.BlockSpec((width, ff), lambda e: (0, e))
-    row = pl.BlockSpec((1, 1, span), lambda e: (e, 0, 0))
     grads = jax.ShapeDtypeStruct(w_gate.shape, BF16)
     rows = jax.ShapeDtypeStruct((span, width), BF16)
     return pl.pallas_call(
-        functools.partial(expert_kernel, capacity),
+        functools.partial(expert_kernel, capacity, own_experts),
         grid=(own_experts,),
-        in_specs=[row, pl.BlockSpec((1, span, 1), lambda e: (e, 0, 0)), row, whole, whole, column, column, column],
+        in_specs=[pl.BlockSpec(route.shape, lambda e: (0, 0)), whole, whole, column, column, column],
         out_specs=[whole, whole, column, column, column],
         out_shape=[rows, rows, grads, grads, grads],
-        scratch_shapes=[pltpu.VMEM((span, width), F32), pltpu.VMEM((span, width), F32)],
+        scratch_shapes=[
+            pltpu.VMEM((span, width), F32),
+            pltpu.VMEM((span, width), F32),
+            pltpu.VMEM((span, LANES), F32),
+            pltpu.VMEM((span, LANES), F32),
+            pltpu.VMEM((16, span), F32),
+        ],
         compiler_params=pltpu.CompilerParams(vmem_limit_bytes=VMEM_LIMIT),
         name="experts",
-    )(slot[:, None, :], slot[:, :, None], weight[:, None, :], normed, cot, w_gate, w_up, w_down)
-
-
-LANES = 128
-
-
-def lane_ids(rows):
-    return lax.broadcasted_iota(jnp.int32, (rows, LANES), 1)
+    )(route, normed, cot, w_gate, w_up, w_down)
 
 
 def turn(x, cosine, sine):
@@ -527,13 +651,16 @@
     out[1, 1, at] = jnp.where(low, zero, block).astype(BF16)
 
 
-def attention_setup(seg_row, seg_col, bias):
+def attention_setup(segment, bias):
     span = bias.shape[0]
+    same = lax.broadcasted_iota(jnp.int32, (LANES, LANES), 0) == lane_ids(LANES)
     for b in range(span // LANES):
         at = pl.ds(b * LANES, LANES)
         row = b * LANES + lax.broadcasted_iota(jnp.int32, (LANES, span), 0)
         col = lax.broadcasted_iota(jnp.int32, (LANES, span), 1)
-        ok = (seg_col[at] == seg_row[...]) & (col <= row)
+        here = segment[:, b * LANES : (b + 1) * LANES]
+        here = jnp.sum(jnp.where(same, here, 0.0), axis=1, keepdims=True)
+        ok = (here == segment[...]) & (col <= row)
         bias[at] = jnp.where(ok, 0.0, -1e30)
 
 
@@ -542,8 +669,7 @@
 
 
 def gain_rows(pack_all, first):
-    pick = lax.broadcasted_iota(jnp.int32, (16, LANES), 0) == lax.broadcasted_iota(jnp.int32, (16, LANES), 1)
-    return mm_nt(pick.astype(BF16), weight_columns(pack_all, first, LANES))
+    return mm_nt(first_lanes(), weight_columns(pack_all, first, LANES))
 
 
 def attend_steps(qkv, kx, vx, bias, probs, attended):
@@ -569,9 +695,9 @@
 
 
 def forward_kernel(
-    members, tokens, cot, route, pack, gate, up, down, seg_row, seg_col, cosine, sine,
-    cot_all, route_all, pack_all, gate_all, up_all, down_all, normed_attn, qkv, kx, vx, probs, attended, residual, normed_all,
-    send, recv, local, tokens_all, bias, acc, from_left, from_right, normed,
+    members, tokens, cot, route, w_query, w_key, w_value, w_out, gain_attn, gain_ffn, gate, up, down, segment, cosine, sine,
+    cot_all, route_all, pack_all, gate_all, up_all, down_all, normed_attn, qkv, kx, vx, probs, attended, residual, normed_all, gains,
+    send, recv, local, pack, tokens_all, bias, acc, from_left, from_right, normed,
 ):
     links = Links(send, recv, local, members)
     links.greet()
@@ -580,13 +706,27 @@
     q_cols = attended.shape[1]
     qkv_cols = qkv.shape[1]
 
+    def pack_chain():
+        loads, at = [], 0
+        for weight in (w_query, w_key, w_value, w_out):
+            cols = weight.shape[1] // members
+            mine = pl.ds(pl.multiple_of(links.z * cols, LANES), cols)
+            loads.append(links.move(weight.at[:, mine], pack.at[:, at : at + cols]))
+            at += cols
+        which = lax.broadcasted_iota(jnp.int32, (16, pack.shape[0]), 0)
+        both = jnp.where(which == 0, gain_attn[...].astype(F32), jnp.where(which == 1, gain_ffn[...].astype(F32), 0.0))
+        pack[:, at:] = mm_tn(both.astype(BF16), first_lanes()).astype(BF16)
+        for load in loads:
+            load.wait()
+        yield from plane_gather(links, pack, pack_all)
+
     def produce(o):
         acc[o] = mm_nt(attended[o * rows : (o + 1) * rows], weight_columns(pack_all, qkv_cols, q_cols)).astype(BF16)
 
     def chain():
-        attention_setup(seg_row, seg_col, bias)
+        attention_setup(segment, bias)
         yield
-        gains = gain_rows(pack_all, qkv_cols + q_cols)
+        gains[...] = gain_rows(pack_all, qkv_cols + q_cols)
 
         @pl.loop(0, span // 16)
         def _(i):
@@ -610,23 +750,23 @@
 
         yield
         yield from attend_steps(qkv, kx, vx, bias, probs, attended)
-        yield from line_scatter(links, produce, acc, from_left, from_right)
-
-        @pl.loop(0, rows // 16)
-        def _(i):
-            at = pl.ds(pl.multiple_of(i * 16, 16), 16)
-            here = tokens[at].astype(F32) + branch_scale * line_result(links.z, acc, from_left, from_right, at)
-            residual[at] = here
-            normed[at] = (here * rms_factor(here) * gains[1:2]).astype(BF16)
-
-        yield from line_gather(links, normed, normed_all)
+
+        def finish(first, count):
+            @pl.loop(0, count // 16)
+            def _(i):
+                at = pl.ds(pl.multiple_of(first + i * 16, 16), 16)
+                here = tokens[at].astype(F32) + branch_scale * line_result(links.z, acc, from_left, from_right, at)
+                residual[at] = here
+                normed[at] = (here * rms_factor(here) * gains[1:2]).astype(BF16)
+
+        yield from line_sum_gather(links, produce, acc, from_left, from_right, finish, normed, normed_all)
 
     run(
         FORWARD_ORDER,
         t=line_gather(links, tokens, tokens_all),
         r=line_gather(links, route, route_all),
         c=line_gather(links, cot, cot_all),
-        p=plane_gather(links, pack, pack_all),
+        p=pack_chain(),
         g=plane_gather(links, gate, gate_all),
         u=plane_gather(links, up, up_all),
         d=plane_gather(links, down, down_all),
@@ -635,22 +775,25 @@
     links.finish()
 
 
-FORWARD_ORDER = "tpptdatpppctpatacpadrpgatcaacdparuagrrttcr"
-
-
-def forward_phase(members, tokens, cot, route, pack, gate, up, down, seg_row, seg_col, cosine, sine, q_cols, qkv_cols):
+FORWARD_ORDER = "tptpdptpcaptgaaacdtrgatcaardaagdattpuparparadrpaarrd"
+
+
+def forward_phase(members, tokens, cot, route, w_query, w_key, w_value, w_out, gain_attn, gain_ffn, gate, up, down, segment, cosine, sine):
     rows, width = tokens.shape
+    q_cols = w_query.shape[1] // members
+    qkv_cols = q_cols + 2 * w_key.shape[1] // members
+    pack = (w_query.shape[0], qkv_cols + q_cols + LANES)
     span = rows * members
     blocks = pltpu.VMEM((members, rows, width), BF16)
     heads = q_cols // HEAD_SIZE
     return comm_call(
-        forward_kernel, "forward", 1, members, 100, 16,
-        [VMEM, ANY, ANY, ANY, ANY, ANY, ANY, VMEM, VMEM, VMEM, VMEM],
-        [ANY, ANY, VMEM, ANY, ANY, ANY, VMEM, VMEM, VMEM, VMEM, VMEM, VMEM, VMEM, ANY],
+        forward_kernel, "forward", 1, members, 120, 16,
+        [VMEM, ANY, ANY, ANY, ANY, ANY, ANY, VMEM, VMEM, ANY, ANY, ANY, VMEM, VMEM, VMEM],
+        [ANY, ANY, VMEM, ANY, ANY, ANY, VMEM, VMEM, VMEM, VMEM, VMEM, VMEM, VMEM, ANY, VMEM],
         [
             sds((members, rows, width), BF16),
             sds((members, *route.shape), F32),
-            sds((8, *pack.shape), BF16),
+            sds((8, *pack), BF16),
             sds((8, *gate.shape), BF16),
             sds((8, *up.shape), BF16),
             sds((8, *down.shape), BF16),
@@ -662,8 +805,10 @@
             sds((span, q_cols), BF16),
             sds((rows, width), F32),
             sds((members, rows, width), BF16),
+            sds((16, width), F32),
         ],
         [
+            pltpu.VMEM(pack, BF16),
             blocks,
             pltpu.VMEM((span, span), F32),
             blocks,
@@ -671,7 +816,7 @@
             blocks,
             pltpu.VMEM((rows, width), BF16),
         ],
-    )(tokens, cot, route, pack, gate, up, down, seg_row, seg_col, cosine, sine)
+    )(tokens, cot, route, w_query, w_key, w_value, w_out, gain_attn, gain_ffn, gate, up, down, segment, cosine, sine)
 
 
 def attend_back_steps(qkv, kx, vx, probs, grad_attended, cosine, sine, grad_k, grad_v, grad_qkv):
@@ -714,7 +859,7 @@
 
 
 def backward_kernel(
-    members, mixture, residual, grad_out_all, grad_residual, gain_ffn_part, tokens, down, pack_all, normed_attn, qkv, kx, vx, probs, attended, cosine, sine,
+    members, mixture, residual, grad_out_all, grad_residual, gain_ffn_part, tokens, down, row_gains, pack_all, normed_attn, qkv, kx, vx, probs, attended, cosine, sine,
     output, grad_tokens, gains, d_query, d_key, d_value, d_out, d_down,
     send, recv, local, acc_m, left_m, right_m, acc, from_left, from_right, grad_attended, grad_k, grad_v, grad_qkv, gain_part,
     for_w_out, for_w_qkv, own_out, own_qkv, all_out, all_qkv, *rest,
@@ -727,7 +872,6 @@
     with_out, with_qkv, with_down = rest[:5], rest[5:10], rest[10:]
     pairs = for_w_out.shape[0] // 2
     step = width // pairs
-    row_gains = gain_rows(pack_all, qkv_cols + q_cols)
 
     def out_chain():
         for i in range(pairs):
@@ -769,8 +913,7 @@
             for_w_qkv[2 * i : 2 * i + 2, :, :qkv_cols] = term.astype(BF16).reshape(2, step // 2, qkv_cols)
         which = lax.broadcasted_iota(jnp.int32, (16, width), 0)
         both = jnp.where(which == 0, gain_part[...] / row_gains[0:1], jnp.where(which == 1, gain_ffn_part[...], 0.0))
-        pick = lax.broadcasted_iota(jnp.int32, (16, LANES), 0) == lax.broadcasted_iota(jnp.int32, (16, LANES), 1)
-        columns = mm_tn(both.astype(BF16), pick.astype(BF16))
+        columns = mm_tn(both.astype(BF16), first_lanes())
         for_w_qkv[:, :, qkv_cols:] = columns.astype(BF16).reshape(2 * pairs, step // 2, LANES)
         yield from plane_scatter(links, for_w_qkv, None, *with_qkv)
         plane_result(for_w_qkv.at[links.d], with_qkv[0], with_qkv[3], with_qkv[4], own_qkv)
@@ -807,7 +950,7 @@
 BACKWARD_ORDER = "amoadmmadaaaoqoqoqaoaq"
 
 
-def backward_phase(members, mixture, residual, grad_out_all, grad_residual, gain_ffn_part, tokens, down, pack_all, normed_attn, qkv, kx, vx, probs, attended, cosine, sine):
+def backward_phase(members, own_experts, mixture, residual, grad_out_all, grad_residual, gain_ffn_part, tokens, down, row_gains, pack_all, normed_attn, qkv, kx, vx, probs, attended, cosine, sine):
     rows, width = tokens.shape
     span, q_cols = attended.shape
     qkv_cols = qkv.shape[1]
@@ -816,7 +959,7 @@
     line = [pltpu.VMEM((members, rows, width), BF16)] * 3
     return comm_call(
         backward_kernel, "backward", 4, members, 100, 32,
-        [ANY, VMEM, VMEM, VMEM, VMEM, VMEM, ANY] + [VMEM] * 9,
+        [ANY, VMEM, VMEM, VMEM, VMEM, VMEM, ANY] + [VMEM] * 10,
         [VMEM] * 8,
         [
             sds((rows, width), BF16),
@@ -826,7 +969,7 @@
             sds((own, members * kv_cols), F32),
             sds((own, members * kv_cols), F32),
             sds((own, members * q_cols), F32),
-            sds(down.shape[1:], F32),
+            sds((own_experts, own, down.shape[2] // own_experts), F32),
         ],
         [
             *line,
@@ -846,7 +989,7 @@
             *plane_scratch(own, qkv_cols + LANES, False),
             *plane_scratch(*down.shape[1:]),
         ],
-    )(mixture, residual, grad_out_all, grad_residual, gain_ffn_part, tokens, down, pack_all, normed_attn, qkv, kx, vx, probs, attended, cosine, sine)
+    )(mixture, residual, grad_out_all, grad_residual, gain_ffn_part, tokens, down, row_gains, pack_all, normed_attn, qkv, kx, vx, probs, attended, cosine, sine)
 
 
 def all_blocks(x, axis):
@@ -968,7 +1111,6 @@
     tokens_all = tokens_all.reshape(span, width).astype(F32)
     cot_all = cot_all.reshape(span, width)
     route_all = route_all.reshape(span, 2 * TOP)
-    ids_all, gates_all = route_all[:, :TOP].astype(jnp.int32), route_all[:, TOP:]
     pack_all = pack_all.reshape(width, -1)
     gate_all = gate_all.reshape(width, -1)
     qkv_cols = q_cols + 2 * kv_cols
@@ -1004,15 +1146,8 @@
     normed_all = normed_all.reshape(span, width)
     up_all, down_all = up_all.reshape(width, -1), down_all.reshape(width, -1)
 
-    expert_of = member * own_experts + jnp.arange(own_experts, dtype=jnp.int32)
-    named = ids_all[None, :, :] == expert_of[:, None, None]
-    chosen = jnp.any(named, axis=2)
-    weight = jnp.sum(jnp.where(named, gates_all[None], 0.0), axis=2)
-    upto = (place[:, None] <= place[None, :]).astype(BF16)
-    slot = dot(chosen.astype(BF16), upto).astype(jnp.int32) - 1
-    slot = jnp.where(chosen & (slot < capacity), slot, -1)
     mixture, grad_normed, *by_kind = experts(
-        slot, weight, normed_all, cot_all, gate_all, up_all, down_all, ff, capacity
+        own_experts, capacity, route_all, normed_all, cot_all, gate_all, up_all, down_all
     )
     output = (residual + branch_scale * scatter(mixture, "expert")).astype(BF16)
     by_kind = [one.reshape(devices, -1, own_experts * ff) for one in by_kind]
@@ -1108,79 +1243,49 @@
 ):
     rows, width = tokens.shape
     members, devices = lax.axis_size("expert"), lax.axis_size("dp")
-    member = lax.axis_index("expert")
     span = rows * members
     own_experts, ff = expert_gate.shape[1], expert_gate.shape[2]
     capacity = rows * TOP // own_experts
-    q_cols = w_query.shape[1] // members
-    kv_cols = key_weight.shape[1] // members
-    qkv_cols = q_cols + 2 * kv_cols
-
-    def mine(weight, cols):
-        return lax.dynamic_slice_in_dim(weight, member * cols, cols, axis=1)
-
-    pack = jnp.concatenate(
-        [
-            mine(w_query, q_cols),
-            mine(key_weight, kv_cols),
-            mine(value_weight, kv_cols),
-            mine(w_out, q_cols),
-            gain_attn[:, None],
-            gain_ffn[:, None],
-            jnp.zeros((gain_attn.shape[0], 126), BF16),
-        ],
-        axis=1,
-    )
     route = jnp.concatenate([expert_ids.astype(F32), gates], axis=1)
     segment, position = layout(lengths[0], order[0], span)
-    cosine, sine = rotation(position)
-    cosine = jnp.tile(cosine, (1, 4))
-    sine = jnp.tile(jnp.concatenate([-sine, sine], axis=1), (1, 2))
-    place = jnp.arange(span, dtype=jnp.int32)
+    lane = jnp.arange(LANES, dtype=jnp.int32) % HEAD_SIZE
+    half = HEAD_SIZE // 2
+    frequency = rope_base ** (-((lane % half).astype(F32) * (2.0 / HEAD_SIZE)))
+    angles = position[:, None] * frequency[None, :]
+    cosine, sine = jnp.cos(angles), jnp.where(lane < half, -1.0, 1.0) * jnp.sin(angles)
     (
         cot_all, route_all, pack_all, gate_all, up_all, down_all,
-        normed_attn, qkv, kx, vx, probs, attended, residual, normed_all,
+        normed_attn, qkv, kx, vx, probs, attended, residual, normed_all, gains,
     ) = forward_phase(
-        members, tokens, cotangent, route, pack,
+        members, tokens, cotangent, route, w_query, key_weight, value_weight, w_out,
+        gain_attn[None], gain_ffn[None],
         expert_gate.reshape(-1, own_experts * ff),
         expert_up.reshape(-1, own_experts * ff),
         expert_down.reshape(-1, own_experts * ff),
-        segment[None, :], segment[:, None],
-        cosine, sine,
-        q_cols, qkv_cols,
+        segment.astype(F32)[None], cosine, sine,
     )
     cot_all = cot_all.reshape(span, width)
     normed_all = normed_all.reshape(span, width)
     route_all = route_all.reshape(span, 2 * TOP)
-    ids_all, gates_all = route_all[:, :TOP].astype(jnp.int32), route_all[:, TOP:]
     gate_all, up_all, down_all = (w.reshape(width, -1) for w in (gate_all, up_all, down_all))
-    gain_two = pack_all[:, :, qkv_cols + q_cols + 1].astype(F32).reshape(1, width)
-
-    expert_of = member * own_experts + jnp.arange(own_experts, dtype=jnp.int32)
-    named = ids_all[None, :, :] == expert_of[:, None, None]
-    chosen = jnp.any(named, axis=2)
-    weight = jnp.sum(jnp.where(named, gates_all[None], 0.0), axis=2)
-    upto = (place[:, None] <= place[None, :]).astype(BF16)
-    slot = dot(chosen.astype(BF16), upto).astype(jnp.int32) - 1
-    slot = jnp.where(chosen & (slot < capacity), slot, -1)
     mixture, grad_normed, *by_kind = experts(
-        slot, weight, normed_all, cot_all, gate_all, up_all, down_all, ff, capacity
+        own_experts, capacity, route_all, normed_all, cot_all, gate_all, up_all, down_all
     )
     by_kind = [one.reshape(devices, -1, own_experts * ff) for one in by_kind]
 
     grad_residual, gain_two_part, grad_attn_out, sum_gate, sum_up = third_phase(
-        members,
+        members, own_experts,
         grad_normed.reshape(members, rows, width),
         residual,
         cotangent,
-        gain_two,
+        gains,
         by_kind[0],
         by_kind[1],
     )
     (
-        output, grad_tokens, gains, d_query, d_key, d_value, d_out, d_down,
+        output, grad_tokens, grad_gains, d_query, d_key, d_value, d_out, d_down,
     ) = backward_phase(
-        members,
+        members, own_experts,
         mixture.reshape(members, rows, width),
         residual,
         grad_attn_out.reshape(span, width),
@@ -1188,21 +1293,22 @@
         gain_two_part,
         tokens,
         by_kind[2],
+        gains,
         pack_all,
         normed_attn, qkv, kx, vx, probs, attended, cosine, sine,
     )
     return (
         output,
         grad_tokens,
-        gains[:, 0],
-        gains[:, 1],
+        grad_gains[:, 0],
+        grad_gains[:, 1],
         d_query,
         d_key,
         d_value,
         d_out,
-        sum_gate.reshape(-1, own_experts, ff),
-        sum_up.reshape(-1, own_experts, ff),
-        d_down.reshape(-1, own_experts, ff),
+        sum_gate.transpose(1, 0, 2),
+        sum_up.transpose(1, 0, 2),
+        d_down.transpose(1, 0, 2),
     )
 
 

time: 433 us -> 400 us (0.924); the launches traced: 424 us -> 400 us
  Pallas kernels: 381 us -> 368 us
  local copies, waits for them, and re-layouts: 38.4 us -> 25.8 us
    pallas_call x3, Pallas kernels: 264 us -> 255 us  [the longest x1 134 us: forward_phase(): comm_call(forward_kernel, 'forward', 1, members, 120, 16, [VMEM, ANY, ANY...]
    pallas_call x3 -> x0, local copies, waits for them, and re-layouts: 6.1 us -> none  [the longest x2 4.06 us: third_phase(): comm_call(third_kernel, 'phase_three', 3, members, 60, 16, [ANY, VMEM, VM...]
    unnamed x35 -> x30, local copies, waits for them, and re-layouts: 14.2 us -> 16.2 us
where the time goes in v6:
time: 400 us
  Pallas kernels  368 us (92%)
  local copies, waits for them, and re-layouts  25.8 us (6%)
  other arithmetic  4.52 us (1%)
    pallas_call x1, Pallas kernels, forward_phase(): comm_call(forward_kernel, 'forward', 1, members, 120, 16, [VMEM, ANY, ANY...  134 us
    pallas_call x1, Pallas kernels, backward_phase(): comm_call(backward_kernel, 'backward', 4, members, 100, 32, [ANY, VMEM, V...  113 us
    pallas_call x1, Pallas kernels, third_phase(): comm_call(third_kernel, 'phase_three', 3, members, 80, 16, [ANY, VMEM, VM...  79.4 us
    pallas_call x1, Pallas kernels, experts(): pl.pallas_call(functools.partial(expert_kernel, capacity, own_experts), g...  42.2 us
    unnamed x30, local copies, waits for them, and re-layouts  16.2 us

profile of v6, /device:TPU:0, one launch (start us, length us, event | category | flops | bytes accessed | tf_op | source)
XLA Modules:
  0.0 399.5 jit_solution(11311041984987745284)
XLA Ops:
  0.6 0.9 select_reduce_fusion.2
  1.5 0.1 select_reduce_fusion.1
  1.6 1.2 broadcast_in_dim.57.gain_attn
  2.8 1.2 broadcast_in_dim.58.gain_ffn
  4.1 0.1 select_reduce_fusion
  4.2 0.6 convert_element_type.36.segment
  4.8 0.7 convert_element_type.33
  5.5 0.7 pad_maximum_fusion
  6.2 0.7 copy.49.route
  6.9 2.0 fusion
  9.0 0.0 copy-start.5
  9.0 1.6 copy.46
  10.6 1.4 copy.50.gate
  11.9 0.0 copy-done.5
  11.9 0.0 copy-start.6
  11.9 0.6 copy.47
  12.5 1.4 copy.51.up
  13.9 0.0 copy-done.6
  13.9 0.6 copy.48
  14.5 1.4 copy.52.down
  15.8 133.7 %forward.1 = (bf16[4,160,1536]{2,1,0:T(8,128)(2,1)}, f32[4,160,16]{2,1,0:T(8,128)}, bf16[8,192,1152]{2,1,0:T(8,128)(2,1)}, bf16[8,192,2560]{2,1,0:T(8,128)(2,1)}...) custom-call(bf16[160,1536]{1,0:T(8,128)(2,1)} %tokens.3, ...), custom_call_target="tpu_custom_call" | custom-call | tf_op jit(solution)/shard_map/forward/pallas_call | solution.py:789
  149.6 42.2 %experts.1 = (bf16[640,1536]{1,0:T(8,128)(2,1)}, bf16[640,1536]{1,0:T(8,128)(2,1)}, bf16[1536,2560]{1,0:T(8,128)(2,1)}, bf16[1536,2560]{1,0:T(8,128)(2,1)}, bf16[1536,2560]{1,0:T(8,128)(2,1)}) custom-call(f32[640,16]{1,0:T(8,128)} %bitcast.37, bf16[640,1536]{1,0:T(8,128)(2,1)} %bitcast.36, bf16[640,1536]{1,0:T(8,128)(2,1)} %bitcast.35, ...), custom_call_target="tpu_custom_call" | custom-call | tf_op jit(solution)/shard_map/experts/pallas_call | solution.py:619
  191.8 79.4 %phase_three.1 = (f32[160,1536]{1,0:T(8,128)}, f32[1,1536]{1,0:T(1,128)}, bf16[4,160,1536]{2,1,0:T(8,128)(2,1)}, f32[5,192,512]{2,1,0:T(8,128)}, f32[5,192,512]{2,1,0:T(8,128)}) custom-call(bf16[4,160,1536]{2,1,0:T(8,128)(2,1)} %bitcast.34, f32[160,1536]{1,0:T(8,128)} %get-tuple-element.51.residual, bf16[160,1536]{1,0:T(8,128)(2,1)} %cot.3, ...), custom_call_target="tpu_custom_call" | custom-call | tf_op jit(solution)/shard_map/phase_three/pallas_call | solution.py:512
  271.1 113.1 %backward.1 = (bf16[160,1536]{1,0:T(8,128)(2,1)}, f32[160,1536]{1,0:T(8,128)}, f32[192,128]{1,0:T(8,128)}, f32[192,1536]{1,0:T(8,128)}, f32[192,512]{1,0:T(8,128...) custom-call(bf16[4,160,1536]{2,1,0:T(8,128)(2,1)} %bitcast.32, ...), custom_call_target="tpu_custom_call" | custom-call | tf_op jit(solution)/shard_map/backward/pallas_call | solution.py:960
  384.3 0.0 copy-start.4
  384.3 1.8 slice_reduce_fusion
  386.1 1.8 copy.62
  387.9 0.0 copy-start.8
  387.9 2.3 copy.63
  390.2 0.0 copy-done.4
  390.2 0.0 copy-start.7
  390.2 0.0 copy-start.3
  390.2 1.0 copy.64
  391.2 0.0 copy-done.8
  391.2 0.0 copy-start.1
  391.2 0.7 copy.65
  392.0 0.0 copy-done.7
  392.0 0.7 copy.66
  392.7 0.0 copy-done.3
  392.7 1.0 copy.67
  393.7 0.0 copy-done.1
  393.7 0.0 copy-start
  393.7 1.3 copy.68
  395.0 1.0 copy-done
  396.0 0.0 copy-start.2
  396.0 1.3 copy.69
  397.3 1.0 copy-done.2
  398.3 1.3 copy.70
  (3 shorter events, 0.0 us)
Async XLA Ops:
  9.0 3.0 copy-start.5
  11.9 1.9 copy-start.6
  384.3 5.9 %copy-start.4 = (f32[192,1536]{1,0:T(8,128)S(1)}, f32[192,1536]{1,0:T(8,128)}, u32[]{:S(2)}) copy-start(f32[192,1536]{1,0:T(8,128)} %get-tuple-element.100) | copy-start | bytes 3538948
  387.9 3.3 copy-start.8
  390.2 1.8 copy-start.7
  390.2 2.5 copy-start.3
  391.2 2.5 copy-start.1
  393.7 2.3 copy-start
  396.0 2.3 copy-start.2

commit v7 on v6

--- a/solution.py
+++ b/solution.py
@@ -192,68 +192,9 @@
         target[at] = (target[at].astype(F32) + other[at].astype(F32)).astype(target.dtype)
 
 
-def line_scatter(links, part, acc, from_left, from_right):
+def line_sum(links, part, acc, from_left, from_right, finish, own=None, full=None, parts=2):
     z, last = links.z, links.members - 1
-    made = set()
-
-    def make(o):
-        if o not in made:
-            made.add(o)
-            part(o)
-
-    to_right = {o: links.remote(acc.at[o], from_left.at[o], (links.d, z + 1)) for o in range(1, last + 1)}
-    to_left = {o: links.remote(acc.at[o], from_right.at[o], (links.d, z - 1)) for o in range(last)}
-
-    def pass_right(o):
-        @pl.when(z > 0)
-        def _():
-            to_right[o].wait_recv()
-            add_rows(acc.at[o], from_left.at[o])
-
-        to_right[o].start()
-
-    def pass_left(o):
-        @pl.when(z < last)
-        def _():
-            to_left[o].wait_recv()
-            add_rows(acc.at[o], from_right.at[o])
-
-        to_left[o].start()
-
-    @pl.when(z == 0)
-    def _():
-        from_left[0] = jnp.zeros(from_left.shape[1:], from_left.dtype)
-
-    @pl.when(z == last)
-    def _():
-        from_right[last] = jnp.zeros(from_right.shape[1:], from_right.dtype)
-
-    for j in range(last):
-        make(last - j)
-        make(j)
-        pl.when((z < last - j) & (2 * z < last))(functools.partial(pass_right, last - j))
-        pl.when(z > j)(functools.partial(pass_left, j))
-        pl.when((z < last - j) & (2 * z >= last))(functools.partial(pass_right, last - j))
-        yield
-    for o in range(last + 1):
-
-        @pl.when(z == o)
-        def _(o=o):
-            if o > 0:
-                to_right[o].wait_recv()
-            if o < last:
-                to_left[o].wait_recv()
-
-    for o in range(last + 1):
-        if o > 0:
-            pl.when(z < o)(to_right[o].wait_send)
-        if o < last:
-            pl.when(z > o)(to_left[o].wait_send)
-
-
-def line_sum_gather(links, part, acc, from_left, from_right, finish, own, full, parts=2):
-    z, last = links.z, links.members - 1
-    rows = own.shape[0] // parts
+    rows = acc.shape[1] // parts
     spans = [pl.ds(h * rows, rows) for h in range(parts)]
     right, left = (links.d, z + 1), (links.d, z - 1)
     sum_r, sum_l, go_r, go_l, local = {}, {}, {}, {}, []
@@ -263,7 +204,7 @@
                 sum_r[h, o] = links.remote(acc.at[o, span], from_left.at[o, span], right)
             if o < last:
                 sum_l[h, o] = links.remote(acc.at[o, span], from_right.at[o, span], left)
-        for s in range(last):
+        for s in range(last if own is not None else 0):
             at_r, at_l = jnp.maximum(z - s, 0), jnp.minimum(z + s, last)
             here_r, here_l = full.at[at_r, span], full.at[at_l, span]
             go_r[h, s] = links.remote(own.at[span] if s == 0 else here_r, here_r, right)
@@ -315,10 +256,12 @@
             if o < last:
                 pl.when(z == o)(sum_l[h, o].wait_recv)
         finish(h * rows, rows)
+        if own is None:
+            continue
         send(h, 0)
         local.append(links.move(own.at[spans[h]], full.at[z, spans[h]]))
         yield
-    for s in range(last):
+    for s in range(last if own is not None else 0):
         for h in range(parts):
             pl.when((z > 0) & (z - 1 >= s))(go_r[h, s].wait_recv)
             pl.when((z < last) & (z + 1 + s <= last))(go_l[h, s].wait_recv)
@@ -331,7 +274,7 @@
                 pl.when(z < o)(sum_r[h, o].wait_send)
             if o < last:
                 pl.when(z > o)(sum_l[h, o].wait_send)
-        for s in range(last):
+        for s in range(last if own is not None else 0):
             pl.when((z < last) & (z >= s))(go_r[h, s].wait_send)
             pl.when((z > 0) & (z + s <= last))(go_l[h, s].wait_send)
     for copy in local:
@@ -397,7 +340,8 @@
             to_end_x = links.push(held[1].at[first], end_x.at[first], links.x)
         if k == 2:
             to_end_y = links.push(held[2].at[second], end_y.at[second], links.y)
-    yield
+        if k != 1:
+            yield
     to_mid_y.wait_recv()
     add_rows(held[1].at[second], mid_y)
     rest_x = links.push(held[1].at[second], end_x.at[second], links.x)
@@ -412,6 +356,7 @@
     to_end_y.wait_recv()
     rest_x.wait_recv()
     rest_y.wait_recv()
+    yield
 
 
 def plane_scratch(rows, cols, mine=True):
@@ -471,7 +416,7 @@
     return jax.ShapeDtypeStruct(shape, dtype)
 
 
-def third_kernel(members, part, residual, cot, gain, gate, up, grad_residual, gain_part, out_all, gate_out, up_out, send, recv, local, acc, from_left, from_right, grad_out, *rest):
+def third_kernel(members, part, mixture, residual, cot, gain, gate, up, output, grad_residual, gain_part, out_all, gate_out, up_out, send, recv, local, acc, from_left, from_right, acc_m, left_m, right_m, grad_out, *rest):
     links = Links(send, recv, local, members)
     links.greet()
     for_gate, for_up = rest[:6], rest[6:]
@@ -491,12 +436,24 @@
     def chain():
         links.move(part, acc).wait()
         gain_part[...] = jnp.zeros(gain_part.shape, F32)
-        yield from line_sum_gather(
+        yield from line_sum(
             links, lambda o: None, acc, from_left, from_right, finish, grad_out, out_all
         )
 
+    def finish_mixture(first, count):
+        @pl.loop(0, count // 16)
+        def _(i):
+            at = pl.ds(pl.multiple_of(first + i * 16, 16), 16)
+            here = residual[at] + branch_scale * line_result(links.z, acc_m, left_m, right_m, at)
+            output[at] = here.astype(BF16)
+
+    def mixture_chain():
+        links.move(mixture, acc_m).wait()
+        yield from line_sum(links, lambda o: None, acc_m, left_m, right_m, finish_mixture)
+
     run(
-        "uuzuzzgzzgzzzzzzg",
+        THIRD_ORDER,
+        m=mixture_chain(),
         z=chain(),
         g=plane_scatter(links, gate, *for_gate),
         u=plane_scatter(links, up, *for_up),
@@ -506,23 +463,28 @@
     links.finish()
 
 
-def third_phase(members, own_experts, part, residual, cot, gain, gate, up):
+THIRD_ORDER = "uzuzzgugmmzzguzzzgzmzmzmmzmugguuzm"
+
+
+def third_phase(members, own_experts, part, mixture, residual, cot, gain, gate, up):
     rows, width = cot.shape
     blocks = pltpu.VMEM((members, rows, width), BF16)
     return comm_call(
         third_kernel, "phase_three", 3, members, 80, 16,
-        [ANY, VMEM, VMEM, VMEM, ANY, ANY], [VMEM, VMEM, ANY, VMEM, VMEM],
+        [ANY, ANY, VMEM, VMEM, VMEM, ANY, ANY], [VMEM, VMEM, VMEM, ANY, VMEM, VMEM],
         [
+            sds((rows, width), BF16),
             sds((rows, width), F32),
             sds((1, width), F32),
             sds((members, rows, width), BF16),
             sds((own_experts, gate.shape[1], gate.shape[2] // own_experts), F32),
             sds((own_experts, up.shape[1], up.shape[2] // own_experts), F32),
         ],
-        [blocks, blocks, blocks, pltpu.VMEM((rows, width), BF16)]
+        [blocks] * 6
+        + [pltpu.VMEM((rows, width), BF16)]
         + plane_scratch(*gate.shape[1:])
         + plane_scratch(*up.shape[1:]),
-    )(part, residual, cot, gain, gate, up)
+    )(part, mixture, residual, cot, gain, gate, up)
 
 
 def lane_ids(rows):
@@ -759,7 +721,7 @@
                 residual[at] = here
                 normed[at] = (here * rms_factor(here) * gains[1:2]).astype(BF16)
 
-        yield from line_sum_gather(links, produce, acc, from_left, from_right, finish, normed, normed_all)
+        yield from line_sum(links, produce, acc, from_left, from_right, finish, normed, normed_all)
 
     run(
         FORWARD_ORDER,
@@ -859,27 +821,43 @@
 
 
 def backward_kernel(
-    members, mixture, residual, grad_out_all, grad_residual, gain_ffn_part, tokens, down, row_gains, pack_all, normed_attn, qkv, kx, vx, probs, attended, cosine, sine,
-    output, grad_tokens, gains, d_query, d_key, d_value, d_out, d_down,
-    send, recv, local, acc_m, left_m, right_m, acc, from_left, from_right, grad_attended, grad_k, grad_v, grad_qkv, gain_part,
-    for_w_out, for_w_qkv, own_out, own_qkv, all_out, all_qkv, *rest,
+    members, grad_out_all, grad_residual, gain_ffn_part, tokens, down, row_gains, pack_all, normed_attn, qkv, kx, vx, probs, attended, cosine, sine,
+    grad_tokens, gains, d_query, d_key, d_value, d_out, d_down,
+    send, recv, local, acc, from_left, from_right, grad_attended, grad_k, grad_v, grad_qkv, gain_part,
+    for_w_out, for_w_query, for_rest, own_out, own_query, own_rest, all_out, all_query, all_rest, *rest,
 ):
     links = Links(send, recv, local, members)
     links.greet()
     rows, width = tokens.shape
     q_cols, qkv_cols = attended.shape[1], qkv.shape[1]
     kv_cols = (qkv_cols - q_cols) // 2
-    with_out, with_qkv, with_down = rest[:5], rest[5:10], rest[10:]
+    with_out, with_query, with_rest, with_down = rest[:5], rest[5:10], rest[10:15], rest[15:]
     pairs = for_w_out.shape[0] // 2
     step = width // pairs
 
-    def out_chain():
+    def weight_term(rows_of, grads, out, cols):
         for i in range(pairs):
-            term = mm_tn(grad_out_all[:, i * step : (i + 1) * step], attended[...])
-            for_w_out[2 * i : 2 * i + 2] = term.astype(BF16).reshape(2, step // 2, q_cols)
-        yield from plane_scatter(links, for_w_out, None, *with_out)
-        plane_result(for_w_out.at[links.d], with_out[0], with_out[3], with_out[4], own_out)
-        yield from line_gather(links, own_out, all_out)
+            term = mm_tn(rows_of[:, i * step : (i + 1) * step], grads)
+            out[2 * i : 2 * i + 2, :, :cols] = term.astype(BF16).reshape(2, step // 2, cols)
+
+    def weight_chain(fill, part, mine, full, scratch):
+        fill()
+        yield from plane_scatter(links, part, None, *scratch)
+        plane_result(part.at[links.d], scratch[0], scratch[3], scratch[4], mine)
+        yield from line_gather(links, mine, full)
+
+    def fill_out():
+        weight_term(grad_out_all, attended[...], for_w_out, q_cols)
+
+    def fill_query():
+        weight_term(normed_attn, grad_qkv[:, :q_cols], for_w_query, q_cols)
+
+    def fill_rest():
+        weight_term(normed_attn, grad_qkv[:, q_cols:], for_rest, 2 * kv_cols)
+        which = lax.broadcasted_iota(jnp.int32, (16, width), 0)
+        both = jnp.where(which == 0, gain_part[...] / row_gains[0:1], jnp.where(which == 1, gain_ffn_part[...], 0.0))
+        columns = mm_tn(both.astype(BF16), first_lanes())
+        for_rest[:, :, 2 * kv_cols :] = columns.astype(BF16).reshape(2 * pairs, step // 2, LANES)
 
     def produce(o):
         at = slice(o * rows, (o + 1) * rows)
@@ -898,71 +876,52 @@
         yield
         yield from attend_back_steps(qkv, kx, vx, probs, grad_attended, cosine, sine, grad_k, grad_v, grad_qkv)
         gain_part[...] = jnp.zeros(gain_part.shape, F32)
-        yield from line_scatter(links, produce, acc, from_left, from_right)
-
-        @pl.loop(0, rows // 16)
-        def _(i):
-            at = pl.ds(pl.multiple_of(i * 16, 16), 16)
-            grad = line_result(links.z, acc, from_left, from_right, at)
-            here = tokens[at].astype(F32)
-            grad_tokens[at] = grad_residual[at] + norm_back(here, rms_factor(here), row_gains[0:1], grad)
-
-    def qkv_chain():
-        for i in range(pairs):
-            term = mm_tn(normed_attn[:, i * step : (i + 1) * step], grad_qkv[...])
-            for_w_qkv[2 * i : 2 * i + 2, :, :qkv_cols] = term.astype(BF16).reshape(2, step // 2, qkv_cols)
-        which = lax.broadcasted_iota(jnp.int32, (16, width), 0)
-        both = jnp.where(which == 0, gain_part[...] / row_gains[0:1], jnp.where(which == 1, gain_ffn_part[...], 0.0))
-        columns = mm_tn(both.astype(BF16), first_lanes())
-        for_w_qkv[:, :, qkv_cols:] = columns.astype(BF16).reshape(2 * pairs, step // 2, LANES)
-        yield from plane_scatter(links, for_w_qkv, None, *with_qkv)
-        plane_result(for_w_qkv.at[links.d], with_qkv[0], with_qkv[3], with_qkv[4], own_qkv)
-        yield from line_gather(links, own_qkv, all_qkv)
-
-    def mixture_chain():
-        links.move(mixture, acc_m).wait()
-        yield from line_scatter(links, lambda o: None, acc_m, left_m, right_m)
-
-        @pl.loop(0, rows // 16)
-        def _(i):
-            at = pl.ds(pl.multiple_of(i * 16, 16), 16)
-            here = residual[at] + branch_scale * line_result(links.z, acc_m, left_m, right_m, at)
-            output[at] = here.astype(BF16)
+        yield
+
+        def finish(first, count):
+            @pl.loop(0, count // 16)
+            def _(i):
+                at = pl.ds(pl.multiple_of(first + i * 16, 16), 16)
+                grad = line_result(links.z, acc, from_left, from_right, at)
+                here = tokens[at].astype(F32)
+                grad_tokens[at] = grad_residual[at] + norm_back(here, rms_factor(here), row_gains[0:1], grad)
+
+        yield from line_sum(links, produce, acc, from_left, from_right, finish)
 
     run(
         BACKWARD_ORDER,
-        m=mixture_chain(),
         d=plane_scatter(links, down, *with_down),
-        o=out_chain(),
+        o=weight_chain(fill_out, for_w_out, own_out, all_out, with_out),
         a=chain(),
-        q=qkv_chain(),
+        q=weight_chain(fill_query, for_w_query, own_query, all_query, with_query),
+        r=weight_chain(fill_rest, for_rest, own_rest, all_rest, with_rest),
     )
     plane_result(with_down[0].at[0], with_down[1], with_down[4], with_down[5], d_down)
     for m in range(members):
         d_out[:, m * q_cols : (m + 1) * q_cols] = all_out[m].astype(F32)
-        d_query[:, m * q_cols : (m + 1) * q_cols] = all_qkv[m, :, :q_cols].astype(F32)
-        d_key[:, m * kv_cols : (m + 1) * kv_cols] = all_qkv[m, :, q_cols : q_cols + kv_cols].astype(F32)
-        d_value[:, m * kv_cols : (m + 1) * kv_cols] = all_qkv[m, :, q_cols + kv_cols : qkv_cols].astype(F32)
-    gains[...] = sum(all_qkv[m, :, qkv_cols:].astype(F32) for m in range(members))
+        d_query[:, m * q_cols : (m + 1) * q_cols] = all_query[m].astype(F32)
+        d_key[:, m * kv_cols : (m + 1) * kv_cols] = all_rest[m, :, :kv_cols].astype(F32)
+        d_value[:, m * kv_cols : (m + 1) * kv_cols] = all_rest[m, :, kv_cols : 2 * kv_cols].astype(F32)
+    gains[...] = sum(all_rest[m, :, 2 * kv_cols :].astype(F32) for m in range(members))
     links.finish()
 
 
-BACKWARD_ORDER = "amoadmmadaaaoqoqoqaoaq"
-
-
-def backward_phase(members, own_experts, mixture, residual, grad_out_all, grad_residual, gain_ffn_part, tokens, down, row_gains, pack_all, normed_attn, qkv, kx, vx, probs, attended, cosine, sine):
+BACKWARD_ORDER = "oadoaoaoaooqaqqdoaqdaqqarorarradrraqrqdaoodaaqdrddrr"
+
+
+def backward_phase(members, own_experts, grad_out_all, grad_residual, gain_ffn_part, tokens, down, row_gains, pack_all, normed_attn, qkv, kx, vx, probs, attended, cosine, sine):
     rows, width = tokens.shape
     span, q_cols = attended.shape
     qkv_cols = qkv.shape[1]
     kv_cols = (qkv_cols - q_cols) // 2
     devices, own = down.shape[:2]
     line = [pltpu.VMEM((members, rows, width), BF16)] * 3
+    three = (q_cols, q_cols, 2 * kv_cols + LANES)
     return comm_call(
         backward_kernel, "backward", 4, members, 100, 32,
-        [ANY, VMEM, VMEM, VMEM, VMEM, VMEM, ANY] + [VMEM] * 10,
-        [VMEM] * 8,
+        [VMEM, VMEM, VMEM, VMEM, ANY] + [VMEM] * 10,
+        [VMEM] * 7,
         [
-            sds((rows, width), BF16),
             sds((rows, width), F32),
             sds((own, LANES), F32),
             sds((own, members * q_cols), F32),
@@ -973,23 +932,18 @@
         ],
         [
             *line,
-            *line,
             pltpu.VMEM((span, q_cols), BF16),
             pltpu.VMEM((2, 2, span, LANES), F32),
             pltpu.VMEM((2, 2, span, LANES), F32),
             pltpu.VMEM((span, qkv_cols), BF16),
             pltpu.VMEM((1, width), F32),
-            pltpu.VMEM((devices, own, q_cols), BF16),
-            pltpu.VMEM((devices, own, qkv_cols + LANES), BF16),
-            pltpu.VMEM((own, q_cols), BF16),
-            pltpu.VMEM((own, qkv_cols + LANES), BF16),
-            pltpu.VMEM((members, own, q_cols), BF16),
-            pltpu.VMEM((members, own, qkv_cols + LANES), BF16),
-            *plane_scratch(own, q_cols, False),
-            *plane_scratch(own, qkv_cols + LANES, False),
+            *[pltpu.VMEM((devices, own, cols), BF16) for cols in three],
+            *[pltpu.VMEM((own, cols), BF16) for cols in three],
+            *[pltpu.VMEM((members, own, cols), BF16) for cols in three],
+            *[one for cols in three for one in plane_scratch(own, cols, False)],
             *plane_scratch(*down.shape[1:]),
         ],
-    )(mixture, residual, grad_out_all, grad_residual, gain_ffn_part, tokens, down, row_gains, pack_all, normed_attn, qkv, kx, vx, probs, attended, cosine, sine)
+    )(grad_out_all, grad_residual, gain_ffn_part, tokens, down, row_gains, pack_all, normed_attn, qkv, kx, vx, probs, attended, cosine, sine)
 
 
 def all_blocks(x, axis):
@@ -1006,12 +960,12 @@
     )
 
 
-def line_sum(part):
+def line_total(part):
     return scatter(part.reshape(-1, part.shape[2]), "expert")
 
 
 def plain_second(members, part, tokens, gain, up, down):
-    residual = tokens.astype(F32) + branch_scale * line_sum(part)
+    residual = tokens.astype(F32) + branch_scale * line_total(part)
     normed = (residual * rms_factor(residual) * gain).astype(BF16)
     return residual, all_blocks(normed, "expert"), all_blocks(up, "dp"), all_blocks(down, "dp")
 
@@ -1021,7 +975,7 @@
 
 
 def plain_third(members, part, residual, cot, gain, gate, up):
-    grad = line_sum(part)
+    grad = line_total(part)
     factor = rms_factor(residual)
     gain_part = jnp.sum(grad * residual * factor, axis=0, keepdims=True)
     total = cot.astype(F32) + norm_back(residual, factor, gain, grad)
@@ -1031,7 +985,7 @@
 
 def plain_fourth(members, part, grad_residual, tokens, gain, pack, down):
     here = tokens.astype(F32)
-    grad_tokens = grad_residual + norm_back(here, rms_factor(here), gain, line_sum(part))
+    grad_tokens = grad_residual + norm_back(here, rms_factor(here), gain, line_total(part))
     return grad_tokens, all_blocks(plane_sum(pack).astype(BF16), "expert"), plane_sum(down)
 
 
@@ -1273,9 +1227,10 @@
     )
     by_kind = [one.reshape(devices, -1, own_experts * ff) for one in by_kind]
 
-    grad_residual, gain_two_part, grad_attn_out, sum_gate, sum_up = third_phase(
+    output, grad_residual, gain_two_part, grad_attn_out, sum_gate, sum_up = third_phase(
         members, own_experts,
         grad_normed.reshape(members, rows, width),
+        mixture.reshape(members, rows, width),
         residual,
         cotangent,
         gains,
@@ -1283,11 +1238,9 @@
         by_kind[1],
     )
     (
-        output, grad_tokens, grad_gains, d_query, d_key, d_value, d_out, d_down,
+        grad_tokens, grad_gains, d_query, d_key, d_value, d_out, d_down,
     ) = backward_phase(
         members, own_experts,
-        mixture.reshape(members, rows, width),
-        residual,
         grad_attn_out.reshape(span, width),
         grad_residual,
         gain_two_part,

time: 400 us -> 385 us (0.963)
  Pallas kernels: 368 us -> 355 us
    pallas_call x2, Pallas kernels: 192 us -> 178 us  [the longest x1 92.8 us: third_phase(): comm_call(third_kernel, 'phase_three', 3, members, 80, 16, [ANY, ANY, VME...]
    unnamed x30 -> x32, local copies, waits for them, and re-layouts: 16.2 us -> 15.2 us
where the time goes in v7:
time: 385 us
  Pallas kernels  355 us (92%)
  local copies, waits for them, and re-layouts  24.8 us (6%)
  other arithmetic  4.52 us (1%)
    pallas_call x1, Pallas kernels, forward_phase(): comm_call(forward_kernel, 'forward', 1, members, 120, 16, [VMEM, ANY, ANY...  134 us
    pallas_call x1, Pallas kernels, third_phase(): comm_call(third_kernel, 'phase_three', 3, members, 80, 16, [ANY, ANY, VME...  92.8 us
    pallas_call x1, Pallas kernels, backward_phase(): comm_call(backward_kernel, 'backward', 4, members, 100, 32, [VMEM, VMEM,...  85.6 us
    pallas_call x1, Pallas kernels, experts(): pl.pallas_call(functools.partial(expert_kernel, capacity, own_experts), g...  42.3 us
    unnamed x32, local copies, waits for them, and re-layouts  15.2 us

profile of v7, /device:TPU:0, one launch (start us, length us, event | category | flops | bytes accessed | tf_op | source)
XLA Modules:
  0.0 384.6 jit_solution(8010917822498436614)
XLA Ops:
  0.6 0.9 select_reduce_fusion.2
  1.5 0.1 select_reduce_fusion.1
  1.6 1.2 broadcast_in_dim.57.gain_attn
  2.8 1.2 broadcast_in_dim.58.gain_ffn
  4.1 0.1 select_reduce_fusion
  4.2 0.6 convert_element_type.36.segment
  4.8 0.7 convert_element_type.33
  5.5 0.7 pad_maximum_fusion
  6.2 0.7 copy.49.route
  6.9 2.0 fusion
  9.0 1.6 copy.46
  10.6 1.4 copy.50.gate
  11.9 0.0 copy-done.5
  11.9 0.0 copy-start.6
  11.9 0.6 copy.47
  12.5 1.4 copy.51.up
  13.9 0.0 copy-done.6
  13.9 0.6 copy.48
  14.5 1.4 copy.52.down
  15.8 133.8 %forward.1 = (bf16[4,160,1536]{2,1,0:T(8,128)(2,1)}, f32[4,160,16]{2,1,0:T(8,128)}, bf16[8,192,1152]{2,1,0:T(8,128)(2,1)}, bf16[8,192,2560]{2,1,0:T(8,128)(2,1)}...) custom-call(bf16[160,1536]{1,0:T(8,128)(2,1)} %tokens.3, ...), custom_call_target="tpu_custom_call" | custom-call | tf_op jit(solution)/shard_map/forward/pallas_call | solution.py:751
  149.6 42.3 %experts.1 = (bf16[640,1536]{1,0:T(8,128)(2,1)}, bf16[640,1536]{1,0:T(8,128)(2,1)}, bf16[1536,2560]{1,0:T(8,128)(2,1)}, bf16[1536,2560]{1,0:T(8,128)(2,1)}, bf16[1536,2560]{1,0:T(8,128)(2,1)}) custom-call(f32[640,16]{1,0:T(8,128)} %bitcast.37, bf16[640,1536]{1,0:T(8,128)(2,1)} %bitcast.34, bf16[640,1536]{1,0:T(8,128)(2,1)} %bitcast.33, ...), custom_call_target="tpu_custom_call" | custom-call | tf_op jit(solution)/shard_map/experts/pallas_call | solution.py:581
  191.9 92.8 %phase_three.1 = (bf16[160,1536]{1,0:T(8,128)(2,1)}, f32[160,1536]{1,0:T(8,128)}, f32[1,1536]{1,0:T(1,128)}, bf16[4,160,1536]{2,1,0:T(8,128)(2,1)}, f32[5,192,512]{2,1,0:T(8,128)}, /*index=5*/f32[5,192,512]{2,1,0:T(8,128)}) custom-call(bf16[4,160,1536]{2,1,0:T(8,128)(2,1)} %bitcast.36, bf16[4,160,1536]{2,1,0:T(8,128)(2,1)} %bitcast.35, ...), custom_call_target="tpu_custom_call" | custom-call | tf_op jit(solution)/shard_map/phase_three/pallas_call | solution.py:472
  284.7 0.0 copy-start.7
  284.7 85.6 %backward.1 = (f32[160,1536]{1,0:T(8,128)}, f32[192,128]{1,0:T(8,128)}, f32[192,1536]{1,0:T(8,128)}, f32[192,512]{1,0:T(8,128)}, f32[192,512]{1,0:T(8,128)}, /*i...) custom-call(bf16[640,1536]{1,0:T(8,128)(2,1)} %bitcast.32, f32[160,1536]{1,0:T(8,128)} %get-tuple-element.58.grad_residual, ...), custom_call_target="tpu_custom_call" | custom-call | tf_op jit(solution)/shard_map/backward/pallas_call | solution.py:920
  370.4 0.0 copy-start.4
  370.4 1.8 slice_reduce_fusion
  372.2 0.0 copy-done.7
  372.2 0.8 copy.62
  373.0 0.0 copy-start.9
  373.0 2.3 copy.63
  375.2 0.0 copy-done.4
  375.2 0.0 copy-start.8
  375.2 0.0 copy-start.3
  375.3 1.0 copy.64
  376.3 0.0 copy-done.9
  376.3 0.0 copy-start.1
  376.3 0.7 copy.65
  377.0 0.0 copy-done.8
  377.0 0.7 copy.66
  377.8 0.0 copy-done.3
  377.8 1.0 copy.67
  378.8 0.0 copy-done.1
  378.8 0.0 copy-start
  378.8 1.3 copy.68
  380.1 1.0 copy-done
  381.0 1.3 copy.69
  382.3 1.0 copy-done.2
  383.3 1.3 copy.70
  (5 shorter events, 0.0 us)
Async XLA Ops:
  9.0 3.0 copy-start.5
  11.9 1.9 copy-start.6
  284.7 87.5 %copy-start.7 = (bf16[160,1536]{1,0:T(8,128)(2,1)S(1)}, bf16[160,1536]{1,0:T(8,128)(2,1)}, u32[]{:S(2)}) copy-start(bf16[160,1536]{1,0:T(8,128)(2,1)} %get-tuple-element.96) | copy-start | bytes 1474564
  370.4 4.9 %copy-start.4 = (f32[192,1536]{1,0:T(8,128)S(1)}, f32[192,1536]{1,0:T(8,128)}, u32[]{:S(2)}) copy-start(f32[192,1536]{1,0:T(8,128)} %get-tuple-element.100) | copy-start | bytes 3538948
  373.0 3.3 copy-start.9
  375.2 1.8 copy-start.8
  375.2 2.5 copy-start.3
  376.3 2.5 copy-start.1
  378.8 2.3 copy-start
  381.0 2.3 copy-start.2

commit v8 on v7

--- a/solution.py
+++ b/solution.py
@@ -622,7 +622,7 @@
         col = lax.broadcasted_iota(jnp.int32, (LANES, span), 1)
         here = segment[:, b * LANES : (b + 1) * LANES]
         here = jnp.sum(jnp.where(same, here, 0.0), axis=1, keepdims=True)
-        ok = (here == segment[...]) & (col <= row)
+        ok = (here == segment) & (col <= row)
         bias[at] = jnp.where(ok, 0.0, -1e30)
 
 
@@ -657,12 +657,18 @@
 
 
 def forward_kernel(
-    members, tokens, cot, route, w_query, w_key, w_value, w_out, gain_attn, gain_ffn, gate, up, down, segment, cosine, sine,
+    members, tokens, cot, ids, gates, w_query, w_key, w_value, w_out, small, gate, up, down, cosine, sine,
     cot_all, route_all, pack_all, gate_all, up_all, down_all, normed_attn, qkv, kx, vx, probs, attended, residual, normed_all, gains,
-    send, recv, local, pack, tokens_all, bias, acc, from_left, from_right, normed,
+    send, recv, local, pack, route, flat, tokens_all, bias, acc, from_left, from_right, normed,
 ):
     links = Links(send, recv, local, members)
+    count, _, cols = gate.shape
+    loads = [
+        [links.move(weight.at[e], flat.at[i, :, e * cols : (e + 1) * cols]) for e in range(count)]
+        for i, weight in enumerate((gate, up, down))
+    ]
     links.greet()
+    route[...] = jnp.concatenate([ids[...].astype(F32), gates[...]], axis=0).T
     rows, width = tokens.shape
     span = rows * members
     q_cols = attended.shape[1]
@@ -676,17 +682,23 @@
             loads.append(links.move(weight.at[:, mine], pack.at[:, at : at + cols]))
             at += cols
         which = lax.broadcasted_iota(jnp.int32, (16, pack.shape[0]), 0)
-        both = jnp.where(which == 0, gain_attn[...].astype(F32), jnp.where(which == 1, gain_ffn[...].astype(F32), 0.0))
+        own = pack.shape[0]
+        both = jnp.where(which == 0, small[1:2, :own], jnp.where(which == 1, small[2:3, :own], 0.0))
         pack[:, at:] = mm_tn(both.astype(BF16), first_lanes()).astype(BF16)
         for load in loads:
             load.wait()
         yield from plane_gather(links, pack, pack_all)
 
+    def expert_chain(i, full):
+        for load in loads[i]:
+            load.wait()
+        yield from plane_gather(links, flat.at[i], full)
+
     def produce(o):
         acc[o] = mm_nt(attended[o * rows : (o + 1) * rows], weight_columns(pack_all, qkv_cols, q_cols)).astype(BF16)
 
     def chain():
-        attention_setup(segment, bias)
+        attention_setup(small[0:1], bias)
         yield
         gains[...] = gain_rows(pack_all, qkv_cols + q_cols)
 
@@ -729,9 +741,9 @@
         r=line_gather(links, route, route_all),
         c=line_gather(links, cot, cot_all),
         p=pack_chain(),
-        g=plane_gather(links, gate, gate_all),
-        u=plane_gather(links, up, up_all),
-        d=plane_gather(links, down, down_all),
+        g=expert_chain(0, gate_all),
+        u=expert_chain(1, up_all),
+        d=expert_chain(2, down_all),
         a=chain(),
     )
     links.finish()
@@ -740,25 +752,27 @@
 FORWARD_ORDER = "tptpdptpcaptgaaacdtrgatcaardaagdattpuparparadrpaarrd"
 
 
-def forward_phase(members, tokens, cot, route, w_query, w_key, w_value, w_out, gain_attn, gain_ffn, gate, up, down, segment, cosine, sine):
+def forward_phase(members, tokens, cot, ids, gates, w_query, w_key, w_value, w_out, small, gate, up, down, cosine, sine):
     rows, width = tokens.shape
     q_cols = w_query.shape[1] // members
     qkv_cols = q_cols + 2 * w_key.shape[1] // members
-    pack = (w_query.shape[0], qkv_cols + q_cols + LANES)
+    count, own, cols = gate.shape
+    pack = (own, qkv_cols + q_cols + LANES)
+    route, flat = (rows, 2 * ids.shape[0]), (own, count * cols)
     span = rows * members
     blocks = pltpu.VMEM((members, rows, width), BF16)
     heads = q_cols // HEAD_SIZE
     return comm_call(
-        forward_kernel, "forward", 1, members, 120, 16,
-        [VMEM, ANY, ANY, ANY, ANY, ANY, ANY, VMEM, VMEM, ANY, ANY, ANY, VMEM, VMEM, VMEM],
+        forward_kernel, "forward", 1, members, 120, 40,
+        [VMEM, ANY, VMEM, VMEM, ANY, ANY, ANY, ANY, VMEM, ANY, ANY, ANY, VMEM, VMEM],
         [ANY, ANY, VMEM, ANY, ANY, ANY, VMEM, VMEM, VMEM, VMEM, VMEM, VMEM, VMEM, ANY, VMEM],
         [
             sds((members, rows, width), BF16),
-            sds((members, *route.shape), F32),
+            sds((members, *route), F32),
             sds((8, *pack), BF16),
-            sds((8, *gate.shape), BF16),
-            sds((8, *up.shape), BF16),
-            sds((8, *down.shape), BF16),
+            sds((8, *flat), BF16),
+            sds((8, *flat), BF16),
+            sds((8, *flat), BF16),
             sds((span, width), BF16),
             sds((span, qkv_cols), BF16),
             sds((2, 2, span, LANES), BF16),
@@ -771,6 +785,8 @@
         ],
         [
             pltpu.VMEM(pack, BF16),
+            pltpu.VMEM(route, F32),
+            pltpu.VMEM((3, *flat), BF16),
             blocks,
             pltpu.VMEM((span, span), F32),
             blocks,
@@ -778,7 +794,7 @@
             blocks,
             pltpu.VMEM((rows, width), BF16),
         ],
-    )(tokens, cot, route, w_query, w_key, w_value, w_out, gain_attn, gain_ffn, gate, up, down, segment, cosine, sine)
+    )(tokens, cot, ids, gates, w_query, w_key, w_value, w_out, small, gate, up, down, cosine, sine)
 
 
 def attend_back_steps(qkv, kx, vx, probs, grad_attended, cosine, sine, grad_k, grad_v, grad_qkv):
@@ -1200,23 +1216,22 @@
     span = rows * members
     own_experts, ff = expert_gate.shape[1], expert_gate.shape[2]
     capacity = rows * TOP // own_experts
-    route = jnp.concatenate([expert_ids.astype(F32), gates], axis=1)
     segment, position = layout(lengths[0], order[0], span)
     lane = jnp.arange(LANES, dtype=jnp.int32) % HEAD_SIZE
     half = HEAD_SIZE // 2
     frequency = rope_base ** (-((lane % half).astype(F32) * (2.0 / HEAD_SIZE)))
     angles = position[:, None] * frequency[None, :]
     cosine, sine = jnp.cos(angles), jnp.where(lane < half, -1.0, 1.0) * jnp.sin(angles)
+    spare = (0, span - gain_attn.shape[0])
+    small = jnp.stack(
+        [segment.astype(F32), jnp.pad(gain_attn.astype(F32), spare), jnp.pad(gain_ffn.astype(F32), spare)]
+    )
     (
         cot_all, route_all, pack_all, gate_all, up_all, down_all,
         normed_attn, qkv, kx, vx, probs, attended, residual, normed_all, gains,
     ) = forward_phase(
-        members, tokens, cotangent, route, w_query, key_weight, value_weight, w_out,
-        gain_attn[None], gain_ffn[None],
-        expert_gate.reshape(-1, own_experts * ff),
-        expert_up.reshape(-1, own_experts * ff),
-        expert_down.reshape(-1, own_experts * ff),
-        segment.astype(F32)[None], cosine, sine,
+        members, tokens, cotangent, expert_ids.T, gates.T, w_query, key_weight, value_weight, w_out,
+        small, *(w.transpose(1, 0, 2) for w in (expert_gate, expert_up, expert_down)), cosine, sine,
     )
     cot_all = cot_all.reshape(span, width)
     normed_all = normed_all.reshape(span, width)

time: 385 us -> 373 us (0.969)
  local copies, waits for them, and re-layouts: 24.8 us -> 14.2 us
    reshape x3 -> x0, local copies, waits for them, and re-layouts: 4.05 us -> none  [the longest x1 1.35 us: shards_fast(): expert_up.reshape(-1, own_experts * ff)]
    unnamed x32 -> x25, local copies, waits for them, and re-layouts: 15.2 us -> 12.4 us
where the time goes in v8:
time: 373 us
  Pallas kernels  353 us (95%)
  local copies, waits for them, and re-layouts  14.2 us (4%)
  other arithmetic  5.06 us (1%)
    pallas_call x1, Pallas kernels, forward_phase(): comm_call(forward_kernel, 'forward', 1, members, 120, 40, [VMEM, ANY, VME...  132 us
    pallas_call x1, Pallas kernels, third_phase(): comm_call(third_kernel, 'phase_three', 3, members, 80, 16, [ANY, ANY, VME...  93.5 us
    pallas_call x1, Pallas kernels, backward_phase(): comm_call(backward_kernel, 'backward', 4, members, 100, 32, [VMEM, VMEM,...  85.8 us
    pallas_call x1, Pallas kernels, experts(): pl.pallas_call(functools.partial(expert_kernel, capacity, own_experts), g...  42.2 us
    unnamed x25, local copies, waits for them, and re-layouts  12.4 us

profile of v8, /device:TPU:0, one launch (start us, length us, event | category | flops | bytes accessed | tf_op | source)
XLA Modules:
  0.0 373.1 jit_solution(9072884137283185505)
XLA Ops:
  0.6 0.9 select_reduce_fusion.2
  1.5 0.1 select_reduce_fusion.1
  1.6 0.7 pad_convert_fusion.1
  2.3 0.7 pad_convert_fusion
  3.0 0.1 select_reduce_fusion
  3.1 0.6 pad_maximum_fusion.small
  3.7 2.0 fusion
  5.7 131.5 %forward.1 = (bf16[4,160,1536]{2,1,0:T(8,128)(2,1)}, f32[4,160,16]{2,1,0:T(8,128)}, bf16[8,192,1152]{2,1,0:T(8,128)(2,1)}, bf16[8,192,2560]{2,1,0:T(8,128)(2,1)}...) custom-call(bf16[160,1536]{1,0:T(8,128)(2,1)} %tokens.3, ...), custom_call_target="tpu_custom_call" | custom-call | tf_op jit(solution)/shard_map/forward/pallas_call | solution.py:765
  137.3 42.2 %experts.1 = (bf16[640,1536]{1,0:T(8,128)(2,1)}, bf16[640,1536]{1,0:T(8,128)(2,1)}, bf16[1536,2560]{1,0:T(8,128)(2,1)}, bf16[1536,2560]{1,0:T(8,128)(2,1)}, bf16[1536,2560]{1,0:T(8,128)(2,1)}) custom-call(f32[640,16]{1,0:T(8,128)} %bitcast.39, bf16[640,1536]{1,0:T(8,128)(2,1)} %bitcast.33, bf16[640,1536]{1,0:T(8,128)(2,1)} %bitcast.32, ...), custom_call_target="tpu_custom_call" | custom-call | tf_op jit(solution)/shard_map/experts/pallas_call | solution.py:581
  179.5 93.5 %phase_three.1 = (bf16[160,1536]{1,0:T(8,128)(2,1)}, f32[160,1536]{1,0:T(8,128)}, f32[1,1536]{1,0:T(1,128)}, bf16[4,160,1536]{2,1,0:T(8,128)(2,1)}, f32[5,192,512]{2,1,0:T(8,128)}, /*index=5*/f32[5,192,512]{2,1,0:T(8,128)}) custom-call(bf16[4,160,1536]{2,1,0:T(8,128)(2,1)} %bitcast.35, bf16[4,160,1536]{2,1,0:T(8,128)(2,1)} %bitcast.34, ...), custom_call_target="tpu_custom_call" | custom-call | tf_op jit(solution)/shard_map/phase_three/pallas_call | solution.py:472
  273.0 0.0 copy-start.5
  273.0 85.8 %backward.1 = (f32[160,1536]{1,0:T(8,128)}, f32[192,128]{1,0:T(8,128)}, f32[192,1536]{1,0:T(8,128)}, f32[192,512]{1,0:T(8,128)}, f32[192,512]{1,0:T(8,128)}, /*i...) custom-call(bf16[640,1536]{1,0:T(8,128)(2,1)} %bitcast.31, f32[160,1536]{1,0:T(8,128)} %get-tuple-element.58.grad_residual, ...), custom_call_target="tpu_custom_call" | custom-call | tf_op jit(solution)/shard_map/backward/pallas_call | solution.py:936
  358.9 0.0 copy-start.4
  358.9 1.8 slice_reduce_fusion
  360.7 0.0 copy-done.5
  360.7 0.8 copy.35
  361.5 0.0 copy-start.7
  361.5 2.3 copy.36
  363.8 0.0 copy-done.4
  363.8 0.0 copy-start.6
  363.8 0.0 copy-start.3
  363.8 1.0 copy.37
  364.8 0.0 copy-done.7
  364.8 0.0 copy-start.1
  364.8 0.7 copy.38
  365.5 0.0 copy-done.6
  365.5 0.7 copy.39
  366.3 0.0 copy-done.3
  366.3 1.0 copy.40
  367.3 0.0 copy-done.1
  367.3 0.0 copy-start
  367.3 1.3 copy.41
  368.6 1.0 copy-done
  369.5 0.0 copy-start.2
  369.6 1.3 copy.42
  370.8 1.0 copy-done.2
  371.8 1.3 copy.43
  (6 shorter events, 0.0 us)
Async XLA Ops:
  273.0 87.7 %copy-start.5 = (bf16[160,1536]{1,0:T(8,128)(2,1)S(1)}, bf16[160,1536]{1,0:T(8,128)(2,1)}, u32[]{:S(2)}) copy-start(bf16[160,1536]{1,0:T(8,128)(2,1)} %get-tuple-element.96) | copy-start | bytes 1474564
  358.9 4.9 %copy-start.4 = (f32[192,1536]{1,0:T(8,128)S(1)}, f32[192,1536]{1,0:T(8,128)}, u32[]{:S(2)}) copy-start(f32[192,1536]{1,0:T(8,128)} %get-tuple-element.100) | copy-start | bytes 3538948
  361.5 3.3 copy-start.7
  363.8 1.8 copy-start.6
  363.8 2.5 copy-start.3
  364.8 2.5 copy-start.1
  367.3 2.3 copy-start
  369.5 2.3 copy-start.2

commit v9 on v8

--- a/solution.py
+++ b/solution.py
@@ -383,6 +383,12 @@
                 out[e, at] = total[:, e * cols : (e + 1) * cols]
 
 
+def plane_total(links, part, scratch, total, out, stores):
+    yield from plane_scatter(links, part, *scratch)
+    plane_result(scratch[0].at[0], scratch[1], scratch[4], scratch[5], total)
+    stores.append(links.move(total, out))
+
+
 def line_result(z, acc, from_left, from_right, at):
     return (
         acc[z, at].astype(F32) + from_left[z, at].astype(F32) + from_right[z, at].astype(F32)
@@ -416,10 +422,11 @@
     return jax.ShapeDtypeStruct(shape, dtype)
 
 
-def third_kernel(members, part, mixture, residual, cot, gain, gate, up, output, grad_residual, gain_part, out_all, gate_out, up_out, send, recv, local, acc, from_left, from_right, acc_m, left_m, right_m, grad_out, *rest):
+def third_kernel(members, part, mixture, residual, cot, gain, gate, up, output, grad_residual, gain_part, out_all, gate_out, up_out, send, recv, local, acc, from_left, from_right, acc_m, left_m, right_m, grad_out, gate_sum, up_sum, *rest):
     links = Links(send, recv, local, members)
     links.greet()
     for_gate, for_up = rest[:6], rest[6:]
+    stores = []
 
     def finish(first, count):
         @pl.loop(0, count // 16)
@@ -455,11 +462,11 @@
         THIRD_ORDER,
         m=mixture_chain(),
         z=chain(),
-        g=plane_scatter(links, gate, *for_gate),
-        u=plane_scatter(links, up, *for_up),
-    )
-    plane_result(for_gate[0].at[0], for_gate[1], for_gate[4], for_gate[5], gate_out)
-    plane_result(for_up[0].at[0], for_up[1], for_up[4], for_up[5], up_out)
+        g=plane_total(links, gate, for_gate, gate_sum, gate_out, stores),
+        u=plane_total(links, up, for_up, up_sum, up_out, stores),
+    )
+    for store in stores:
+        store.wait()
     links.finish()
 
 
@@ -470,8 +477,8 @@
     rows, width = cot.shape
     blocks = pltpu.VMEM((members, rows, width), BF16)
     return comm_call(
-        third_kernel, "phase_three", 3, members, 80, 16,
-        [ANY, ANY, VMEM, VMEM, VMEM, ANY, ANY], [VMEM, VMEM, VMEM, ANY, VMEM, VMEM],
+        third_kernel, "phase_three", 3, members, 80, 24,
+        [ANY, ANY, VMEM, VMEM, VMEM, ANY, ANY], [VMEM, VMEM, VMEM, ANY, ANY, ANY],
         [
             sds((rows, width), BF16),
             sds((rows, width), F32),
@@ -482,6 +489,7 @@
         ],
         [blocks] * 6
         + [pltpu.VMEM((rows, width), BF16)]
+        + [pltpu.VMEM((own_experts, gate.shape[1], gate.shape[2] // own_experts), F32)] * 2
         + plane_scratch(*gate.shape[1:])
         + plane_scratch(*up.shape[1:]),
     )(part, mixture, residual, cot, gain, gate, up)
@@ -658,10 +666,12 @@
 
 def forward_kernel(
     members, tokens, cot, ids, gates, w_query, w_key, w_value, w_out, small, gate, up, down, cosine, sine,
-    cot_all, route_all, pack_all, gate_all, up_all, down_all, normed_attn, qkv, kx, vx, probs, attended, residual, normed_all, gains,
+    cot_all, route_all, pack_out, gate_all, up_all, down_all, normed_out, qkv_out, kx_out, vx_out, probs_out, attended_out, residual, normed_all, gains,
     send, recv, local, pack, route, flat, tokens_all, bias, acc, from_left, from_right, normed,
+    pack_all, normed_attn, qkv, kx, vx, probs, attended,
 ):
     links = Links(send, recv, local, members)
+    stores = []
     count, _, cols = gate.shape
     loads = [
         [links.move(weight.at[e], flat.at[i, :, e * cols : (e + 1) * cols]) for e in range(count)]
@@ -724,6 +734,11 @@
 
         yield
         yield from attend_steps(qkv, kx, vx, bias, probs, attended)
+        for kept, out in (
+            (pack_all, pack_out), (normed_attn, normed_out), (qkv, qkv_out), (kx, kx_out),
+            (vx, vx_out), (probs, probs_out), (attended, attended_out),
+        ):
+            stores.append(links.move(kept, out))
 
         def finish(first, count):
             @pl.loop(0, count // 16)
@@ -746,6 +761,8 @@
         d=expert_chain(2, down_all),
         a=chain(),
     )
+    for store in stores:
+        store.wait()
     links.finish()
 
 
@@ -765,7 +782,7 @@
     return comm_call(
         forward_kernel, "forward", 1, members, 120, 40,
         [VMEM, ANY, VMEM, VMEM, ANY, ANY, ANY, ANY, VMEM, ANY, ANY, ANY, VMEM, VMEM],
-        [ANY, ANY, VMEM, ANY, ANY, ANY, VMEM, VMEM, VMEM, VMEM, VMEM, VMEM, VMEM, ANY, VMEM],
+        [ANY] * 12 + [VMEM, ANY, VMEM],
         [
             sds((members, rows, width), BF16),
             sds((members, *route), F32),
@@ -793,6 +810,13 @@
             blocks,
             blocks,
             pltpu.VMEM((rows, width), BF16),
+            pltpu.VMEM((8, *pack), BF16),
+            pltpu.VMEM((span, width), BF16),
+            pltpu.VMEM((span, qkv_cols), BF16),
+            pltpu.VMEM((2, 2, span, LANES), BF16),
+            pltpu.VMEM((2, 2, span, LANES), BF16),
+            pltpu.VMEM((heads, span, span), BF16),
+            pltpu.VMEM((span, q_cols), BF16),
         ],
     )(tokens, cot, ids, gates, w_query, w_key, w_value, w_out, small, gate, up, down, cosine, sine)
 
@@ -837,12 +861,30 @@
 
 
 def backward_kernel(
-    members, grad_out_all, grad_residual, gain_ffn_part, tokens, down, row_gains, pack_all, normed_attn, qkv, kx, vx, probs, attended, cosine, sine,
-    grad_tokens, gains, d_query, d_key, d_value, d_out, d_down,
+    members, grad_out_in, grad_residual, gain_ffn_part, tokens, down, row_gains, pack_in, normed_in, qkv_in, kx_in, vx_in, probs_in, attended_in, cosine, sine,
+    grad_tokens, gains, d_query, d_key, d_value, d_out, down_out,
     send, recv, local, acc, from_left, from_right, grad_attended, grad_k, grad_v, grad_qkv, gain_part,
-    for_w_out, for_w_query, for_rest, own_out, own_query, own_rest, all_out, all_query, all_rest, *rest,
+    for_w_out, for_w_query, for_rest, own_out, own_query, own_rest, all_out, all_query, all_rest,
+    grad_out_all, pack_all, normed_attn, qkv, kx, vx, probs, attended, d_down, *rest,
 ):
     links = Links(send, recv, local, members)
+    loads = {
+        "attended": links.move(attended_in, attended),
+        "grad": links.move(grad_out_in, grad_out_all),
+        "pack": links.move(pack_in, pack_all),
+        "qkv": links.move(qkv_in, qkv),
+        "kx": links.move(kx_in, kx),
+        "vx": links.move(vx_in, vx),
+        "probs": links.move(probs_in, probs),
+        "normed": links.move(normed_in, normed_attn),
+    }
+    stores = []
+
+    def need(*names):
+        for name in names:
+            if name in loads:
+                loads.pop(name).wait()
+
     links.greet()
     rows, width = tokens.shape
     q_cols, qkv_cols = attended.shape[1], qkv.shape[1]
@@ -856,16 +898,33 @@
             term = mm_tn(rows_of[:, i * step : (i + 1) * step], grads)
             out[2 * i : 2 * i + 2, :, :cols] = term.astype(BF16).reshape(2, step // 2, cols)
 
-    def weight_chain(fill, part, mine, full, scratch):
+    def put_out():
+        for m in range(members):
+            d_out[:, m * q_cols : (m + 1) * q_cols] = all_out[m].astype(F32)
+
+    def put_query():
+        for m in range(members):
+            d_query[:, m * q_cols : (m + 1) * q_cols] = all_query[m].astype(F32)
+
+    def put_rest():
+        for m in range(members):
+            d_key[:, m * kv_cols : (m + 1) * kv_cols] = all_rest[m, :, :kv_cols].astype(F32)
+            d_value[:, m * kv_cols : (m + 1) * kv_cols] = all_rest[m, :, kv_cols : 2 * kv_cols].astype(F32)
+        gains[...] = sum(all_rest[m, :, 2 * kv_cols :].astype(F32) for m in range(members))
+
+    def weight_chain(fill, part, mine, full, scratch, put):
         fill()
         yield from plane_scatter(links, part, None, *scratch)
         plane_result(part.at[links.d], scratch[0], scratch[3], scratch[4], mine)
         yield from line_gather(links, mine, full)
+        put()
 
     def fill_out():
+        need("grad", "attended")
         weight_term(grad_out_all, attended[...], for_w_out, q_cols)
 
     def fill_query():
+        need("normed")
         weight_term(normed_attn, grad_qkv[:, :q_cols], for_w_query, q_cols)
 
     def fill_rest():
@@ -882,6 +941,7 @@
         acc[o] = part.astype(BF16)
 
     def chain():
+        need("grad", "pack")
         wo = weight_columns(pack_all, qkv_cols, q_cols)
 
         @pl.loop(0, grad_attended.shape[0] // LANES)
@@ -890,8 +950,10 @@
             grad_attended[at] = mm(grad_out_all[at], wo).astype(BF16)
 
         yield
+        need("qkv", "kx", "vx", "probs")
         yield from attend_back_steps(qkv, kx, vx, probs, grad_attended, cosine, sine, grad_k, grad_v, grad_qkv)
         gain_part[...] = jnp.zeros(gain_part.shape, F32)
+        need("normed")
         yield
 
         def finish(first, count):
@@ -906,19 +968,14 @@
 
     run(
         BACKWARD_ORDER,
-        d=plane_scatter(links, down, *with_down),
-        o=weight_chain(fill_out, for_w_out, own_out, all_out, with_out),
+        d=plane_total(links, down, with_down, d_down, down_out, stores),
+        o=weight_chain(fill_out, for_w_out, own_out, all_out, with_out, put_out),
         a=chain(),
-        q=weight_chain(fill_query, for_w_query, own_query, all_query, with_query),
-        r=weight_chain(fill_rest, for_rest, own_rest, all_rest, with_rest),
-    )
-    plane_result(with_down[0].at[0], with_down[1], with_down[4], with_down[5], d_down)
-    for m in range(members):
-        d_out[:, m * q_cols : (m + 1) * q_cols] = all_out[m].astype(F32)
-        d_query[:, m * q_cols : (m + 1) * q_cols] = all_query[m].astype(F32)
-        d_key[:, m * kv_cols : (m + 1) * kv_cols] = all_rest[m, :, :kv_cols].astype(F32)
-        d_value[:, m * kv_cols : (m + 1) * kv_cols] = all_rest[m, :, kv_cols : 2 * kv_cols].astype(F32)
-    gains[...] = sum(all_rest[m, :, 2 * kv_cols :].astype(F32) for m in range(members))
+        q=weight_chain(fill_query, for_w_query, own_query, all_query, with_query, put_query),
+        r=weight_chain(fill_rest, for_rest, own_rest, all_rest, with_rest, put_rest),
+    )
+    for store in stores:
+        store.wait()
     links.finish()
 
 
@@ -935,8 +992,8 @@
     three = (q_cols, q_cols, 2 * kv_cols + LANES)
     return comm_call(
         backward_kernel, "backward", 4, members, 100, 32,
-        [VMEM, VMEM, VMEM, VMEM, ANY] + [VMEM] * 10,
-        [VMEM] * 7,
+        [ANY, VMEM, VMEM, VMEM, ANY, VMEM] + [ANY] * 7 + [VMEM] * 2,
+        [VMEM] * 6 + [ANY],
         [
             sds((rows, width), F32),
             sds((own, LANES), F32),
@@ -956,6 +1013,8 @@
             *[pltpu.VMEM((devices, own, cols), BF16) for cols in three],
             *[pltpu.VMEM((own, cols), BF16) for cols in three],
             *[pltpu.VMEM((members, own, cols), BF16) for cols in three],
+            *[pltpu.VMEM(a.shape, BF16) for a in (grad_out_all, pack_all, normed_attn, qkv, kx, vx, probs, attended)],
+            pltpu.VMEM((own_experts, own, down.shape[2] // own_experts), F32),
             *[one for cols in three for one in plane_scratch(own, cols, False)],
             *plane_scratch(*down.shape[1:]),
         ],

time: 373 us -> 362 us (0.971)
  Pallas kernels: 353 us -> 342 us
    pallas_call x2, Pallas kernels: 179 us -> 173 us  [the longest x1 91.9 us: third_phase(): comm_call(third_kernel, 'phase_three', 3, members, 80, 24, [ANY, ANY, VME...]
    pallas_call x1, Pallas kernels: 132 us -> 127 us  [forward_phase(): comm_call(forward_kernel, 'forward', 1, members, 120, 40, [VMEM, ANY, VME...]
where the time goes in v9:
time: 362 us
  Pallas kernels  342 us (94%)
  local copies, waits for them, and re-layouts  14.2 us (4%)
  other arithmetic  5.06 us (1%)
    pallas_call x1, Pallas kernels, forward_phase(): comm_call(forward_kernel, 'forward', 1, members, 120, 40, [VMEM, ANY, VME...  127 us
    pallas_call x1, Pallas kernels, third_phase(): comm_call(third_kernel, 'phase_three', 3, members, 80, 24, [ANY, ANY, VME...  91.9 us
    pallas_call x1, Pallas kernels, backward_phase(): comm_call(backward_kernel, 'backward', 4, members, 100, 32, [ANY, VMEM, V...  80.6 us
    pallas_call x1, Pallas kernels, experts(): pl.pallas_call(functools.partial(expert_kernel, capacity, own_experts), g...  42.1 us
    unnamed x25, local copies, waits for them, and re-layouts  12.4 us

profile of v9, /device:TPU:0, one launch (start us, length us, event | category | flops | bytes accessed | tf_op | source)
XLA Modules:
  0.0 361.8 jit_solution(4334934021295085183)
XLA Ops:
  0.6 0.9 select_reduce_fusion.2
  1.5 0.1 select_reduce_fusion.1
  1.6 0.7 pad_convert_fusion.1
  2.3 0.7 pad_convert_fusion
  3.0 0.1 select_reduce_fusion
  3.1 0.6 pad_maximum_fusion.small
  3.7 2.0 fusion
  5.7 127.3 %forward.1 = (bf16[4,160,1536]{2,1,0:T(8,128)(2,1)}, f32[4,160,16]{2,1,0:T(8,128)}, bf16[8,192,1152]{2,1,0:T(8,128)(2,1)}, bf16[8,192,2560]{2,1,0:T(8,128)(2,1)}...) custom-call(bf16[160,1536]{1,0:T(8,128)(2,1)} %tokens.3, ...), custom_call_target="tpu_custom_call" | custom-call | tf_op jit(solution)/shard_map/forward/pallas_call | solution.py:782
  133.0 42.1 %experts.1 = (bf16[640,1536]{1,0:T(8,128)(2,1)}, bf16[640,1536]{1,0:T(8,128)(2,1)}, bf16[1536,2560]{1,0:T(8,128)(2,1)}, bf16[1536,2560]{1,0:T(8,128)(2,1)}, bf16[1536,2560]{1,0:T(8,128)(2,1)}) custom-call(f32[640,16]{1,0:T(8,128)} %bitcast.39, bf16[640,1536]{1,0:T(8,128)(2,1)} %bitcast.33, bf16[640,1536]{1,0:T(8,128)(2,1)} %bitcast.32, ...), custom_call_target="tpu_custom_call" | custom-call | tf_op jit(solution)/shard_map/experts/pallas_call | solution.py:589
  175.1 91.9 %phase_three.1 = (bf16[160,1536]{1,0:T(8,128)(2,1)}, f32[160,1536]{1,0:T(8,128)}, f32[1,1536]{1,0:T(1,128)}, bf16[4,160,1536]{2,1,0:T(8,128)(2,1)}, f32[5,192,512]{2,1,0:T(8,128)}, /*index=5*/f32[5,192,512]{2,1,0:T(8,128)}) custom-call(bf16[4,160,1536]{2,1,0:T(8,128)(2,1)} %bitcast.35, bf16[4,160,1536]{2,1,0:T(8,128)(2,1)} %bitcast.34, ...), custom_call_target="tpu_custom_call" | custom-call | tf_op jit(solution)/shard_map/phase_three/pallas_call | solution.py:479
  267.0 0.0 copy-start.5
  267.0 80.6 %backward.1 = (f32[160,1536]{1,0:T(8,128)}, f32[192,128]{1,0:T(8,128)}, f32[192,1536]{1,0:T(8,128)}, f32[192,512]{1,0:T(8,128)}, f32[192,512]{1,0:T(8,128)}, /*i...) custom-call(bf16[640,1536]{1,0:T(8,128)(2,1)} %bitcast.31, f32[160,1536]{1,0:T(8,128)} %get-tuple-element.58.grad_residual, ...), custom_call_target="tpu_custom_call" | custom-call | tf_op jit(solution)/shard_map/backward/pallas_call | solution.py:993
  347.6 0.0 copy-start.4
  347.6 1.8 slice_reduce_fusion
  349.5 0.0 copy-done.5
  349.5 0.8 copy.35
  350.2 0.0 copy-start.7
  350.2 2.3 copy.36
  352.5 0.0 copy-done.4
  352.5 0.0 copy-start.6
  352.5 0.0 copy-start.3
  352.5 1.0 copy.37
  353.5 0.0 copy-done.7
  353.5 0.0 copy-start.1
  353.5 0.7 copy.38
  354.3 0.0 copy-done.6
  354.3 0.7 copy.39
  355.0 0.0 copy-done.3
  355.0 1.0 copy.40
  356.0 0.0 copy-done.1
  356.0 0.0 copy-start
  356.0 1.3 copy.41
  357.3 1.0 copy-done
  358.3 0.0 copy-start.2
  358.3 1.3 copy.42
  359.6 1.0 copy-done.2
  360.6 1.3 copy.43
  (6 shorter events, 0.0 us)
Async XLA Ops:
  267.0 82.4 %copy-start.5 = (bf16[160,1536]{1,0:T(8,128)(2,1)S(1)}, bf16[160,1536]{1,0:T(8,128)(2,1)}, u32[]{:S(2)}) copy-start(bf16[160,1536]{1,0:T(8,128)(2,1)} %get-tuple-element.96) | copy-start | bytes 1474564
  347.6 4.9 %copy-start.4 = (f32[192,1536]{1,0:T(8,128)S(1)}, f32[192,1536]{1,0:T(8,128)}, u32[]{:S(2)}) copy-start(f32[192,1536]{1,0:T(8,128)} %get-tuple-element.100) | copy-start | bytes 3538948
  350.2 3.3 copy-start.7
  352.5 1.8 copy-start.6
  352.5 2.5 copy-start.3
  353.5 2.5 copy-start.1
  356.0 2.3 copy-start
  358.3 2.3 copy-start.2

commit v10 on v9

--- a/solution.py
+++ b/solution.py
@@ -424,9 +424,15 @@
 
 def third_kernel(members, part, mixture, residual, cot, gain, gate, up, output, grad_residual, gain_part, out_all, gate_out, up_out, send, recv, local, acc, from_left, from_right, acc_m, left_m, right_m, grad_out, gate_sum, up_sum, *rest):
     links = Links(send, recv, local, members)
-    links.greet()
     for_gate, for_up = rest[:6], rest[6:]
     stores = []
+
+    def block_loads(source, into):
+        loads = [links.move(source.at[o], into.at[o]) for o in range(members)]
+        return lambda o: loads[o].wait()
+
+    load_part, load_mixture = block_loads(part, acc), block_loads(mixture, acc_m)
+    links.greet()
 
     def finish(first, count):
         @pl.loop(0, count // 16)
@@ -441,10 +447,9 @@
             grad_out[at] = (branch_scale * total).astype(BF16)
 
     def chain():
-        links.move(part, acc).wait()
         gain_part[...] = jnp.zeros(gain_part.shape, F32)
         yield from line_sum(
-            links, lambda o: None, acc, from_left, from_right, finish, grad_out, out_all
+            links, load_part, acc, from_left, from_right, finish, grad_out, out_all
         )
 
     def finish_mixture(first, count):
@@ -455,8 +460,7 @@
             output[at] = here.astype(BF16)
 
     def mixture_chain():
-        links.move(mixture, acc_m).wait()
-        yield from line_sum(links, lambda o: None, acc_m, left_m, right_m, finish_mixture)
+        yield from line_sum(links, load_mixture, acc_m, left_m, right_m, finish_mixture)
 
     run(
         THIRD_ORDER,
@@ -766,7 +770,7 @@
     links.finish()
 
 
-FORWARD_ORDER = "tptpdptpcaptgaaacdtrgatcaardaagdattpuparparadrpaarrd"
+FORWARD_ORDER = "tpptpadtcpgptpaatcargadctaatracauaacrtaagpgrrtaargtgdcrtp"
 
 
 def forward_phase(members, tokens, cot, ids, gates, w_query, w_key, w_value, w_out, small, gate, up, down, cosine, sine):
@@ -910,7 +914,8 @@
         for m in range(members):
             d_key[:, m * kv_cols : (m + 1) * kv_cols] = all_rest[m, :, :kv_cols].astype(F32)
             d_value[:, m * kv_cols : (m + 1) * kv_cols] = all_rest[m, :, kv_cols : 2 * kv_cols].astype(F32)
-        gains[...] = sum(all_rest[m, :, 2 * kv_cols :].astype(F32) for m in range(members))
+        total = sum(all_rest[m, :, 2 * kv_cols :].astype(F32) for m in range(members))
+        gains[...] = total.T[: gains.shape[0]]
 
     def weight_chain(fill, part, mine, full, scratch, put):
         fill()
@@ -996,7 +1001,7 @@
         [VMEM] * 6 + [ANY],
         [
             sds((rows, width), F32),
-            sds((own, LANES), F32),
+            sds((8, own), F32),
             sds((own, members * q_cols), F32),
             sds((own, members * kv_cols), F32),
             sds((own, members * kv_cols), F32),
@@ -1327,8 +1332,8 @@
     return (
         output,
         grad_tokens,
-        grad_gains[:, 0],
-        grad_gains[:, 1],
+        grad_gains[0],
+        grad_gains[1],
         d_query,
         d_key,
         d_value,

time: 362 us -> 355 us (0.981)
  Pallas kernels: 342 us -> 335 us
    pallas_call x1, Pallas kernels: 91.9 us -> 85.3 us  [third_phase(): comm_call(third_kernel, 'phase_three', 3, members, 80, 24, [ANY, ANY, VME...]
where the time goes in v10:
time: 355 us; the launch traced here: 354 us
  Pallas kernels  335 us (94%)
  local copies, waits for them, and re-layouts  13.8 us (4%)
  other arithmetic  5.06 us (1%)
    pallas_call x1, Pallas kernels, forward_phase(): comm_call(forward_kernel, 'forward', 1, members, 120, 40, [VMEM, ANY, VME...  126 us
    pallas_call x1, Pallas kernels, third_phase(): comm_call(third_kernel, 'phase_three', 3, members, 80, 24, [ANY, ANY, VME...  85.3 us
    pallas_call x1, Pallas kernels, backward_phase(): comm_call(backward_kernel, 'backward', 4, members, 100, 32, [ANY, VMEM, V...  81.4 us
    pallas_call x1, Pallas kernels, experts(): pl.pallas_call(functools.partial(expert_kernel, capacity, own_experts), g...  42.1 us
    unnamed x25, local copies, waits for them, and re-layouts  12.4 us

profile of v10, /device:TPU:0, one launch (start us, length us, event | category | flops | bytes accessed | tf_op | source)
XLA Modules:
  0.0 354.2 jit_solution(6418307407818109553)
XLA Ops:
  0.6 0.9 select_reduce_fusion.2
  1.5 0.1 select_reduce_fusion.1
  1.6 0.7 pad_convert_fusion.1
  2.3 0.7 pad_convert_fusion
  3.0 0.1 select_reduce_fusion
  3.1 0.6 pad_maximum_fusion.small
  3.7 2.0 fusion
  5.7 125.8 %forward.1 = (bf16[4,160,1536]{2,1,0:T(8,128)(2,1)}, f32[4,160,16]{2,1,0:T(8,128)}, bf16[8,192,1152]{2,1,0:T(8,128)(2,1)}, bf16[8,192,2560]{2,1,0:T(8,128)(2,1)}...) custom-call(bf16[160,1536]{1,0:T(8,128)(2,1)} %tokens.3, ...), custom_call_target="tpu_custom_call" | custom-call | tf_op jit(solution)/shard_map/forward/pallas_call | solution.py:786
  131.6 42.1 %experts.1 = (bf16[640,1536]{1,0:T(8,128)(2,1)}, bf16[640,1536]{1,0:T(8,128)(2,1)}, bf16[1536,2560]{1,0:T(8,128)(2,1)}, bf16[1536,2560]{1,0:T(8,128)(2,1)}, bf16[1536,2560]{1,0:T(8,128)(2,1)}) custom-call(f32[640,16]{1,0:T(8,128)} %bitcast.41, bf16[640,1536]{1,0:T(8,128)(2,1)} %bitcast.35, bf16[640,1536]{1,0:T(8,128)(2,1)} %bitcast.34, ...), custom_call_target="tpu_custom_call" | custom-call | tf_op jit(solution)/shard_map/experts/pallas_call | solution.py:593
  173.7 85.3 %phase_three.1 = (bf16[160,1536]{1,0:T(8,128)(2,1)}, f32[160,1536]{1,0:T(8,128)}, f32[1,1536]{1,0:T(1,128)}, bf16[4,160,1536]{2,1,0:T(8,128)(2,1)}, f32[5,192,512]{2,1,0:T(8,128)}, /*index=5*/f32[5,192,512]{2,1,0:T(8,128)}) custom-call(bf16[4,160,1536]{2,1,0:T(8,128)(2,1)} %bitcast.37, bf16[4,160,1536]{2,1,0:T(8,128)(2,1)} %bitcast.36, ...), custom_call_target="tpu_custom_call" | custom-call | tf_op jit(solution)/shard_map/phase_three/pallas_call | solution.py:483
  259.0 0.0 copy-start.5
  259.0 81.4 %backward.1 = (f32[160,1536]{1,0:T(8,128)}, f32[8,192]{1,0:T(8,128)}, f32[192,1536]{1,0:T(8,128)}, f32[192,512]{1,0:T(8,128)}, f32[192,512]{1,0:T(8,128)}, /*index=5*/f32[192,1536]{1,0:T(8,128)}, f32[5,192,512]{2,1,0:T(8,128)}) custom-call(bf16[640,1536]{1,0:T(8,128)(2,1)} %bitcast.33, f32[160,1536]{1,0:T(8,128)} %get-tuple-element.58.grad_residual, ...), custom_call_target="tpu_custom_call" | custom-call | tf_op jit(solution)/shard_map/backward/pallas_call | solution.py:998
  340.4 0.0 copy-start.4
  340.4 1.4 fusion.6
  341.8 0.0 copy-done.5
  341.8 0.8 copy.35
  342.6 0.0 copy-start.7
  342.6 2.3 copy.36
  344.9 0.0 copy-done.4
  344.9 0.0 copy-start.6
  344.9 0.0 copy-start.3
  344.9 1.0 copy.37
  345.9 0.0 copy-done.7
  345.9 0.0 copy-start.1
  345.9 0.7 copy.38
  346.6 0.0 copy-done.6
  346.6 0.7 copy.39
  347.4 0.0 copy-done.3
  347.4 1.0 copy.40
  348.4 0.0 copy-done.1
  348.4 0.0 copy-start
  348.4 1.3 copy.41
  349.7 1.0 copy-done
  350.7 0.0 copy-start.2
  350.7 1.3 copy.42
  351.9 1.0 copy-done.2
  352.9 1.3 copy.43
  (6 shorter events, 0.0 us)
Async XLA Ops:
  259.0 82.8 %copy-start.5 = (bf16[160,1536]{1,0:T(8,128)(2,1)S(1)}, bf16[160,1536]{1,0:T(8,128)(2,1)}, u32[]{:S(2)}) copy-start(bf16[160,1536]{1,0:T(8,128)(2,1)} %get-tuple-element.96) | copy-start | bytes 1474564
  340.4 4.4 %copy-start.4 = (f32[192,1536]{1,0:T(8,128)S(1)}, f32[192,1536]{1,0:T(8,128)}, u32[]{:S(2)}) copy-start(f32[192,1536]{1,0:T(8,128)} %get-tuple-element.100) | copy-start | bytes 3538948
  342.6 3.3 copy-start.7
  344.9 1.8 copy-start.6
  344.9 2.5 copy-start.3
  345.9 2.5 copy-start.1
  348.4 2.3 copy-start
  350.7 2.3 copy-start.2

commit v11 on v10

--- a/solution.py
+++ b/solution.py
@@ -1026,6 +1026,36 @@
     )(grad_out_all, grad_residual, gain_ffn_part, tokens, down, row_gains, pack_all, normed_attn, qkv, kx, vx, probs, attended, cosine, sine)
 
 
+def results_kernel(count, *refs):
+    sources, targets, held, came, went = refs[:count], refs[count : 2 * count], refs[2 * count : -2], refs[-2], refs[-1]
+    moves = []
+    for source, target, here in zip(sources, targets, held):
+        pieces = source.shape[0] if len(source.shape) == 3 else 2
+        step = source.shape[0] // pieces
+        for i in range(pieces):
+            at, k = pl.ds(i * step, step), len(moves)
+            load = pltpu.make_async_copy(source.at[at], here.at[at], came.at[k])
+            load.start()
+            moves.append((load, pltpu.make_async_copy(here.at[at], target.at[at], went.at[k])))
+    for load, store in moves:
+        load.wait()
+        store.start()
+    for _, store in moves:
+        store.wait()
+
+
+def results(*arrays):
+    return pl.pallas_call(
+        functools.partial(results_kernel, len(arrays)),
+        out_shape=[sds(a.shape, a.dtype) for a in arrays],
+        in_specs=[ANY] * len(arrays),
+        out_specs=[ANY] * len(arrays),
+        scratch_shapes=[pltpu.VMEM(a.shape, a.dtype) for a in arrays] + [pltpu.SemaphoreType.DMA((64,))] * 2,
+        compiler_params=pltpu.CompilerParams(vmem_limit_bytes=VMEM_LIMIT),
+        name="results",
+    )(*arrays)
+
+
 def all_blocks(x, axis):
     return lax.all_gather(x, axis, axis=0)
 
@@ -1329,6 +1359,9 @@
         pack_all,
         normed_attn, qkv, kx, vx, probs, attended, cosine, sine,
     )
+    output, grad_tokens, d_query, d_key, d_value, d_out, sum_gate, sum_up, d_down = results(
+        output, grad_tokens, d_query, d_key, d_value, d_out, sum_gate, sum_up, d_down
+    )
     return (
         output,
         grad_tokens,

time: 355 us -> 351 us (0.989)
  local copies, waits for them, and re-layouts: 13.8 us -> 1.36 us
  Pallas kernels: 335 us -> 343 us
    unnamed x25 -> x0, local copies, waits for them, and re-layouts: 12.4 us -> none
    pallas_call x0 -> x1, Pallas kernels: none -> 8.92 us  [results(): pl.pallas_call(functools.partial(results_kernel, len(arrays)), out_shape=...]
where the time goes in v11:
time: 351 us
  Pallas kernels  343 us (98%)
  other arithmetic  5.06 us (1%)
    pallas_call x1, Pallas kernels, forward_phase(): comm_call(forward_kernel, 'forward', 1, members, 120, 40, [VMEM, ANY, VME...  126 us
    pallas_call x1, Pallas kernels, third_phase(): comm_call(third_kernel, 'phase_three', 3, members, 80, 24, [ANY, ANY, VME...  84.6 us
    pallas_call x1, Pallas kernels, backward_phase(): comm_call(backward_kernel, 'backward', 4, members, 100, 32, [ANY, VMEM, V...  82 us
    pallas_call x1, Pallas kernels, experts(): pl.pallas_call(functools.partial(expert_kernel, capacity, own_experts), g...  42.1 us
    pallas_call x1, Pallas kernels, results(): pl.pallas_call(functools.partial(results_kernel, len(arrays)), out_shape=...  8.92 us

profile of v11, /device:TPU:0, one launch (start us, length us, event | category | flops | bytes accessed | tf_op | source)
XLA Modules:
  0.0 350.5 jit_solution(4812996873026214164)
XLA Ops:
  0.6 0.9 select_reduce_fusion.2
  1.5 0.1 select_reduce_fusion.1
  1.6 0.7 pad_convert_fusion.1
  2.3 0.7 pad_convert_fusion
  3.0 0.1 select_reduce_fusion
  3.1 0.6 pad_maximum_fusion.small
  3.7 2.0 fusion
  5.7 125.8 %forward.1 = (bf16[4,160,1536]{2,1,0:T(8,128)(2,1)}, f32[4,160,16]{2,1,0:T(8,128)}, bf16[8,192,1152]{2,1,0:T(8,128)(2,1)}, bf16[8,192,2560]{2,1,0:T(8,128)(2,1)}...) custom-call(bf16[160,1536]{1,0:T(8,128)(2,1)} %tokens.3, ...), custom_call_target="tpu_custom_call" | custom-call | tf_op jit(solution)/shard_map/forward/pallas_call | solution.py:786
  131.6 42.1 %experts.1 = (bf16[640,1536]{1,0:T(8,128)(2,1)}, bf16[640,1536]{1,0:T(8,128)(2,1)}, bf16[1536,2560]{1,0:T(8,128)(2,1)}, bf16[1536,2560]{1,0:T(8,128)(2,1)}, bf16[1536,2560]{1,0:T(8,128)(2,1)}) custom-call(f32[640,16]{1,0:T(8,128)} %bitcast.38, bf16[640,1536]{1,0:T(8,128)(2,1)} %bitcast.32, bf16[640,1536]{1,0:T(8,128)(2,1)} %bitcast.31, ...), custom_call_target="tpu_custom_call" | custom-call | tf_op jit(solution)/shard_map/experts/pallas_call | solution.py:593
  173.7 84.6 %phase_three.1 = (bf16[160,1536]{1,0:T(8,128)(2,1)}, f32[160,1536]{1,0:T(8,128)}, f32[1,1536]{1,0:T(1,128)}, bf16[4,160,1536]{2,1,0:T(8,128)(2,1)}, f32[5,192,512]{2,1,0:T(8,128)}, /*index=5*/f32[5,192,512]{2,1,0:T(8,128)}) custom-call(bf16[4,160,1536]{2,1,0:T(8,128)(2,1)} %bitcast.34, bf16[4,160,1536]{2,1,0:T(8,128)(2,1)} %bitcast.33, ...), custom_call_target="tpu_custom_call" | custom-call | tf_op jit(solution)/shard_map/phase_three/pallas_call | solution.py:483
  258.2 82.0 %backward.1 = (f32[160,1536]{1,0:T(8,128)}, f32[8,192]{1,0:T(8,128)}, f32[192,1536]{1,0:T(8,128)}, f32[192,512]{1,0:T(8,128)}, f32[192,512]{1,0:T(8,128)}, /*index=5*/f32[192,1536]{1,0:T(8,128)}, f32[5,192,512]{2,1,0:T(8,128)}) custom-call(bf16[640,1536]{1,0:T(8,128)(2,1)} %bitcast.30, f32[160,1536]{1,0:T(8,128)} %get-tuple-element.67.grad_residual, ...), custom_call_target="tpu_custom_call" | custom-call | tf_op jit(solution)/shard_map/backward/pallas_call | solution.py:998
  340.3 8.9 %results.1 = (bf16[160,1536]{1,0:T(8,128)(2,1)}, f32[160,1536]{1,0:T(8,128)}, f32[192,1536]{1,0:T(8,128)}, f32[192,512]{1,0:T(8,128)}, f32[192,512]{1,0:T(8,128)...) custom-call(bf16[160,1536]{1,0:T(8,128)(2,1)} %get-tuple-element.65.refs_0_, ...), custom_call_target="tpu_custom_call" | custom-call | tf_op jit(solution)/shard_map/results/pallas_call | solution.py:1048
  349.2 1.3 fusion.6
  (6 shorter events, 0.0 us)

commit v12 on v11

--- a/solution.py
+++ b/solution.py
@@ -530,8 +530,6 @@
 
     @pl.when(e == 0)
     def _():
-        mix_sum[...] = jnp.zeros(mix_sum.shape, F32)
-        grad_sum[...] = jnp.zeros(grad_sum.shape, F32)
         lane = lane_ids(LANES)
         name = (lax.axis_index("expert") * own_experts + lane).astype(F32)
         name = jnp.where(lane < own_experts, name, -1.0)
@@ -550,6 +548,9 @@
             before = before + jnp.sum(chosen, axis=0, keepdims=True)
         slot_rows[...] = mm_nt(first_lanes(), slot_cols[...].astype(BF16))
 
+    def add_to(total, term):
+        total[...] = jnp.where(e == 0, 0.0, total[...]) + term
+
     def column(values):
         return jnp.sum(jnp.where(lane_ids(span) == e, values[...], 0.0), axis=1, keepdims=True)
 
@@ -566,13 +567,13 @@
     silu = pre_gate * sig
     activ = (silu * pre_up).astype(BF16)
     produced = (gate_col * mm_nt(activ, w_down[...])).astype(BF16)
-    mix_sum[...] += mm(put, produced)
+    add_to(mix_sum, mm(put, produced))
     grad_out = (gate_col * (branch_scale * mm(pick, cot[...]))).astype(BF16)
     grad_activ = mm(grad_out, w_down[...])
     grad_gate = (grad_activ * pre_up * (sig * (1.0 + pre_gate * (1.0 - sig)))).astype(BF16)
     grad_up = (grad_activ * silu).astype(BF16)
     grad_pair = (mm_nt(grad_gate, w_gate[...]) + mm_nt(grad_up, w_up[...])).astype(BF16)
-    grad_sum[...] += mm(put, grad_pair)
+    add_to(grad_sum, mm(put, grad_pair))
     d_gate[...] = mm_tn(received, grad_gate).astype(BF16)
     d_up[...] = mm_tn(received, grad_up).astype(BF16)
     d_down[...] = mm_tn(grad_out, activ).astype(BF16)
@@ -1359,8 +1360,8 @@
         pack_all,
         normed_attn, qkv, kx, vx, probs, attended, cosine, sine,
     )
-    output, grad_tokens, d_query, d_key, d_value, d_out, sum_gate, sum_up, d_down = results(
-        output, grad_tokens, d_query, d_key, d_value, d_out, sum_gate, sum_up, d_down
+    sum_gate, sum_up, d_down, d_query, d_out, grad_tokens, output, d_key, d_value = results(
+        sum_gate, sum_up, d_down, d_query, d_out, grad_tokens, output, d_key, d_value
     )
     return (
         output,

time: 351 us -> 351 us (level)
  no operation moved by 1% of the time
where the time goes in v12:
time: 351 us; the launch traced here: 350 us
  Pallas kernels  343 us (98%)
  other arithmetic  5.06 us (1%)
    pallas_call x1, Pallas kernels, forward_phase(): comm_call(forward_kernel, 'forward', 1, members, 120, 40, [VMEM, ANY, VME...  126 us
    pallas_call x1, Pallas kernels, third_phase(): comm_call(third_kernel, 'phase_three', 3, members, 80, 24, [ANY, ANY, VME...  85.3 us
    pallas_call x1, Pallas kernels, backward_phase(): comm_call(backward_kernel, 'backward', 4, members, 100, 32, [ANY, VMEM, V...  81.3 us
    pallas_call x1, Pallas kernels, experts(): pl.pallas_call(functools.partial(expert_kernel, capacity, own_experts), g...  42 us
    pallas_call x1, Pallas kernels, results(): pl.pallas_call(functools.partial(results_kernel, len(arrays)), out_shape=...  8.81 us

profile of v12, /device:TPU:0, one launch (start us, length us, event | category | flops | bytes accessed | tf_op | source)
XLA Modules:
  0.0 350.4 jit_solution(5795485891351956881)
XLA Ops:
  0.6 0.9 select_reduce_fusion.2
  1.5 0.1 select_reduce_fusion.1
  1.6 0.7 pad_convert_fusion.1
  2.3 0.7 pad_convert_fusion
  3.0 0.1 select_reduce_fusion
  3.1 0.6 pad_maximum_fusion.small
  3.7 2.0 fusion
  5.7 125.8 %forward.1 = (bf16[4,160,1536]{2,1,0:T(8,128)(2,1)}, f32[4,160,16]{2,1,0:T(8,128)}, bf16[8,192,1152]{2,1,0:T(8,128)(2,1)}, bf16[8,192,2560]{2,1,0:T(8,128)(2,1)}...) custom-call(bf16[160,1536]{1,0:T(8,128)(2,1)} %tokens.3, ...), custom_call_target="tpu_custom_call" | custom-call | tf_op jit(solution)/shard_map/forward/pallas_call | solution.py:787
  131.6 42.0 %experts.1 = (bf16[640,1536]{1,0:T(8,128)(2,1)}, bf16[640,1536]{1,0:T(8,128)(2,1)}, bf16[1536,2560]{1,0:T(8,128)(2,1)}, bf16[1536,2560]{1,0:T(8,128)(2,1)}, bf16[1536,2560]{1,0:T(8,128)(2,1)}) custom-call(f32[640,16]{1,0:T(8,128)} %bitcast.38, bf16[640,1536]{1,0:T(8,128)(2,1)} %bitcast.32, bf16[640,1536]{1,0:T(8,128)(2,1)} %bitcast.31, ...), custom_call_target="tpu_custom_call" | custom-call | tf_op jit(solution)/shard_map/experts/pallas_call | solution.py:594
  173.6 85.3 %phase_three.1 = (bf16[160,1536]{1,0:T(8,128)(2,1)}, f32[160,1536]{1,0:T(8,128)}, f32[1,1536]{1,0:T(1,128)}, bf16[4,160,1536]{2,1,0:T(8,128)(2,1)}, f32[5,192,512]{2,1,0:T(8,128)}, /*index=5*/f32[5,192,512]{2,1,0:T(8,128)}) custom-call(bf16[4,160,1536]{2,1,0:T(8,128)(2,1)} %bitcast.34, bf16[4,160,1536]{2,1,0:T(8,128)(2,1)} %bitcast.33, ...), custom_call_target="tpu_custom_call" | custom-call | tf_op jit(solution)/shard_map/phase_three/pallas_call | solution.py:483
  258.9 81.3 %backward.1 = (f32[160,1536]{1,0:T(8,128)}, f32[8,192]{1,0:T(8,128)}, f32[192,1536]{1,0:T(8,128)}, f32[192,512]{1,0:T(8,128)}, f32[192,512]{1,0:T(8,128)}, /*index=5*/f32[192,1536]{1,0:T(8,128)}, f32[5,192,512]{2,1,0:T(8,128)}) custom-call(bf16[640,1536]{1,0:T(8,128)(2,1)} %bitcast.30, f32[160,1536]{1,0:T(8,128)} %get-tuple-element.68.grad_residual, ...), custom_call_target="tpu_custom_call" | custom-call | tf_op jit(solution)/shard_map/backward/pallas_call | solution.py:999
  340.2 8.8 %results.1 = (f32[5,192,512]{2,1,0:T(8,128)}, f32[5,192,512]{2,1,0:T(8,128)}, f32[5,192,512]{2,1,0:T(8,128)}, f32[192,1536]{1,0:T(8,128)}, f32[192,1536]{1,0:T(8...) custom-call(f32[5,192,512]{2,1,0:T(8,128)} %get-tuple-element.65.refs_0_, ...), custom_call_target="tpu_custom_call" | custom-call | tf_op jit(solution)/shard_map/results/pallas_call | solution.py:1049
  349.0 1.3 fusion.6
  (6 shorter events, 0.0 us)
